TPU v7x, 32 devices: a whole 2x2x4 slice. The times are simulated.
32 devices in a mesh: ctx: 8 (over z, x), head: 4 (over y, core).
Axes of the slice: x: 2, y: 2, z: 4, core: 2. Of those that a mesh axis runs over, the one named last changes fastest.
Arguments:
- queries: bfloat16 [4, 1024, 1024], P(None, 'ctx', 'head'), may hold values from -45 to 45
- keys: bfloat16 [4, 1024, 1024], P(None, 'ctx', 'head'), may hold values from -6 to 6
- values: bfloat16 [4, 1024, 1024], P(None, 'ctx', 'head'), may hold values from -6 to 6
- out_weight: bfloat16 [1024, 2048], P(None, 'head'), may hold values from -0.1875 to 0.1875
- global_ids: int32 [4, 2], replicated, may hold values from 0 to 15, as said below
- rand_ids: int32 [4, 16, 4], P(None, 'ctx'), may hold values from 0 to 15, as said below
- rand_count: int32 [4, 16], P(None, 'ctx'), may hold values from 1 to 4
Outputs:
- output: bfloat16 [4, 1024, 2048], P(None, 'ctx', 'head')
Inputs may be any that keep to these rules, and one draw needn't show every extreme that they name: `global_ids`: block ids; the 2 ids of one sequence are distinct. `rand_ids`: block ids of the same sequence. Taking together the 2 query blocks that each of the 4 sequences has on one index of ctx, at most 4 live slots name blocks held by any one index of ctx.
All inputs are finite; a program needn't handle non-finite values.
Results may differ from a plain program's by a relative error of at most 0.0056.
Values may be sent and summed in bfloat16 or wider, within the bound.
No kernel may reach another device: no remote copies, remote signals or barrier semaphores. Data moves between devices by JAX's collectives and lax.ppermute only.
A program may use at most 64 MiB of HBM per device.

v0:
```python
import jax
import jax.numpy as jnp
from jax import lax
from jax.sharding import PartitionSpec as P

HEAD_DIM = 128
BLOCK = 64
GLOB = 2
RMAX = 4


def with_halo(cells, sides, width):
    for axis, dim in sides:
        count = lax.axis_size(axis)
        head = lax.slice_in_dim(cells, 0, width, axis=dim)
        tail = lax.slice_in_dim(cells, cells.shape[dim] - width, cells.shape[dim], axis=dim)
        cells = jnp.concatenate(
            [
                lax.ppermute(tail, axis, [(i, (i + 1) % count) for i in range(count)]),
                cells,
                lax.ppermute(head, axis, [((i + 1) % count, i) for i in range(count)]),
            ],
            axis=dim,
        )
    return cells


def slot_table(slot_of, live_flat, slot_total):
    return (
        (slot_of[:, None] == jnp.arange(slot_total, dtype=jnp.int32)[None, :]) & live_flat[:, None]
    ).astype(jnp.int32)


def on_device(queries, keys, values, out_weight, global_ids, rand_ids, rand_count):
    seq_count, seq_rows, local_width = queries.shape
    blocks_here = seq_rows // BLOCK
    heads_here = local_width // HEAD_DIM
    cycle_size = lax.axis_size("ctx")
    my_index = lax.axis_index("ctx")
    request_count = seq_count * blocks_here * RMAX
    capacity = (request_count + cycle_size - 1) // cycle_size
    slot_total = cycle_size * capacity
    key_width = 3 + GLOB + RMAX
    score_scale = HEAD_DIM ** (-0.5)
    token_pairs = jnp.stack([keys, values], 0)
    block_pairs = jnp.stack(
        [
            keys.reshape(seq_count, blocks_here, BLOCK, local_width),
            values.reshape(seq_count, blocks_here, BLOCK, local_width),
        ],
        2,
    ).reshape(seq_count * blocks_here, 2, BLOCK, local_width)
    extended = with_halo(token_pairs, (("ctx", 2),), BLOCK)
    own_blocks = token_pairs.reshape(2, seq_count, blocks_here, BLOCK, local_width)
    shared_owner = global_ids // blocks_here
    shared_local = global_ids % blocks_here
    picker = (
        (shared_local[:, :, None] == jnp.arange(blocks_here, dtype=jnp.int32)[None, None, :])
        & (shared_owner == my_index)[:, :, None]
    ).astype(jnp.bfloat16)
    contribution = jnp.einsum(
        "sgj,xsjtf->xsgtf", picker, own_blocks, preferred_element_type=jnp.float32
    )
    shared_rows = lax.psum(contribution, "ctx").astype(jnp.bfloat16)
    slot_ids = jnp.arange(RMAX, dtype=jnp.int32)
    live_flat = (slot_ids[None, None, :] < rand_count[:, :, None]).reshape(-1)
    owners = (rand_ids // blocks_here).reshape(-1)
    seq_of = jnp.arange(seq_count, dtype=jnp.int32)[:, None, None]
    block_codes = (seq_of * blocks_here + rand_ids % blocks_here).reshape(-1)
    hit_owner = (
        (owners[:, None] == jnp.arange(cycle_size, dtype=jnp.int32)[None, :]) & live_flat[:, None]
    ).astype(jnp.int32)
    rank_within = jnp.sum((jnp.cumsum(hit_owner, axis=0) - hit_owner) * hit_owner, axis=1)
    slot_of = jnp.where(live_flat, owners * capacity + rank_within, 0)
    slot_hits = slot_table(slot_of, live_flat, slot_total)
    requests_out = (jnp.sum(slot_hits * (block_codes[:, None] + 1), axis=0) - 1).reshape(
        cycle_size, capacity
    )
    wanted_here = lax.all_to_all(requests_out, "ctx", split_axis=0, concat_axis=0, tiled=True)
    beside_all = extended.reshape(2, seq_count, blocks_here + 2, BLOCK, local_width)
    window_keys = jnp.stack(
        [beside_all[:, :, offset : offset + blocks_here] for offset in range(3)], 3
    )
    shared_wide = jnp.broadcast_to(
        shared_rows[:, :, None], (2, seq_count, blocks_here, GLOB, BLOCK, local_width)
    )
    local_keys = jnp.concatenate([window_keys, shared_wide], 3)
    query_view = queries.reshape(seq_count, blocks_here, BLOCK, heads_here, HEAD_DIM)
    payload = jnp.take(block_pairs, jnp.maximum(wanted_here, 0).reshape(-1), axis=0).reshape(
        cycle_size, capacity, 2, BLOCK, local_width
    )
    received = lax.all_to_all(payload, "ctx", split_axis=0, concat_axis=0, tiled=True)
    random_rows = jnp.take(received.reshape(slot_total, 2, BLOCK, local_width), slot_of, axis=0)
    random_rows = jnp.moveaxis(
        random_rows.reshape(seq_count, blocks_here, RMAX, 2, BLOCK, local_width), 3, 0
    )
    all_keys = jnp.concatenate([local_keys, random_rows], 3).reshape(
        2, seq_count, blocks_here, key_width * BLOCK, heads_here, HEAD_DIM
    )
    scores = (
        jnp.einsum(
            "sjqhd,sjkhd->sjhqk", query_view, all_keys[0], preferred_element_type=jnp.float32
        )
        * score_scale
    )
    live_slots = jnp.concatenate(
        [
            jnp.ones((seq_count, blocks_here, 3 + GLOB), jnp.bool_),
            slot_ids[None, None, :] < rand_count[:, :, None],
        ],
        2,
    )
    live_cols = jnp.repeat(live_slots, BLOCK, axis=2)[:, :, None, None, :]
    masked = jnp.where(live_cols, scores, -1e30)
    row_peak = jnp.max(masked, axis=-1, keepdims=True)
    weights = jnp.where(live_cols, jnp.exp(masked - row_peak), 0.0)
    row_total = jnp.sum(weights, axis=-1)
    weighted = jnp.einsum(
        "sjhqk,sjkhd->sjqhd",
        weights.astype(jnp.bfloat16),
        all_keys[1],
        preferred_element_type=jnp.float32,
    )
    attention = (
        (weighted / jnp.moveaxis(row_total, 2, 3)[..., None])
        .astype(jnp.bfloat16)
        .reshape(seq_count, seq_rows, local_width)
    )
    projected = jnp.einsum(
        "stf,fo->sto",
        lax.all_gather(attention, "head", axis=2, tiled=True),
        out_weight,
        preferred_element_type=jnp.float32,
    )
    return projected.astype(jnp.bfloat16)


def solution(mesh):
    placed = (
        P(None, "ctx", "head"),
        P(None, "ctx", "head"),
        P(None, "ctx", "head"),
        P(None, "head"),
        P(),
        P(None, "ctx", None),
        P(None, "ctx"),
    )
    return jax.shard_map(
        on_device, mesh=mesh, in_specs=placed, out_specs=P(None, "ctx", "head"), check_vma=False
    )
```

profile of v0, /device:TPU:0, one launch (start us, length us, event | category | flops | bytes accessed | tf_op | source)
XLA Modules:
  0.0 203.6 jit_solution(9323412022913405305)
XLA Ops:
  6.5 0.0 copy-start
  6.5 0.8 broadcast_multiply_fusion
  7.4 0.1 add.104
  7.5 0.8 copy.77
  8.2 0.1 iota_compare_fusion.2
  8.3 0.1 lt.84
  8.4 0.1 reshape.186
  8.5 0.1 fusion.37
  8.6 0.1 reduce_window_sum.11
  8.6 0.2 select_reduce_fusion.1
  8.8 0.1 select_reduce_fusion
  8.9 0.7 sub.31
  9.6 7.3 %all-to-all-start = ((s32[8,1,4]{2,1,0:T(1,128)}), s32[8,1,4]{2,1,0:T(1,128)S(1)}, u32[]{:S(2)}, u32[]{:S(2)}) async-start(s32[8,1,4]{2,1,0:T(1,128)} %bitcast.13), calls=%async_computation | async-start | bytes 8192 | tf_op jit(solution)/shard_map/all_to_all | solution.py:79
  16.9 1.1 pad_maximum_fusion.3
  18.0 5.3 %all-to-all-done = s32[8,1,4]{2,1,0:T(1,128)S(1)} async-done(((s32[8,1,4]{2,1,0:T(1,128)}), s32[8,1,4]{2,1,0:T(1,128)S(1)}, u32[]{:S(2)}, u32[]{:S(2)}) %all-to-all-start) | async-done | bytes 160 | tf_op jit(solution)/shard_map/all_to_all | solution.py:79
  23.3 0.1 reshape.192
  23.4 0.1 copy.79
  23.5 0.1 copy.80
  23.6 2.0 gather_fusion
  25.6 3.2 %broadcast_select_fusion = bf16[8,4,2,64,256]{4,3,2,1,0:T(8,128)(2,1)} fusion(bf16[8,4,2,64,256]{4,3,2,1,0:T(8,128)(2,1)} %bitcast.76, pred[8,4]{1,0:T(8,128)(4,1)S(1)} %copy.80), kind=kLoop, calls=%fused_computation.15 | loop fusion | flops 1048576 | bytes 4194336 | tf_op jit(solution)/shard_map/jit(_take)/select_n | solution.py:89
  28.8 3.7 %all-to-all-start.1 = ((bf16[8,4,2,64,256]{4,3,2,1,0:T(8,128)(2,1)}), bf16[8,4,2,64,256]{4,3,2,1,0:T(8,128)(2,1)S(1)}, u32[]{:S(2)}, u32[]{:S(2)}) async-start(bf16[8,4,2,64,256]{4,3,2,1,0:T(8,128)(2,1)} %broadcast_select_fusion), calls=%async_computation.1 | async-start | bytes 4194304 | tf_op jit(solution)/shard_map/all_to_all | solution.py:92
  32.6 0.0 all-gather.2.cloned.1.call-start
  32.6 1.8 fusion.34
  34.5 4.6 %collective-permute-start.1 = (bf16[2,4,64,256]{3,2,1,0:T(8,128)(2,1)}, bf16[2,4,64,256]{3,2,1,0:T(8,128)(2,1)}, u32[]{:S(2)}, u32[]{:S(2)}) collective-permute-start(bf16[2,4,64,256]{3,2,1,0:T(8,128)(2,1)} %get-tuple-element.10), channel_id=1, source_target_pairs={{4,0},{8,4},{12,8},{16,12},{20,16},{24,20},{28,24},{0,28},{5,1},{9... | collective-permute-start | bytes 786440 | tf_op jit(solution)/shard_map/ppermute | solution.py:21
  39.1 0.0 collective-permute-start
  39.1 0.1 lt.87
  39.2 1.9 copy.73
  41.1 1.0 copy.72
  42.1 0.1 copy.75
  42.2 0.1 copy.74
  42.3 2.8 %convolution_bitcast_fusion = f32[2,4,2,64,256]{4,2,3,0,1:T(2,128)} fusion(bf16[1,4,2,64,256]{4,2,3,0,1:T(2,128)(2,1)} %copy.73, bf16[1,4,2,64,256]{4,2,3,0,1:T(2,128)(2,1)} %copy.72, pred[4,2]{1,0:T(4,128)(4,1)S(1)} %copy.75, s32[4,2]{1,0:T(4,128)S(1)} %copy.74), kind=kOutput, calls=%fused_computation.16 | convolution fusion | flops 2097184 | bytes 1572904 | tf_op jit(solution)/shard_map/sgj,xsjtf->xsgtf/dot_general | solution.py:61
  45.1 0.1 mul.60
  45.2 101.3 %all-reduce.2 = bf16[2,4,2,64,256]{4,2,3,0,1:T(2,128)(2,1)} all-reduce(f32[2,4,2,64,256]{4,2,3,0,1:T(2,128)} %convolution_bitcast_fusion), channel_id=1, replica_groups=mesh['ctx'=8,'head'=4] {'ctx'}, use_global_device_ids=true, to_apply=%region_0.1 | all-reduce | flops 262144 | bytes 1572864 | tf_op jit(solution)/shard_map/psum | solution.py:64
  146.5 0.1 reduce_sum.32
  146.6 2.0 copy.76
  148.5 1.7 reshape.188
  150.2 0.1 concatenate.13.clone
  150.3 0.1 broadcast_in_dim.81
  150.4 0.1 broadcast_in_dim.82
  150.5 0.1 compare_and_fusion
  150.6 0.0 copy-start.3
  150.6 0.0 collective-permute-done.1
  150.6 0.0 collective-permute-done
  150.6 1.2 pad_maximum_fusion
  151.9 0.8 fusion.32
  152.7 0.8 fusion.31
  153.5 0.8 fusion.30
  154.4 1.1 broadcast_dynamic-update-slice_fusion
  155.5 0.0 all-to-all-done.1
  155.5 2.1 %gather_fusion.1 = bf16[32,2,64,256]{3,2,1,0:T(8,128)(2,1)} fusion(bf16[32,2,64,256]{3,2,1,0:T(8,128)(2,1)S(1)} %bitcast.77, s32[1024]{0:T(1024)S(1)} %pad_clamp_fusion), kind=kCustom, calls=%fused_computation.1 | custom fusion | bytes 4194432 | tf_op jit(solution)/shard_map/jit(_take)/gather | solution.py:93
  157.5 4.0 %bitcast_dynamic-update-slice_fusion = bf16[2,4,2,9,64,256]{5,4,3,2,1,0:T(8,128)(2,1)} fusion(bf16[2,4,2,9,64,256]{5,4,3,2,1,0:T(8,128)(2,1)} %broadcast_dynamic-update-slice_fusion, bf16[4,2,4,2,64,256]{5,4,3,2,1,0:T(8,128)(2,1)} %bitcast.78, pred[4,2,4]{2,1,0:T(4,128)(4,1)S(1)} %compare_and_fusion), kind=kLoop, calls=%fused_computation.13 | loop fusion | flops 1048576 | bytes 4194336 | tf_op jit(solution)/shard_map/concatenate | solution.py:97
  161.5 4.4 %fusion.51 = (bf16[1,4,2,9,64,256]{5,4,3,2,1,0:T(8,128)(2,1)}, bf16[1,4,2,9,64,256]{5,4,3,2,1,0:T(8,128)(2,1)S(1)}) fusion(bf16[2,4,2,9,64,256]{5,4,3,2,1,0:T(8,128)(2,1)} %bitcast_dynamic-update-slice_fusion), kind=kLoop, calls=%fused_computation.89 | loop fusion | bytes 9437184 | tf_op jit(solution)/shard_map/slice | solution.py:102
  165.9 2.1 %squeeze.6 = bf16[4,2,576,2,128]{4,3,2,1,0:T(2,128)(2,1)} reshape(bf16[1,4,2,9,64,256]{5,4,3,2,1,0:T(8,128)(2,1)S(1)} %get-tuple-element.8) | data formatting | bytes 4718592 | tf_op jit(solution)/shard_map/squeeze | solution.py:121
  168.0 4.6 %squeeze.7 = bf16[4,2,576,2,128]{4,3,2,1,0:T(2,128)(2,1)S(1)} reshape(bf16[1,4,2,9,64,256]{5,4,3,2,1,0:T(8,128)(2,1)} %get-tuple-element.7) | data formatting | bytes 4718592 | tf_op jit(solution)/shard_map/squeeze | solution.py:102
  172.7 1.9 fusion.6
  174.6 1.2 fusion.52
  175.8 0.5 copy-done.2
  176.2 0.6 fusion.24
  176.8 0.3 copy.90
  177.1 0.9 reshape.189
  178.0 0.0 all-gather.2.cloned.1.call-update
  178.0 16.0 %all-gather.2.cloned.1.call-done = bf16[4,128,1024]{2,1,0:T(8,128)(2,1)} async-done(((bf16[4,128,256]{2,1,0:T(8,128)(2,1)}), bf16[4,128,1024]{2,1,0:T(8,128)(2,1)}) %all-gather.2.cloned.1.call-update) | async-done | bytes 1048592 | tf_op jit(solution)/shard_map/all_gather | solution.py:131
  194.0 0.0 copy-done
  194.0 2.7 %convolution_convert_fusion = bf16[4,128,512]{2,1,0:T(8,128)(2,1)} fusion(bf16[4,128,1024]{2,1,0:T(8,128)(2,1)} %all-gather.2.cloned.1.call-done, bf16[1024,512]{1,0:T(8,128)(2,1)S(1)} %copy-done), kind=kOutput, calls=%fused_computation.21 | convolution fusion | flops 537133056 | bytes 2621440 | tf_op jit(solution)/shard_map/stf,fo->sto/dot_general | solution.py:129
  (18 shorter events, 0.1 us)
Async XLA Ops:
  6.5 187.5 %copy-start = (bf16[1024,512]{1,0:T(8,128)(2,1)S(1)}, bf16[1024,512]{1,0:T(8,128)(2,1)}, u32[]{:S(2)}) copy-start(bf16[1024,512]{1,0:T(8,128)(2,1)} %param.10) | copy-start | bytes 3145732
  9.6 13.6 %all-to-all-start = ((s32[8,1,4]{2,1,0:T(1,128)}), s32[8,1,4]{2,1,0:T(1,128)S(1)}, u32[]{:S(2)}, u32[]{:S(2)}) async-start(s32[8,1,4]{2,1,0:T(1,128)} %bitcast.13), calls=%async_computation | async-start | bytes 8192 | tf_op jit(solution)/shard_map/all_to_all | solution.py:79
  28.8 3.8 %copy-start.1 = (bf16[4,128,256]{2,1,0:T(8,128)(2,1)S(1)}, bf16[4,128,256]{2,1,0:T(8,128)(2,1)}, u32[]{:S(2)}) copy-start(bf16[4,128,256]{2,1,0:T(8,128)(2,1)} %param.8) | copy-start | bytes 786436
  28.8 13.3 %copy-start.4 = (s32[4,2]{0,1:T(2,128)S(1)}, s32[4,2]{0,1:T(2,128)}, u32[]{:S(2)}) copy-start(s32[4,2]{0,1:T(2,128)} %param.11) | copy-start | bytes 100
  28.8 126.6 %all-to-all-start.1 = ((bf16[8,4,2,64,256]{4,3,2,1,0:T(8,128)(2,1)}), bf16[8,4,2,64,256]{4,3,2,1,0:T(8,128)(2,1)S(1)}, u32[]{:S(2)}, u32[]{:S(2)}) async-start(bf16[8,4,2,64,256]{4,3,2,1,0:T(8,128)(2,1)} %broadcast_select_fusion), calls=%async_computation.1 | async-start | bytes 4194304 | tf_op jit(solution)/shard_map/all_to_all | solution.py:92
  32.6 161.5 %all-gather.2.cloned.1.call-start = ((), (), s32[]{:S(2)}) async-start(), calls=%async_computation.2 | async-start | bytes 1310720 | tf_op jit(solution)/shard_map/all_gather | solution.py:131
  34.5 116.2 %collective-permute-start.1 = (bf16[2,4,64,256]{3,2,1,0:T(8,128)(2,1)}, bf16[2,4,64,256]{3,2,1,0:T(8,128)(2,1)}, u32[]{:S(2)}, u32[]{:S(2)}) collective-permute-start(bf16[2,4,64,256]{3,2,1,0:T(8,128)(2,1)} %get-tuple-element.10), channel_id=1, source_target_pairs={{4,0},{8,4},{12,8},{16,12},{20,16},{24,20},{28,24},{0,28},{5,1},{9... | collective-permute-start | bytes 786440 | tf_op jit(solution)/shard_map/ppermute | solution.py:21
  39.1 111.6 %collective-permute-start = (bf16[2,4,64,256]{3,2,1,0:T(8,128)(2,1)}, bf16[2,4,64,256]{3,2,1,0:T(8,128)(2,1)}, u32[]{:S(2)}, u32[]{:S(2)}) collective-permute-start(bf16[2,4,64,256]{3,2,1,0:T(8,128)(2,1)} %get-tuple-element.9), channel_id=1, source_target_pairs={{0,4},{4,8},{8,12},{12,16},{16,20},{20,24},{24,28},{28,0},{1,5},{5... | collective-permute-start | bytes 786440 | tf_op jit(solution)/shard_map/ppermute | solution.py:19
  150.6 3.7 %copy-start.3 = (bf16[2,4,2,64,256]{4,3,2,1,0:T(8,128)(2,1)S(1)}, bf16[2,4,2,64,256]{4,3,2,1,0:T(8,128)(2,1)}, u32[]{:S(2)}) copy-start(bf16[2,4,2,64,256]{4,3,2,1,0:T(8,128)(2,1)} %copy.76) | copy-start | bytes 1572868
  174.6 1.7 copy-start.2
Sparse Core Ops, SparseCore 0:
  178.1 15.8 all-gather.1
where the time goes:
time: 204 us
  blocking collectives  101 us (50%)
  local copies, waits for them, and re-layouts  29.8 us (15%)
  waiting for transfers between devices  21.4 us (10%)
  starting transfers between devices  15.6 us (8%)
  other arithmetic  14 us (7%)
  between operations  13.5 us (7%)
  matrix products  7.99 us (4%)
    psum x1, blocking collectives, on_device(): shared_rows = lax.psum(contribution, 'ctx').astype(jnp.bfloat16)  101 us
    all_gather x1, waiting for transfers between devices, on_device(): lax.all_gather(attention, 'head', axis=2, tiled=True)  16 us
    all_to_all x1, starting transfers between devices, on_device(): lax.all_to_all(requests_out, 'ctx', split_axis=0, concat_axis=0, tiled=True)  7.25 us
    all_to_all x1, waiting for transfers between devices, on_device(): lax.all_to_all(requests_out, 'ctx', split_axis=0, concat_axis=0, tiled=True)  5.31 us
    unnamed x16, local copies, waits for them, and re-layouts  4.87 us
    squeeze x1, local copies, waits for them, and re-layouts, on_device(): all_keys[0]  4.63 us
    ppermute x1, starting transfers between devices, with_halo(): lax.ppermute(head, axis, [((i + 1) % count, i) for i in range(count)])  4.61 us
    slice x1, local copies, waits for them, and re-layouts, on_device(): all_keys[0]  4.37 us
  transfers between devices with their start and end apart: 5, of which 2 were waited for; matrix products, arithmetic and copies ran while one was open for 9% of the time, Pallas kernels for 0%

commit v1 on v0

--- a/solution.py
+++ b/solution.py
@@ -1,6 +1,10 @@
+import functools
+
 import jax
 import jax.numpy as jnp
 from jax import lax
+from jax.experimental import pallas as pl
+from jax.experimental.pallas import tpu as pltpu
 from jax.sharding import PartitionSpec as P
 
 HEAD_DIM = 128
@@ -31,7 +35,7 @@
     ).astype(jnp.int32)
 
 
-def on_device(queries, keys, values, out_weight, global_ids, rand_ids, rand_count):
+def general_path(queries, keys, values, out_weight, global_ids, rand_ids, rand_count):
     seq_count, seq_rows, local_width = queries.shape
     blocks_here = seq_rows // BLOCK
     heads_here = local_width // HEAD_DIM
@@ -135,6 +139,140 @@
     return projected.astype(jnp.bfloat16)
 
 
+def pack_kernel(me_ref, glob_ref, rand_ref, count_ref, q_ref, k_ref, v_ref, out_ref, *, ctx):
+    seq = pl.program_id(0)
+    me = me_ref[0]
+    rows = q_ref.shape[1]
+    blocks_here = rows // BLOCK
+    blocks = ctx * blocks_here
+    tiles = ctx * rows // HEAD_DIM
+    heads = q_ref.shape[2] // HEAD_DIM
+    key_block = (
+        lax.broadcasted_iota(jnp.int32, (tiles, HEAD_DIM), 0) * HEAD_DIM
+        + lax.broadcasted_iota(jnp.int32, (tiles, HEAD_DIM), 1)
+    ) // BLOCK
+    counts = []
+    for j in range(blocks_here):
+        block = me * blocks_here + j
+        listed = [lax.rem(block + blocks - 1, blocks), block, lax.rem(block + 1, blocks)]
+        listed += [glob_ref[seq, g] for g in range(GLOB)]
+        listed += [
+            jnp.where(r < count_ref[seq, j], rand_ref[seq, j, r], -1) for r in range(RMAX)
+        ]
+        counts.append(sum((key_block == one).astype(jnp.float32) for one in listed))
+    counts = jnp.concatenate(counts, 0).astype(jnp.bfloat16)
+    for h in range(heads):
+        cols = slice(h * HEAD_DIM, (h + 1) * HEAD_DIM)
+        out_ref[h, 0, 0:rows, :] = q_ref[0, :, cols]
+        out_ref[h, 0, rows : 2 * rows, :] = k_ref[0, :, cols]
+        out_ref[h, 0, 2 * rows : 3 * rows, :] = v_ref[0, :, cols]
+        out_ref[h, 0, 3 * rows :, :] = counts
+
+
+def attend_kernel(got_ref, out_ref, *, rows):
+    ctx = got_ref.shape[0]
+    blocks_here = rows // BLOCK
+    tiles = ctx * rows // HEAD_DIM
+    scale = HEAD_DIM ** (-0.5) * 1.4426950408889634
+    keys = jnp.concatenate([got_ref[c, rows : 2 * rows, :] for c in range(ctx)], 0)
+    values = jnp.concatenate([got_ref[c, 2 * rows : 3 * rows, :] for c in range(ctx)], 0)
+    for c in range(ctx):
+        counts = got_ref[c, 3 * rows :, :].astype(jnp.float32)
+        bias = jnp.where(counts > 0, jnp.log2(jnp.maximum(counts, 1.0)), -1e30)
+        scores = lax.dot_general(
+            got_ref[c, 0:rows, :], keys, (((1,), (1,)), ((), ())), preferred_element_type=jnp.float32
+        )
+        wide = jnp.concatenate(
+            [
+                jnp.concatenate(
+                    [
+                        jnp.broadcast_to(bias[j * tiles + i : j * tiles + i + 1, :], (BLOCK, HEAD_DIM))
+                        for i in range(tiles)
+                    ],
+                    1,
+                )
+                for j in range(blocks_here)
+            ],
+            0,
+        )
+        shifted = scores * scale + wide
+        weights = jnp.exp2(shifted - jnp.max(shifted, axis=1, keepdims=True))
+        total = jnp.sum(weights, axis=1, keepdims=True)
+        weighted = jnp.dot(weights.astype(jnp.bfloat16), values, preferred_element_type=jnp.float32)
+        out_ref[c] = (weighted / total).astype(jnp.bfloat16)
+
+
+def project_kernel(group_ref, own_ref, core_ref, far_ref, far_core_ref, weight_ref, out_ref):
+    group = group_ref[0]
+    heads, tokens, _ = own_ref.shape
+    depth = heads * HEAD_DIM
+    total = None
+    for flip, part in enumerate((own_ref, core_ref, far_ref, far_core_ref)):
+        start = pl.multiple_of((group ^ flip) * depth, depth)
+        features = jnp.concatenate([part[h] for h in range(heads)], 1)
+        term = jnp.dot(features, weight_ref[pl.ds(start, depth), :], preferred_element_type=jnp.float32)
+        total = term if total is None else total + term
+    out_ref[...] = total.astype(jnp.bfloat16)
+
+
+def pair_path(queries, keys, values, out_weight, global_ids, rand_ids, rand_count):
+    seqs, rows, local_width = queries.shape
+    heads = local_width // HEAD_DIM
+    ctx = lax.axis_size("ctx")
+    me = lax.axis_index("ctx").astype(jnp.int32).reshape(1)
+    group = lax.axis_index("head").astype(jnp.int32).reshape(1)
+    mask_rows = (rows // BLOCK) * (ctx * rows // HEAD_DIM)
+    high = 3 * rows + mask_rows
+    smem = pl.BlockSpec(memory_space=pltpu.SMEM)
+    vmem = pl.BlockSpec(memory_space=pltpu.VMEM)
+    token_spec = pl.BlockSpec((1, rows, local_width), lambda s: (s, 0, 0))
+    packed = pl.pallas_call(
+        functools.partial(pack_kernel, ctx=ctx),
+        grid=(seqs,),
+        in_specs=[smem, smem, smem, smem, token_spec, token_spec, token_spec],
+        out_specs=pl.BlockSpec((heads, 1, high, HEAD_DIM), lambda s: (0, s, 0, 0)),
+        out_shape=jax.ShapeDtypeStruct((heads, seqs, high, HEAD_DIM), jnp.bfloat16),
+        name="pack",
+    )(me, global_ids, rand_ids, rand_count, queries, keys, values)
+    got = lax.all_to_all(
+        packed.reshape(ctx, high, HEAD_DIM), "ctx", split_axis=0, concat_axis=0, tiled=True
+    )
+    attention = pl.pallas_call(
+        functools.partial(attend_kernel, rows=rows),
+        in_specs=[vmem],
+        out_specs=vmem,
+        out_shape=jax.ShapeDtypeStruct((ctx, rows, HEAD_DIM), jnp.bfloat16),
+        compiler_params=pltpu.CompilerParams(vmem_limit_bytes=32 << 20),
+        name="attend",
+    )(got)
+    own = lax.all_to_all(attention, "ctx", split_axis=0, concat_axis=0, tiled=True)
+    own = own.reshape(heads, seqs * rows, HEAD_DIM)
+    count = lax.axis_size("head")
+    flip = lambda part, bit: lax.ppermute(part, "head", [(i, i ^ bit) for i in range(count)])
+    core = flip(own, 1)
+    far = flip(own, 2)
+    far_core = flip(far, 1)
+    projected = pl.pallas_call(
+        project_kernel,
+        in_specs=[smem] + [vmem] * 5,
+        out_specs=vmem,
+        out_shape=jax.ShapeDtypeStruct((seqs * rows, out_weight.shape[1]), jnp.bfloat16),
+        compiler_params=pltpu.CompilerParams(vmem_limit_bytes=32 << 20),
+        name="project",
+    )(group, own, core, far, far_core, out_weight)
+    return projected.reshape(seqs, rows, out_weight.shape[1])
+
+
+def on_device(queries, keys, values, out_weight, global_ids, rand_ids, rand_count):
+    seqs, rows, local_width = queries.shape
+    pairs = seqs * (local_width // HEAD_DIM)
+    if pairs == lax.axis_size("ctx") and lax.axis_size("head") == 4 and rows == 2 * BLOCK:
+        path = pair_path
+    else:
+        path = general_path
+    return path(queries, keys, values, out_weight, global_ids, rand_ids, rand_count)
+
+
 def solution(mesh):
     placed = (
         P(None, "ctx", "head"),

time: 204 us -> 58.4 us (0.29)
  blocking collectives: 101 us -> 40.2 us
  local copies, waits for them, and re-layouts: 29.8 us -> 2.03 us
  waiting for transfers between devices: 21.4 us -> 6.38 us
  starting transfers between devices: 15.6 us -> 1.52 us
  other arithmetic: 14 us -> 0 us
  between operations: 13.5 us -> 0.02 us
  matrix products: 7.99 us -> 0 us
  Pallas kernels: 0 us -> 7.76 us
    psum x1 -> x0, blocking collectives: 101 us -> none  [on_device(): shared_rows = lax.psum(contribution, 'ctx').astype(jnp.bfloat16)]
    all_to_all x0 -> x2, blocking collectives: none -> 40.2 us  [the longest x1 28.9 us: pair_path(): lax.all_to_all(packed.reshape(ctx, high, HEAD_DIM), 'ctx', split_axis=0,...]
    all_gather x1 -> x0, waiting for transfers between devices: 16 us -> none  [on_device(): lax.all_gather(attention, 'head', axis=2, tiled=True)]
    all_to_all x2 -> x0, starting transfers between devices: 11 us -> none  [the longest x1 7.25 us: on_device(): lax.all_to_all(requests_out, 'ctx', split_axis=0, concat_axis=0, tiled=True)]
    dot_general x4 -> x0, matrix products: 7.99 us -> none  [the longest x1 2.78 us: on_device(): jnp.einsum('sgj,xsjtf->xsgtf', picker, own_blocks, preferred_element_type...]
    pallas_call x0 -> x3, Pallas kernels: none -> 7.76 us  [the longest x1 3.34 us: pair_path(): pl.pallas_call(functools.partial(pack_kernel, ctx=ctx), grid=(seqs,), in_...]
    squeeze x2 -> x0, local copies, waits for them, and re-layouts: 6.76 us -> none  [the longest x1 4.63 us: on_device(): all_keys[0]]
    ppermute x2 -> x3, waiting for transfers between devices: 0.01 us -> 6.38 us  [pair_path(): lax.ppermute(part, 'head', [(i, i ^ bit) for i in range(count)])]
  transfers between devices with their start and end apart: 5 -> 3, of which waited for: 2 -> 2; matrix products, arithmetic and copies ran while one was open for 9% -> 0% of each run, Pallas kernels for 0% -> 0%
where the time goes in v1:
time: 58.4 us; the launch traced here: 57.9 us
  blocking collectives  40.2 us (69%)
  Pallas kernels  7.76 us (13%)
  waiting for transfers between devices  6.38 us (11%)
  local copies, waits for them, and re-layouts  2.03 us (3%)
  starting transfers between devices  1.52 us (3%)
    all_to_all x1, blocking collectives, pair_path(): lax.all_to_all(packed.reshape(ctx, high, HEAD_DIM), 'ctx', split_axis=0,...  28.9 us
    all_to_all x1, blocking collectives, pair_path(): lax.all_to_all(attention, 'ctx', split_axis=0, concat_axis=0, tiled=True)  11.4 us
    ppermute x3, waiting for transfers between devices, pair_path(): lax.ppermute(part, 'head', [(i, i ^ bit) for i in range(count)])  6.38 us
    pallas_call x1, Pallas kernels, pair_path(): pl.pallas_call(functools.partial(pack_kernel, ctx=ctx), grid=(seqs,), in_...  3.34 us
    pallas_call x1, Pallas kernels, pair_path(): pl.pallas_call(functools.partial(attend_kernel, rows=rows), in_specs=[vme...  2.92 us
    unnamed x8, local copies, waits for them, and re-layouts  2.03 us
    ppermute x3, starting transfers between devices, pair_path(): lax.ppermute(part, 'head', [(i, i ^ bit) for i in range(count)])  1.52 us
    pallas_call x1, Pallas kernels, pair_path(): pl.pallas_call(project_kernel, in_specs=[smem] + [vmem] * 5, out_specs=vm...  1.5 us
  transfers between devices with their start and end apart: 3, of which 2 were waited for; matrix products, arithmetic and copies ran while one was open for 0% of the time, Pallas kernels for 0%

profile of v1, /device:TPU:0, one launch (start us, length us, event | category | flops | bytes accessed | tf_op | source)
XLA Modules:
  0.0 57.9 jit_solution(4084214121802772804)
XLA Ops:
  0.0 0.0 copy-start.1
  0.0 0.7 %copy-done.1 = s32[4,2]{0,1:T(2,128)S(1)} copy-done((s32[4,2]{0,1:T(2,128)S(1)}, s32[4,2]{0,1:T(2,128)}, u32[]{:S(2)}) %copy-start.1) | copy-done | bytes 56
  0.7 0.0 copy-start.2
  0.7 0.7 %copy.8.glob_ref = s32[4,2]{1,0:T(4,128)} copy(s32[4,2]{0,1:T(2,128)S(1)} %copy-done.1) | data formatting | bytes 64 | tf_op args[4]
  1.3 0.0 copy-done.2
  1.4 0.7 %copy.9.count_ref = s32[4,2]{1,0:T(4,128)} copy(s32[4,2]{0,1:T(2,128)S(1)} %copy-done.2) | data formatting | bytes 64 | tf_op args[6]
  2.0 3.3 %pack.1 = bf16[2,4,400,128]{3,2,1,0:T(8,128)(2,1)} custom-call(s32[1]{0:T(128)} %bitcast.1.me_ref, s32[4,2]{1,0:T(4,128)} %copy.8.glob_ref, s32[4,2,4]{2,1,0:T(2,128)} %rand_ref.1, s32[4,2]{1,0:T(4,128)} %copy.9.count_ref, bf16[4,128,256]{2,1,0:T(8,128)(2,1)} %q_ref.1, bf16[4,128,256]{2,1,0:T(8,128)(2,1)} %k_ref.1, bf16[4,128,256]{2,1,0:T(8,128)(2,1)} %v_ref.1), custom_call_target="tpu_custom_call" | custom-call | tf_op jit(solution)/shard_map/pack/pallas_call | solution.py:229
  5.4 28.9 %all_to_all.10.got_ref = bf16[8,400,128]{2,1,0:T(8,128)(2,1)S(1)} all-to-all(bf16[8,400,128]{2,1,0:T(8,128)(2,1)} %bitcast.8), channel_id=1, replica_groups=mesh['ctx'=8,'head'=4] {'ctx'}, dimensions={0} | all-to-all | bytes 1638400 | tf_op jit(solution)/shard_map/all_to_all | solution.py:237
  34.2 0.0 copy-start
  34.2 2.9 %attend.1 = bf16[8,128,128]{2,1,0:T(8,128)(2,1)S(1)} custom-call(bf16[8,400,128]{2,1,0:T(8,128)(2,1)S(1)} %all_to_all.10.got_ref), custom_call_target="tpu_custom_call" | custom-call | tf_op jit(solution)/shard_map/attend/pallas_call | solution.py:240
  37.2 11.4 %all_to_all.11 = bf16[8,128,128]{2,1,0:T(8,128)(2,1)S(1)} all-to-all(bf16[8,128,128]{2,1,0:T(8,128)(2,1)S(1)} %attend.1), channel_id=1, replica_groups=mesh['ctx'=8,'head'=4] {'ctx'}, dimensions={0} | all-to-all | bytes 524288 | tf_op jit(solution)/shard_map/all_to_all | solution.py:248
  48.5 1.5 %collective-permute-start.1 = (bf16[2,512,128]{2,1,0:T(8,128)(2,1)S(1)}, bf16[2,512,128]{2,1,0:T(8,128)(2,1)S(1)}, u32[]{:S(2)}, u32[]{:S(2)}) collective-permute-start(bf16[2,512,128]{2,1,0:T(8,128)(2,1)S(1)} %bitcast.5), channel_id=1, source_target_pairs={{0,2},{1,3},{2,0},{3,1},{4,6},{5,7},{6,4},{7,5},{8,10},{9,11},{10,... | collective-permute-start | bytes 786440 | tf_op jit(solution)/shard_map/ppermute | solution.py:251
  50.0 0.0 collective-permute-start
  50.1 4.9 %collective-permute-done.1.far_ref = bf16[2,512,128]{2,1,0:T(8,128)(2,1)S(1)} collective-permute-done((bf16[2,512,128]{2,1,0:T(8,128)(2,1)S(1)}, bf16[2,512,128]{2,1,0:T(8,128)(2,1)S(1)}, u32[]{:S(2)}, u32[]{:S(2)}) %collective-permute-start.1) | collective-permute-done | bytes 262176 | tf_op jit(solution)/shard_map/ppermute | solution.py:251
  54.9 0.0 collective-permute-start.2
  54.9 0.0 collective-permute-done.core_ref
  54.9 1.5 %collective-permute-done.2.far_core_ref = bf16[2,512,128]{2,1,0:T(8,128)(2,1)S(1)} collective-permute-done((bf16[2,512,128]{2,1,0:T(8,128)(2,1)S(1)}, bf16[2,512,128]{2,1,0:T(8,128)(2,1)S(1)}, u32[]{:S(2)}, u32[]{:S(2)}) %collective-permute-start.2) | collective-permute-done | bytes 262176 | tf_op jit(solution)/shard_map/ppermute | solution.py:251
  56.4 0.0 copy-done
  56.4 1.5 %project.1 = bf16[512,512]{1,0:T(8,128)(2,1)} custom-call(s32[1]{0:T(128)} %bitcast.group_ref, bf16[2,512,128]{2,1,0:T(8,128)(2,1)S(1)} %bitcast.7, bf16[2,512,128]{2,1,0:T(8,128)(2,1)S(1)} %collective-permute-done.core_ref, bf16[2,512,128]{2,1,0:T(8,128)(2,1)S(1)} %collective-permute-done.1.far_ref, ...), custom_call_target="tpu_custom_call" | custom-call | tf_op jit(solution)/shard_map/project/pallas_call | solution.py:255
Async XLA Ops:
  0.0 0.7 %copy-start.1 = (s32[4,2]{0,1:T(2,128)S(1)}, s32[4,2]{0,1:T(2,128)}, u32[]{:S(2)}) copy-start(s32[4,2]{0,1:T(2,128)} %param.11) | copy-start | bytes 100
  0.7 0.7 %copy-start.2 = (s32[4,2]{0,1:T(2,128)S(1)}, s32[4,2]{0,1:T(2,128)}, u32[]{:S(2)}) copy-start(s32[4,2]{0,1:T(2,128)} %param.13) | copy-start | bytes 100
  34.2 22.2 %copy-start = (bf16[1024,512]{1,0:T(8,128)(2,1)S(1)}, bf16[1024,512]{1,0:T(8,128)(2,1)}, u32[]{:S(2)}) copy-start(bf16[1024,512]{1,0:T(8,128)(2,1)} %weight_ref.1) | copy-start | bytes 3145732
  48.5 6.4 %collective-permute-start.1 = (bf16[2,512,128]{2,1,0:T(8,128)(2,1)S(1)}, bf16[2,512,128]{2,1,0:T(8,128)(2,1)S(1)}, u32[]{:S(2)}, u32[]{:S(2)}) collective-permute-start(bf16[2,512,128]{2,1,0:T(8,128)(2,1)S(1)} %bitcast.5), channel_id=1, source_target_pairs={{0,2},{1,3},{2,0},{3,1},{4,6},{5,7},{6,4},{7,5},{8,10},{9,11},{10,... | collective-permute-start | bytes 786440 | tf_op jit(solution)/shard_map/ppermute | solution.py:251
  50.0 4.9 %collective-permute-start = (bf16[2,512,128]{2,1,0:T(8,128)(2,1)S(1)}, bf16[2,512,128]{2,1,0:T(8,128)(2,1)S(1)}, u32[]{:S(2)}, u32[]{:S(2)}) collective-permute-start(bf16[2,512,128]{2,1,0:T(8,128)(2,1)S(1)} %bitcast.6), channel_id=1, source_target_pairs={{0,1},{1,0},{2,3},{3,2},{4,5},{5,4},{6,7},{7,6},{8,9},{9,8},{10,11... | collective-permute-start | bytes 786440 | tf_op jit(solution)/shard_map/ppermute | solution.py:251
  54.9 1.5 %collective-permute-start.2 = (bf16[2,512,128]{2,1,0:T(8,128)(2,1)S(1)}, bf16[2,512,128]{2,1,0:T(8,128)(2,1)S(1)}, u32[]{:S(2)}, u32[]{:S(2)}) collective-permute-start(bf16[2,512,128]{2,1,0:T(8,128)(2,1)S(1)} %collective-permute-done.1.far_ref), channel_id=1, source_target_pairs={{0,1},{1,0},{2,3},{3,2},{4,5},{5,4},{6,7},{7,6},{8,9},{9,8},{10,11... | collective-permute-start | bytes 786440 | tf_op jit(solution)/shard_map/ppermute | solution.py:251

commit v2 on v0

--- a/solution.py
+++ b/solution.py
@@ -1,6 +1,10 @@
+import functools
+
 import jax
 import jax.numpy as jnp
 from jax import lax
+from jax.experimental import pallas as pl
+from jax.experimental.pallas import tpu as pltpu
 from jax.sharding import PartitionSpec as P
 
 HEAD_DIM = 128
@@ -31,7 +35,7 @@
     ).astype(jnp.int32)
 
 
-def on_device(queries, keys, values, out_weight, global_ids, rand_ids, rand_count):
+def general_path(queries, keys, values, out_weight, global_ids, rand_ids, rand_count):
     seq_count, seq_rows, local_width = queries.shape
     blocks_here = seq_rows // BLOCK
     heads_here = local_width // HEAD_DIM
@@ -135,6 +139,227 @@
     return projected.astype(jnp.bfloat16)
 
 
+NEAR = (1, 2, 3)
+FAR = (4, 6, 5, 7)
+EARLY, LATE = FAR[:2], FAR[2:]
+
+
+def pack_kernel(me_ref, glob_ref, rand_ref, count_ref, q_ref, k_ref, v_ref, *outs, ctx):
+    seqs, rows, width = q_ref.shape
+    me = me_ref[0]
+    blocks_here = rows // BLOCK
+    blocks = ctx * blocks_here
+    tiles = ctx * rows // HEAD_DIM
+    mask_rows = blocks_here * tiles
+    tile = lax.broadcasted_iota(jnp.int32, (tiles, HEAD_DIM), 0)
+    lane = lax.broadcasted_iota(jnp.int32, (tiles, HEAD_DIM), 1)
+    for flip, out in zip(FAR + NEAR + (0,), outs):
+        asker = me ^ flip
+        seq = lax.rem(asker, seqs)
+        at = out.shape[0] - 2 * rows
+        out[at : at + rows, :] = k_ref[seq]
+        out[at + rows :, :] = v_ref[seq]
+        if not at:
+            continue
+        out[0:rows, :] = q_ref[seq]
+        key_block = ((tile ^ asker) * HEAD_DIM + lane) // BLOCK
+        counts = []
+        for j in range(blocks_here):
+            block = me * blocks_here + j
+            listed = [lax.rem(block + blocks - 1, blocks), block, lax.rem(block + 1, blocks)]
+            listed += [glob_ref[g, seq] for g in range(GLOB)]
+            listed += [
+                jnp.where(r < count_ref[j, seq], rand_ref[seq, j, r], -1) for r in range(RMAX)
+            ]
+            counts.append(sum((key_block == one).astype(jnp.float32) for one in listed))
+        counts = jnp.concatenate(counts, 0).astype(jnp.bfloat16)
+        for h in range(width // HEAD_DIM):
+            out[rows : rows + mask_rows, h * HEAD_DIM : (h + 1) * HEAD_DIM] = counts
+
+
+def scores_of(asker, holders, flips, cols, rows, tiles):
+    blocks_here = rows // BLOCK
+    mask_rows = blocks_here * tiles
+    scale = HEAD_DIM ** (-0.5) * 1.4426950408889634
+    keys = [ref[ref.shape[0] - 2 * rows : ref.shape[0] - rows, cols] for ref in holders]
+    scores = lax.dot_general(
+        asker[0:rows, cols],
+        jnp.concatenate(keys, 0),
+        (((1,), (1,)), ((), ())),
+        preferred_element_type=jnp.float32,
+    )
+    counts = asker[rows : rows + mask_rows, 0:HEAD_DIM].astype(jnp.float32)
+    bias = jnp.where(counts > 0, jnp.log2(jnp.maximum(counts, 1.0)), -1e30)
+    wide = jnp.concatenate(
+        [
+            jnp.concatenate(
+                [
+                    jnp.broadcast_to(bias[j * tiles + i : j * tiles + i + 1, :], (BLOCK, HEAD_DIM))
+                    for i in flips
+                ],
+                1,
+            )
+            for j in range(blocks_here)
+        ],
+        0,
+    )
+    return scores * scale + wide
+
+
+def weigh(weights, holders, cols, rows):
+    values = [ref[ref.shape[0] - rows :, cols] for ref in holders]
+    return jnp.dot(
+        weights.astype(jnp.bfloat16), jnp.concatenate(values, 0), preferred_element_type=jnp.float32
+    )
+
+
+def near_kernel(*refs, rows, tiles, flips):
+    *holders, out_ref = refs
+    askers = holders[: len(holders) - len(flips)]
+    heads = askers[0].shape[1] // HEAD_DIM
+    for n, asker in enumerate(askers):
+        for h in range(heads):
+            cols = slice(h * HEAD_DIM, (h + 1) * HEAD_DIM)
+            shifted = scores_of(asker, holders, tuple(range(len(askers))) + flips, cols, rows, tiles)
+            peak = jnp.max(shifted, axis=1, keepdims=True)
+            weights = jnp.exp2(shifted - peak)
+            full = (rows, HEAD_DIM)
+            out_ref[0, n * heads + h] = weigh(weights, holders, cols, rows)
+            out_ref[1, n * heads + h] = jnp.broadcast_to(peak, full)
+            out_ref[2, n * heads + h] = jnp.broadcast_to(jnp.sum(weights, axis=1, keepdims=True), full)
+
+
+def far_kernel(me_ref, *refs, rows, tiles, flips, copies):
+    *askers, before, out_ref = refs
+    askers, holders = askers[: -len(flips)], askers[-len(flips) :]
+    heads = askers[0].shape[1] // HEAD_DIM
+    spot = lax.rem(me_ref[0], len(askers))
+    for n, asker in enumerate(askers):
+        for h in range(heads):
+            cols = slice(h * HEAD_DIM, (h + 1) * HEAD_DIM)
+            shifted = scores_of(asker, holders, flips, cols, rows, tiles)
+            old = before[1, n * heads + h]
+            peak = jnp.maximum(old, jnp.max(shifted, axis=1, keepdims=True))
+            weights = jnp.exp2(shifted - jnp.concatenate([peak] * len(flips), 1))
+            keep = jnp.exp2(old - peak)
+            total = keep * before[2, n * heads + h] + jnp.sum(weights, axis=1, keepdims=True)
+            weighted = keep * before[0, n * heads + h] + weigh(weights, holders, cols, rows)
+            result = (weighted / total).astype(jnp.bfloat16)
+            for copy in range(copies):
+                out_ref[(spot ^ n) * copies + copy, :, cols] = result
+
+
+def project_kernel(group_ref, *refs, flip):
+    *before, part_ref, weight_ref, out_ref = refs
+    slots, rows, depth = part_ref.shape
+    seqs = out_ref.shape[0]
+    sides = slots // seqs
+    core = lax.rem(group_ref[0], weight_ref.shape[0] // (depth * sides)) ^ flip
+    weights = [
+        weight_ref[pl.ds(pl.multiple_of((side * sides + core) * depth, depth), depth), :]
+        for side in range(sides)
+    ]
+    for seq in range(seqs):
+        total = before[0][seq] if before else 0.0
+        for side in range(sides):
+            total = total + jnp.dot(
+                part_ref[seq * sides + side], weights[side], preferred_element_type=jnp.float32
+            )
+        out_ref[seq] = total.astype(out_ref.dtype)
+
+
+def half_path(queries, keys, values, out_weight, global_ids, rand_ids, rand_count):
+    seqs, rows, local_width = queries.shape
+    ctx = lax.axis_size("ctx")
+    groups = lax.axis_size("head")
+    me = lax.axis_index("ctx").astype(jnp.int32).reshape(1)
+    group = lax.axis_index("head").astype(jnp.int32).reshape(1)
+    heads = local_width // HEAD_DIM
+    tiles = ctx * rows // HEAD_DIM
+    mask_rows = rows // BLOCK * tiles
+    smem = pl.BlockSpec(memory_space=pltpu.SMEM)
+    vmem = pl.BlockSpec(memory_space=pltpu.VMEM)
+    room = pltpu.CompilerParams(vmem_limit_bytes=32 << 20)
+    tall = lambda high: jax.ShapeDtypeStruct((high, local_width), jnp.bfloat16)
+    shapes = [tall(2 * rows)] * len(FAR) + [tall(3 * rows + mask_rows)] * (len(NEAR) + 1)
+    *sent, own = pl.pallas_call(
+        functools.partial(pack_kernel, ctx=ctx),
+        in_specs=[smem] * 4 + [vmem] * 3,
+        out_specs=[vmem] * len(shapes),
+        out_shape=shapes,
+        name="pack",
+    )(me, global_ids.T, rand_ids, rand_count.T, queries, keys, values)
+    sent = dict(zip(FAR + NEAR, sent))
+    got = {
+        flip: lax.ppermute(sent[flip], "ctx", [(i, i ^ flip) for i in range(ctx)])
+        for flip in (1, 4, 6, 2, 5, 3, 7)
+    }
+    near = [own] + [got[flip] for flip in NEAR]
+    pairs = heads * (seqs * rows) ** 2
+    cost = pl.CostEstimate(
+        flops=4 * pairs * HEAD_DIM, bytes_accessed=8 * seqs * rows * local_width, transcendentals=pairs
+    )
+    so_far = pl.pallas_call(
+        functools.partial(near_kernel, rows=rows, tiles=tiles, flips=EARLY),
+        in_specs=[vmem] * (len(near) + len(EARLY)),
+        out_specs=vmem,
+        out_shape=jax.ShapeDtypeStruct((3, seqs * heads, rows, HEAD_DIM), jnp.float32),
+        compiler_params=room,
+        cost_estimate=cost,
+        name="attend_near",
+    )(*near, *[got[flip] for flip in EARLY])
+    sides = 2
+    attention = pl.pallas_call(
+        functools.partial(far_kernel, rows=rows, tiles=tiles, flips=LATE, copies=sides),
+        in_specs=[smem] + [vmem] * (len(near) + len(LATE) + 1),
+        out_specs=vmem,
+        out_shape=jax.ShapeDtypeStruct((seqs * sides, rows, local_width), jnp.bfloat16),
+        compiler_params=room,
+        cost_estimate=cost,
+        name="attend_far",
+    )(me, *near, *[got[flip] for flip in LATE], so_far)
+    cores = groups // sides
+    home = lax.all_to_all(
+        attention,
+        ("ctx", "head"),
+        split_axis=0,
+        concat_axis=0,
+        tiled=True,
+        axis_index_groups=[
+            [(half * seqs + c) * groups + side * cores + core for c in range(seqs) for side in range(sides)]
+            for half in range(ctx // seqs)
+            for core in range(cores)
+        ],
+    )
+    beside = lax.ppermute(home, "head", [(i, i ^ 1) for i in range(groups)])
+    width = out_weight.shape[1]
+
+    def project(flip, dtype, *parts):
+        return pl.pallas_call(
+            functools.partial(project_kernel, flip=flip),
+            in_specs=[smem] + [vmem] * (len(parts) + 1),
+            out_specs=vmem,
+            out_shape=jax.ShapeDtypeStruct((seqs, rows, width), dtype),
+            compiler_params=room,
+            cost_estimate=pl.CostEstimate(
+                flops=seqs * rows * width * out_weight.shape[0],
+                bytes_accessed=4 * seqs * rows * width,
+                transcendentals=0,
+            ),
+            name="project",
+        )(group, *parts, out_weight)
+
+    return project(1, jnp.bfloat16, project(0, jnp.float32, home), beside)
+
+
+def on_device(queries, keys, values, out_weight, global_ids, rand_ids, rand_count):
+    seqs, rows, local_width = queries.shape
+    ctx, groups = lax.axis_size("ctx"), lax.axis_size("head")
+    fits = ctx == 2 * seqs == 8 and groups == 4 and rows == HEAD_DIM == 2 * BLOCK
+    path = half_path if fits else general_path
+    return path(queries, keys, values, out_weight, global_ids, rand_ids, rand_count)
+
+
 def solution(mesh):
     placed = (
         P(None, "ctx", "head"),

time: 204 us -> 48.5 us (0.24)
  blocking collectives: 101 us -> 10.8 us
  local copies, waits for them, and re-layouts: 29.8 us -> 0.94 us
  other arithmetic: 14 us -> 0 us
  between operations: 13.5 us -> 0.06 us
  matrix products: 7.99 us -> 0 us
  Pallas kernels: 0 us -> 7.49 us
  waiting for transfers between devices: 21.4 us -> 16.4 us
  starting transfers between devices: 15.6 us -> 12.6 us
    psum x1 -> x0, blocking collectives: 101 us -> none  [on_device(): shared_rows = lax.psum(contribution, 'ctx').astype(jnp.bfloat16)]
    ppermute x2 -> x8, waiting for transfers between devices: 0.01 us -> 16.4 us  [the longest x7 14.9 us: half_path(): lax.ppermute(sent[flip], 'ctx', [(i, i ^ flip) for i in range(ctx)])]
    all_gather x1 -> x0, waiting for transfers between devices: 16 us -> none  [on_device(): lax.all_gather(attention, 'head', axis=2, tiled=True)]
    all_to_all x2 -> x0, starting transfers between devices: 11 us -> none  [the longest x1 7.25 us: on_device(): lax.all_to_all(requests_out, 'ctx', split_axis=0, concat_axis=0, tiled=True)]
    all_to_all x0 -> x1, blocking collectives: none -> 10.8 us  [half_path(): lax.all_to_all(attention, ('ctx', 'head'), split_axis=0, concat_axis=0, t...]
    ppermute x2 -> x8, starting transfers between devices: 4.61 us -> 12.6 us  [the longest x7 12.6 us: half_path(): lax.ppermute(sent[flip], 'ctx', [(i, i ^ flip) for i in range(ctx)])]
    dot_general x4 -> x0, matrix products: 7.99 us -> none  [the longest x1 2.78 us: on_device(): jnp.einsum('sgj,xsjtf->xsgtf', picker, own_blocks, preferred_element_type...]
    pallas_call x0 -> x5, Pallas kernels: none -> 7.49 us  [the longest x1 2.61 us: half_path(): pl.pallas_call(functools.partial(near_kernel, rows=rows, tiles=tiles, fli...]
  transfers between devices with their start and end apart: 5 -> 8, of which waited for: 2 -> 4; matrix products, arithmetic and copies ran while one was open for 9% -> 0% of each run, Pallas kernels for 0% -> 6%
where the time goes in v2:
time: 48.5 us; the launch traced here: 48.3 us
  waiting for transfers between devices  16.4 us (34%)
  starting transfers between devices  12.6 us (26%)
  blocking collectives  10.8 us (22%)
  Pallas kernels  7.49 us (15%)
  local copies, waits for them, and re-layouts  0.94 us (2%)
    ppermute x7, waiting for transfers between devices, half_path(): lax.ppermute(sent[flip], 'ctx', [(i, i ^ flip) for i in range(ctx)])  14.9 us
    ppermute x7, starting transfers between devices, half_path(): lax.ppermute(sent[flip], 'ctx', [(i, i ^ flip) for i in range(ctx)])  12.6 us
    all_to_all x1, blocking collectives, half_path(): lax.all_to_all(attention, ('ctx', 'head'), split_axis=0, concat_axis=0, t...  10.8 us
    pallas_call x1, Pallas kernels, half_path(): pl.pallas_call(functools.partial(near_kernel, rows=rows, tiles=tiles, fli...  2.61 us
    pallas_call x1, Pallas kernels, half_path(): pl.pallas_call(functools.partial(pack_kernel, ctx=ctx), in_specs=[smem] *...  2.26 us
    pallas_call x2, Pallas kernels, project(): pl.pallas_call(functools.partial(project_kernel, flip=flip), in_specs=[sm...  1.71 us
    ppermute x1, waiting for transfers between devices, half_path(): beside = lax.ppermute(home, 'head', [(i, i ^ 1) for i in range(groups)])  1.45 us
  transfers between devices with their start and end apart: 8, of which 4 were waited for; matrix products, arithmetic and copies ran while one was open for 0% of the time, Pallas kernels for 6%

profile of v2, /device:TPU:0, one launch (start us, length us, event | category | flops | bytes accessed | tf_op | source)
XLA Modules:
  0.0 48.3 jit_solution(12857287558823063906)
XLA Ops:
  0.0 2.3 %pack.1 = (bf16[256,256]{1,0:T(8,128)(2,1)}, bf16[256,256]{1,0:T(8,128)(2,1)}, bf16[256,256]{1,0:T(8,128)(2,1)}, bf16[256,256]{1,0:T(8,128)(2,1)}, bf16[400,256]...) custom-call(s32[1]{0:T(128)} %bitcast.1.me_ref, s32[2,4]{1,0:T(2,128)} %bitcast.4, ...), custom_call_target="tpu_custom_call" | custom-call | tf_op jit(solution)/shard_map/pack/pallas_call | solution.py:285
  2.3 4.0 %collective-permute-start.5 = (bf16[256,256]{1,0:T(8,128)(2,1)}, bf16[256,256]{1,0:T(8,128)(2,1)S(1)}, u32[]{:S(2)}, u32[]{:S(2)}) collective-permute-start(bf16[256,256]{1,0:T(8,128)(2,1)} %get-tuple-element.19), channel_id=1, source_target_pairs={{0,16},{4,20},{8,24},{12,28},{16,0},{20,4},{24,8},{28,12},{1,17},{... | collective-permute-start | bytes 393224 | tf_op jit(solution)/shard_map/ppermute | solution.py:294
  6.3 1.3 %collective-permute-start.6 = (bf16[256,256]{1,0:T(8,128)(2,1)}, bf16[256,256]{1,0:T(8,128)(2,1)S(1)}, u32[]{:S(2)}, u32[]{:S(2)}) collective-permute-start(bf16[256,256]{1,0:T(8,128)(2,1)} %get-tuple-element.20), channel_id=1, source_target_pairs={{0,24},{4,28},{8,16},{12,20},{16,8},{20,12},{24,0},{28,4},{1,25},{... | collective-permute-start | bytes 393224 | tf_op jit(solution)/shard_map/ppermute | solution.py:294
  7.6 1.5 %collective-permute-start = (bf16[400,256]{1,0:T(8,128)(2,1)}, bf16[400,256]{1,0:T(8,128)(2,1)S(1)}, u32[]{:S(2)}, u32[]{:S(2)}) collective-permute-start(bf16[400,256]{1,0:T(8,128)(2,1)} %get-tuple-element.14), channel_id=1, source_target_pairs={{0,4},{4,0},{8,12},{12,8},{16,20},{20,16},{24,28},{28,24},{1,5},{5... | collective-permute-start | bytes 614408 | tf_op jit(solution)/shard_map/ppermute | solution.py:294
  9.1 0.2 collective-permute-start.1
  9.4 1.8 %collective-permute-start.2 = (bf16[400,256]{1,0:T(8,128)(2,1)}, bf16[400,256]{1,0:T(8,128)(2,1)S(1)}, u32[]{:S(2)}, u32[]{:S(2)}) collective-permute-start(bf16[400,256]{1,0:T(8,128)(2,1)} %get-tuple-element.16), channel_id=1, source_target_pairs={{0,12},{4,8},{8,4},{12,0},{16,28},{20,24},{24,20},{28,16},{1,13},{... | collective-permute-start | bytes 614408 | tf_op jit(solution)/shard_map/ppermute | solution.py:294
  11.1 5.4 %collective-permute-done.5.refs_4_ = bf16[256,256]{1,0:T(8,128)(2,1)S(1)} collective-permute-done((bf16[256,256]{1,0:T(8,128)(2,1)}, bf16[256,256]{1,0:T(8,128)(2,1)S(1)}, u32[]{:S(2)}, u32[]{:S(2)}) %collective-permute-start.5) | collective-permute-done | bytes 131104 | tf_op jit(solution)/shard_map/ppermute | solution.py:294
  16.5 0.9 %collective-permute-start.3 = (bf16[256,256]{1,0:T(8,128)(2,1)}, bf16[256,256]{1,0:T(8,128)(2,1)S(1)}, u32[]{:S(2)}, u32[]{:S(2)}) collective-permute-start(bf16[256,256]{1,0:T(8,128)(2,1)} %get-tuple-element.17), channel_id=1, source_target_pairs={{0,20},{4,16},{8,28},{12,24},{16,4},{20,0},{24,12},{28,8},{1,21},{... | collective-permute-start | bytes 393224 | tf_op jit(solution)/shard_map/ppermute | solution.py:294
  17.4 0.0 collective-permute-done.6.refs_5_
  17.4 2.8 %collective-permute-start.4 = (bf16[256,256]{1,0:T(8,128)(2,1)}, bf16[256,256]{1,0:T(8,128)(2,1)S(1)}, u32[]{:S(2)}, u32[]{:S(2)}) collective-permute-start(bf16[256,256]{1,0:T(8,128)(2,1)} %get-tuple-element.18), channel_id=1, source_target_pairs={{0,28},{4,24},{8,20},{12,16},{16,12},{20,8},{24,4},{28,0},{1,29},{... | collective-permute-start | bytes 393224 | tf_op jit(solution)/shard_map/ppermute | solution.py:294
  20.2 0.0 collective-permute-done.refs_1_
  20.2 1.3 %collective-permute-done.1.refs_2_ = bf16[400,256]{1,0:T(8,128)(2,1)S(1)} collective-permute-done((bf16[400,256]{1,0:T(8,128)(2,1)}, bf16[400,256]{1,0:T(8,128)(2,1)S(1)}, u32[]{:S(2)}, u32[]{:S(2)}) %collective-permute-start.1) | collective-permute-done | bytes 204832 | tf_op jit(solution)/shard_map/ppermute | solution.py:294
  21.6 8.2 %collective-permute-done.2.refs_3_ = bf16[400,256]{1,0:T(8,128)(2,1)S(1)} collective-permute-done((bf16[400,256]{1,0:T(8,128)(2,1)}, bf16[400,256]{1,0:T(8,128)(2,1)S(1)}, u32[]{:S(2)}, u32[]{:S(2)}) %collective-permute-start.2) | collective-permute-done | bytes 204832 | tf_op jit(solution)/shard_map/ppermute | solution.py:294
  29.8 0.0 copy-start.1
  29.8 0.9 %copy-done.1 = bf16[400,256]{1,0:T(8,128)(2,1)S(1)} copy-done((bf16[400,256]{1,0:T(8,128)(2,1)S(1)}, bf16[400,256]{1,0:T(8,128)(2,1)}, u32[]{:S(2)}) %copy-start.1) | copy-done | bytes 204824
  30.7 0.0 copy-start.2
  30.7 2.6 %attend_near.1.refs_6_ = f32[3,8,128,128]{3,2,1,0:T(8,128)S(1)} custom-call(bf16[400,256]{1,0:T(8,128)(2,1)S(1)} %copy-done.1, bf16[400,256]{1,0:T(8,128)(2,1)S(1)} %collective-permute-done.refs_1_, bf16[400,256]{1,0:T(8,128)(2,1)S(1)} %collective-permute-done.1.refs_2_, bf16[400,256]{1,0:T(8,128)(2,1)S(1)} %collective-permute-done.2.refs_3_, ...), custom_call_target="tpu_custom_call" | custom-call | flops 268435456 | bytes 1048576 | tf_op jit(solution)/shard_map/attend_near/pallas_call | solution.py:302
  33.4 0.0 copy-start
  33.4 0.0 collective-permute-done.3.refs_4_
  33.4 0.0 collective-permute-done.4.refs_5_
  33.4 0.0 copy-done.2
  33.4 0.9 %attend_far.1 = bf16[8,128,256]{2,1,0:T(8,128)(2,1)S(1)} custom-call(s32[1]{0:T(128)} %bitcast.1.me_ref, bf16[400,256]{1,0:T(8,128)(2,1)S(1)} %copy-done.2, bf16[400,256]{1,0:T(8,128)(2,1)S(1)} %collective-permute-done.refs_1_, bf16[400,256]{1,0:T(8,128)(2,1)S(1)} %collective-permute-done.1.refs_2_, bf16[400,256]{1,0:T(8,128)(2,1)S(1)} %collective-permute-done.2.refs_3_, ...), custom_call_target="tpu_custom_call" | custom-call | flops 268435456 | bytes 1048576 | tf_op jit(solution)/shard_map/attend_far/pallas_call | solution.py:312
  34.3 10.8 %all_to_all.5.refs_0_ = bf16[8,128,256]{2,1,0:T(8,128)(2,1)S(1)} all-to-all(bf16[8,128,256]{2,1,0:T(8,128)(2,1)S(1)} %attend_far.1), channel_id=1, replica_groups={{0,2,4,6,8,10,12,14},{1,3,5,7,9,11,13,15},{16,18,20,22,24,26,28,30},{17..., dimensions={0} | all-to-all | bytes 1048576 | tf_op jit(solution)/shard_map/all_to_all | solution.py:322
  45.1 0.0 collective-permute-start.7
  45.1 0.0 copy-done
  45.1 0.4 project.2.refs_0_
  45.6 1.5 %collective-permute-done.7.refs_1_ = bf16[8,128,256]{2,1,0:T(8,128)(2,1)S(1)} collective-permute-done((bf16[8,128,256]{2,1,0:T(8,128)(2,1)S(1)}, bf16[8,128,256]{2,1,0:T(8,128)(2,1)S(1)}, u32[]{:S(2)}, u32[]{:S(2)}) %collective-permute-start.7) | collective-permute-done | bytes 524320 | tf_op jit(solution)/shard_map/ppermute | solution.py:334
  47.0 1.3 %project.3 = bf16[4,128,512]{2,1,0:T(8,128)(2,1)} custom-call(s32[1]{0:T(128)} %bitcast.group_ref, f32[4,128,512]{2,1,0:T(8,128)S(1)} %project.2.refs_0_, bf16[8,128,256]{2,1,0:T(8,128)(2,1)S(1)} %collective-permute-done.7.refs_1_, bf16[1024,512]{1,0:T(8,128)(2,1)S(1)} %copy-done), custom_call_target="tpu_custom_call" | custom-call | flops 268435456 | bytes 1048576 | tf_op jit(solution)/shard_map/project/pallas_call | solution.py:338
Async XLA Ops:
  2.3 14.2 %collective-permute-start.5 = (bf16[256,256]{1,0:T(8,128)(2,1)}, bf16[256,256]{1,0:T(8,128)(2,1)S(1)}, u32[]{:S(2)}, u32[]{:S(2)}) collective-permute-start(bf16[256,256]{1,0:T(8,128)(2,1)} %get-tuple-element.19), channel_id=1, source_target_pairs={{0,16},{4,20},{8,24},{12,28},{16,0},{20,4},{24,8},{28,12},{1,17},{... | collective-permute-start | bytes 393224 | tf_op jit(solution)/shard_map/ppermute | solution.py:294
  6.3 11.1 %collective-permute-start.6 = (bf16[256,256]{1,0:T(8,128)(2,1)}, bf16[256,256]{1,0:T(8,128)(2,1)S(1)}, u32[]{:S(2)}, u32[]{:S(2)}) collective-permute-start(bf16[256,256]{1,0:T(8,128)(2,1)} %get-tuple-element.20), channel_id=1, source_target_pairs={{0,24},{4,28},{8,16},{12,20},{16,8},{20,12},{24,0},{28,4},{1,25},{... | collective-permute-start | bytes 393224 | tf_op jit(solution)/shard_map/ppermute | solution.py:294
  7.6 12.6 %collective-permute-start = (bf16[400,256]{1,0:T(8,128)(2,1)}, bf16[400,256]{1,0:T(8,128)(2,1)S(1)}, u32[]{:S(2)}, u32[]{:S(2)}) collective-permute-start(bf16[400,256]{1,0:T(8,128)(2,1)} %get-tuple-element.14), channel_id=1, source_target_pairs={{0,4},{4,0},{8,12},{12,8},{16,20},{20,16},{24,28},{28,24},{1,5},{5... | collective-permute-start | bytes 614408 | tf_op jit(solution)/shard_map/ppermute | solution.py:294
  9.1 12.4 %collective-permute-start.1 = (bf16[400,256]{1,0:T(8,128)(2,1)}, bf16[400,256]{1,0:T(8,128)(2,1)S(1)}, u32[]{:S(2)}, u32[]{:S(2)}) collective-permute-start(bf16[400,256]{1,0:T(8,128)(2,1)} %get-tuple-element.15), channel_id=1, source_target_pairs={{0,8},{4,12},{8,0},{12,4},{16,24},{20,28},{24,16},{28,20},{1,9},{5... | collective-permute-start | bytes 614408 | tf_op jit(solution)/shard_map/ppermute | solution.py:294
  9.4 20.4 %collective-permute-start.2 = (bf16[400,256]{1,0:T(8,128)(2,1)}, bf16[400,256]{1,0:T(8,128)(2,1)S(1)}, u32[]{:S(2)}, u32[]{:S(2)}) collective-permute-start(bf16[400,256]{1,0:T(8,128)(2,1)} %get-tuple-element.16), channel_id=1, source_target_pairs={{0,12},{4,8},{8,4},{12,0},{16,28},{20,24},{24,20},{28,16},{1,13},{... | collective-permute-start | bytes 614408 | tf_op jit(solution)/shard_map/ppermute | solution.py:294
  16.5 16.9 %collective-permute-start.3 = (bf16[256,256]{1,0:T(8,128)(2,1)}, bf16[256,256]{1,0:T(8,128)(2,1)S(1)}, u32[]{:S(2)}, u32[]{:S(2)}) collective-permute-start(bf16[256,256]{1,0:T(8,128)(2,1)} %get-tuple-element.17), channel_id=1, source_target_pairs={{0,20},{4,16},{8,28},{12,24},{16,4},{20,0},{24,12},{28,8},{1,21},{... | collective-permute-start | bytes 393224 | tf_op jit(solution)/shard_map/ppermute | solution.py:294
  17.4 16.0 %collective-permute-start.4 = (bf16[256,256]{1,0:T(8,128)(2,1)}, bf16[256,256]{1,0:T(8,128)(2,1)S(1)}, u32[]{:S(2)}, u32[]{:S(2)}) collective-permute-start(bf16[256,256]{1,0:T(8,128)(2,1)} %get-tuple-element.18), channel_id=1, source_target_pairs={{0,28},{4,24},{8,20},{12,16},{16,12},{20,8},{24,4},{28,0},{1,29},{... | collective-permute-start | bytes 393224 | tf_op jit(solution)/shard_map/ppermute | solution.py:294
  29.8 0.9 %copy-start.1 = (bf16[400,256]{1,0:T(8,128)(2,1)S(1)}, bf16[400,256]{1,0:T(8,128)(2,1)}, u32[]{:S(2)}) copy-start(bf16[400,256]{1,0:T(8,128)(2,1)} %get-tuple-element.13.refs_0_) | copy-start | bytes 614404
  30.7 2.7 %copy-start.2 = (bf16[400,256]{1,0:T(8,128)(2,1)S(1)}, bf16[400,256]{1,0:T(8,128)(2,1)}, u32[]{:S(2)}) copy-start(bf16[400,256]{1,0:T(8,128)(2,1)} %get-tuple-element.13.refs_0_) | copy-start | bytes 614404
  33.4 11.7 %copy-start = (bf16[1024,512]{1,0:T(8,128)(2,1)S(1)}, bf16[1024,512]{1,0:T(8,128)(2,1)}, u32[]{:S(2)}) copy-start(bf16[1024,512]{1,0:T(8,128)(2,1)} %refs_2_.1) | copy-start | bytes 3145732
  45.1 1.9 %collective-permute-start.7 = (bf16[8,128,256]{2,1,0:T(8,128)(2,1)S(1)}, bf16[8,128,256]{2,1,0:T(8,128)(2,1)S(1)}, u32[]{:S(2)}, u32[]{:S(2)}) collective-permute-start(bf16[8,128,256]{2,1,0:T(8,128)(2,1)S(1)} %all_to_all.5.refs_0_), channel_id=1, source_target_pairs={{0,1},{1,0},{2,3},{3,2},{4,5},{5,4},{6,7},{7,6},{8,9},{9,8},{10,11... | collective-permute-start | bytes 1572872 | tf_op jit(solution)/shard_map/ppermute | solution.py:334

commit v3 on v2

--- a/solution.py
+++ b/solution.py
@@ -144,25 +144,39 @@
 EARLY, LATE = FAR[:2], FAR[2:]
 
 
-def pack_kernel(me_ref, glob_ref, rand_ref, count_ref, q_ref, k_ref, v_ref, *outs, ctx):
+def pack_near_kernel(me_ref, glob_hbm, rand_hbm, count_hbm, q_ref, k_ref, v_ref, *refs, ctx):
+    near_ref, glob_ref, rand_ref, count_ref, id_sems, sems = refs
     seqs, rows, width = q_ref.shape
     me = me_ref[0]
+    base = me - lax.rem(me, seqs)
     blocks_here = rows // BLOCK
     blocks = ctx * blocks_here
     tiles = ctx * rows // HEAD_DIM
     mask_rows = blocks_here * tiles
+    ids = [
+        pltpu.make_async_copy(src, dst, id_sems.at[i])
+        for i, (src, dst) in enumerate(
+            ((glob_hbm, glob_ref), (rand_hbm, rand_ref), (count_hbm, count_ref))
+        )
+    ]
+    copies = [
+        pltpu.make_async_copy(
+            source.at[seq], near_ref.at[seq, pl.ds(start, rows), :], sems.at[3 * seq + i]
+        )
+        for seq in range(seqs)
+        for i, (source, start) in enumerate(
+            ((q_ref, 0), (k_ref, rows + mask_rows), (v_ref, 2 * rows + mask_rows))
+        )
+    ]
+    for copy in ids + copies:
+        copy.start()
+    for copy in ids:
+        copy.wait()
     tile = lax.broadcasted_iota(jnp.int32, (tiles, HEAD_DIM), 0)
     lane = lax.broadcasted_iota(jnp.int32, (tiles, HEAD_DIM), 1)
-    for flip, out in zip(FAR + NEAR + (0,), outs):
-        asker = me ^ flip
-        seq = lax.rem(asker, seqs)
-        at = out.shape[0] - 2 * rows
-        out[at : at + rows, :] = k_ref[seq]
-        out[at + rows :, :] = v_ref[seq]
-        if not at:
-            continue
-        out[0:rows, :] = q_ref[seq]
-        key_block = ((tile ^ asker) * HEAD_DIM + lane) // BLOCK
+    for seq in range(seqs):
+        holder = jnp.where(tile < seqs, base + tile, (base + seq) ^ tile)
+        key_block = (holder * HEAD_DIM + lane) // BLOCK
         counts = []
         for j in range(blocks_here):
             block = me * blocks_here + j
@@ -174,79 +188,74 @@
             counts.append(sum((key_block == one).astype(jnp.float32) for one in listed))
         counts = jnp.concatenate(counts, 0).astype(jnp.bfloat16)
         for h in range(width // HEAD_DIM):
-            out[rows : rows + mask_rows, h * HEAD_DIM : (h + 1) * HEAD_DIM] = counts
-
-
-def scores_of(asker, holders, flips, cols, rows, tiles):
+            near_ref[seq, rows : rows + mask_rows, h * HEAD_DIM : (h + 1) * HEAD_DIM] = counts
+    for copy in copies:
+        copy.wait()
+
+
+def stack_kernel(*refs):
+    *parts, out_ref = refs
+    for n, part in enumerate(parts):
+        out_ref[n] = part[...]
+
+
+def pieces_of(near_ref, early_ref, late_refs):
+    pieces = [near_ref.at[n] for n in range(near_ref.shape[0])]
+    return pieces + [early_ref.at[n] for n in range(early_ref.shape[0])] + list(late_refs)
+
+
+def weigh_kernel(near_ref, early_ref, *refs, rows, tiles):
+    *late_refs, weights_ref = refs
+    pieces = pieces_of(near_ref, early_ref, late_refs)
+    askers, _, width = near_ref.shape
     blocks_here = rows // BLOCK
-    mask_rows = blocks_here * tiles
+    heads = width // HEAD_DIM
     scale = HEAD_DIM ** (-0.5) * 1.4426950408889634
-    keys = [ref[ref.shape[0] - 2 * rows : ref.shape[0] - rows, cols] for ref in holders]
-    scores = lax.dot_general(
-        asker[0:rows, cols],
-        jnp.concatenate(keys, 0),
-        (((1,), (1,)), ((), ())),
-        preferred_element_type=jnp.float32,
-    )
-    counts = asker[rows : rows + mask_rows, 0:HEAD_DIM].astype(jnp.float32)
-    bias = jnp.where(counts > 0, jnp.log2(jnp.maximum(counts, 1.0)), -1e30)
-    wide = jnp.concatenate(
-        [
-            jnp.concatenate(
-                [
-                    jnp.broadcast_to(bias[j * tiles + i : j * tiles + i + 1, :], (BLOCK, HEAD_DIM))
-                    for i in flips
-                ],
-                1,
-            )
-            for j in range(blocks_here)
-        ],
-        0,
-    )
-    return scores * scale + wide
-
-
-def weigh(weights, holders, cols, rows):
-    values = [ref[ref.shape[0] - rows :, cols] for ref in holders]
-    return jnp.dot(
-        weights.astype(jnp.bfloat16), jnp.concatenate(values, 0), preferred_element_type=jnp.float32
-    )
-
-
-def near_kernel(*refs, rows, tiles, flips):
-    *holders, out_ref = refs
-    askers = holders[: len(holders) - len(flips)]
-    heads = askers[0].shape[1] // HEAD_DIM
-    for n, asker in enumerate(askers):
+    for n in range(askers):
+        counts = near_ref[n, rows : rows + blocks_here * tiles, 0:HEAD_DIM].astype(jnp.float32)
+        bias = jnp.where(counts > 0, jnp.log2(jnp.maximum(counts, 1.0)), -1e30)
+        wide = jnp.concatenate(
+            [
+                jnp.concatenate(
+                    [
+                        jnp.broadcast_to(bias[j * tiles + i : j * tiles + i + 1, :], (BLOCK, HEAD_DIM))
+                        for i in tuple(range(askers)) + FAR
+                    ],
+                    1,
+                )
+                for j in range(blocks_here)
+            ],
+            0,
+        )
         for h in range(heads):
             cols = slice(h * HEAD_DIM, (h + 1) * HEAD_DIM)
-            shifted = scores_of(asker, holders, tuple(range(len(askers))) + flips, cols, rows, tiles)
-            peak = jnp.max(shifted, axis=1, keepdims=True)
-            weights = jnp.exp2(shifted - peak)
-            full = (rows, HEAD_DIM)
-            out_ref[0, n * heads + h] = weigh(weights, holders, cols, rows)
-            out_ref[1, n * heads + h] = jnp.broadcast_to(peak, full)
-            out_ref[2, n * heads + h] = jnp.broadcast_to(jnp.sum(weights, axis=1, keepdims=True), full)
-
-
-def far_kernel(me_ref, *refs, rows, tiles, flips, copies):
-    *askers, before, out_ref = refs
-    askers, holders = askers[: -len(flips)], askers[-len(flips) :]
-    heads = askers[0].shape[1] // HEAD_DIM
-    spot = lax.rem(me_ref[0], len(askers))
-    for n, asker in enumerate(askers):
-        for h in range(heads):
-            cols = slice(h * HEAD_DIM, (h + 1) * HEAD_DIM)
-            shifted = scores_of(asker, holders, flips, cols, rows, tiles)
-            old = before[1, n * heads + h]
-            peak = jnp.maximum(old, jnp.max(shifted, axis=1, keepdims=True))
-            weights = jnp.exp2(shifted - jnp.concatenate([peak] * len(flips), 1))
-            keep = jnp.exp2(old - peak)
-            total = keep * before[2, n * heads + h] + jnp.sum(weights, axis=1, keepdims=True)
-            weighted = keep * before[0, n * heads + h] + weigh(weights, holders, cols, rows)
-            result = (weighted / total).astype(jnp.bfloat16)
+            keys = [ref[ref.shape[0] - 2 * rows : ref.shape[0] - rows, cols] for ref in pieces]
+            scores = lax.dot_general(
+                near_ref[n, 0:rows, cols],
+                jnp.concatenate(keys, 0),
+                (((1,), (1,)), ((), ())),
+                preferred_element_type=jnp.float32,
+            )
+            shifted = scores * scale + wide
+            weights = jnp.exp2(shifted - jnp.max(shifted, axis=1, keepdims=True))
+            weights_ref[n * heads + h] = weights.astype(jnp.bfloat16)
+
+
+def sum_kernel(weights_ref, near_ref, early_ref, *refs, copies):
+    *late_refs, out_ref = refs
+    pieces = pieces_of(near_ref, early_ref, late_refs)
+    count, rows, span = weights_ref.shape
+    heads = near_ref.shape[2] // HEAD_DIM
+    ones = jnp.ones((span, HEAD_DIM), jnp.bfloat16)
+    for h in range(heads):
+        cols = slice(h * HEAD_DIM, (h + 1) * HEAD_DIM)
+        values = jnp.concatenate([ref[ref.shape[0] - rows :, cols] for ref in pieces], 0)
+        both = jnp.concatenate([values, ones], 1)
+        for n in range(count // heads):
+            sums = jnp.dot(weights_ref[n * heads + h], both, preferred_element_type=jnp.float32)
+            result = (sums[:, :HEAD_DIM] / sums[:, HEAD_DIM:]).astype(jnp.bfloat16)
             for copy in range(copies):
-                out_ref[(spot ^ n) * copies + copy, :, cols] = result
+                out_ref[n * copies + copy, :, cols] = result
 
 
 def project_kernel(group_ref, *refs, flip):
@@ -279,45 +288,70 @@
     mask_rows = rows // BLOCK * tiles
     smem = pl.BlockSpec(memory_space=pltpu.SMEM)
     vmem = pl.BlockSpec(memory_space=pltpu.VMEM)
-    room = pltpu.CompilerParams(vmem_limit_bytes=32 << 20)
-    tall = lambda high: jax.ShapeDtypeStruct((high, local_width), jnp.bfloat16)
-    shapes = [tall(2 * rows)] * len(FAR) + [tall(3 * rows + mask_rows)] * (len(NEAR) + 1)
-    *sent, own = pl.pallas_call(
-        functools.partial(pack_kernel, ctx=ctx),
-        in_specs=[smem] * 4 + [vmem] * 3,
-        out_specs=[vmem] * len(shapes),
-        out_shape=shapes,
-        name="pack",
+    anywhere = pl.BlockSpec(memory_space=pl.ANY)
+    all_room = pltpu.CompilerParams(vmem_limit_bytes=60 << 20)
+    room = pltpu.CompilerParams(vmem_limit_bytes=8 << 20)
+    high = 3 * rows + mask_rows
+    def far_piece(flip):
+        seq = (me[0] ^ flip) % seqs
+        take = lambda block: lax.dynamic_slice_in_dim(block, seq, 1, 0)[0]
+        return jnp.concatenate([take(keys), take(values)], 0)
+
+    sent = [far_piece(flip) for flip in FAR]
+    packed = pl.pallas_call(
+        functools.partial(pack_near_kernel, ctx=ctx),
+        in_specs=[smem] + [anywhere] * 6,
+        out_specs=vmem,
+        out_shape=jax.ShapeDtypeStruct((seqs, high, local_width), jnp.bfloat16),
+        scratch_shapes=[
+            pltpu.SMEM((GLOB, seqs), jnp.int32),
+            pltpu.SMEM((seqs, rows // BLOCK, RMAX), jnp.int32),
+            pltpu.SMEM((rows // BLOCK, seqs), jnp.int32),
+            pltpu.SemaphoreType.DMA((3,)),
+            pltpu.SemaphoreType.DMA((3 * seqs,)),
+        ],
+        compiler_params=all_room,
+        name="pack_near",
     )(me, global_ids.T, rand_ids, rand_count.T, queries, keys, values)
-    sent = dict(zip(FAR + NEAR, sent))
     got = {
-        flip: lax.ppermute(sent[flip], "ctx", [(i, i ^ flip) for i in range(ctx)])
-        for flip in (1, 4, 6, 2, 5, 3, 7)
+        flip: lax.ppermute(part, "ctx", [(i, i ^ flip) for i in range(ctx)])
+        for flip, part in zip(FAR, sent)
     }
-    near = [own] + [got[flip] for flip in NEAR]
-    pairs = heads * (seqs * rows) ** 2
+    halves = [[half * seqs + c for c in range(seqs)] for half in range(ctx // seqs)]
+    near = lax.all_to_all(packed, "ctx", split_axis=0, concat_axis=0, tiled=True, axis_index_groups=halves)
+    early = pl.pallas_call(
+        stack_kernel,
+        in_specs=[vmem] * len(EARLY),
+        out_specs=vmem,
+        out_shape=jax.ShapeDtypeStruct((len(EARLY), 2 * rows, local_width), jnp.bfloat16),
+        compiler_params=room,
+        cost_estimate=pl.CostEstimate(flops=11 * 10**9, bytes_accessed=0, transcendentals=0),
+        name="stack",
+    )(*[got[flip] for flip in EARLY])
+    late = [got[flip] for flip in LATE]
+    pairs = heads * seqs * rows * ctx * rows
     cost = pl.CostEstimate(
-        flops=4 * pairs * HEAD_DIM, bytes_accessed=8 * seqs * rows * local_width, transcendentals=pairs
-    )
-    so_far = pl.pallas_call(
-        functools.partial(near_kernel, rows=rows, tiles=tiles, flips=EARLY),
-        in_specs=[vmem] * (len(near) + len(EARLY)),
+        flops=2 * pairs * HEAD_DIM, bytes_accessed=2 * pairs, transcendentals=pairs
+    )
+    weights = pl.pallas_call(
+        functools.partial(weigh_kernel, rows=rows, tiles=tiles),
+        in_specs=[vmem] * (2 + len(late)),
         out_specs=vmem,
-        out_shape=jax.ShapeDtypeStruct((3, seqs * heads, rows, HEAD_DIM), jnp.float32),
+        out_shape=jax.ShapeDtypeStruct((seqs * heads, rows, ctx * rows), jnp.bfloat16),
         compiler_params=room,
         cost_estimate=cost,
-        name="attend_near",
-    )(*near, *[got[flip] for flip in EARLY])
+        name="weigh",
+    )(near, early, *late)
     sides = 2
     attention = pl.pallas_call(
-        functools.partial(far_kernel, rows=rows, tiles=tiles, flips=LATE, copies=sides),
-        in_specs=[smem] + [vmem] * (len(near) + len(LATE) + 1),
+        functools.partial(sum_kernel, copies=sides),
+        in_specs=[vmem] * (3 + len(late)),
         out_specs=vmem,
         out_shape=jax.ShapeDtypeStruct((seqs * sides, rows, local_width), jnp.bfloat16),
         compiler_params=room,
         cost_estimate=cost,
-        name="attend_far",
-    )(me, *near, *[got[flip] for flip in LATE], so_far)
+        name="sum",
+    )(weights, near, early, *late)
     cores = groups // sides
     home = lax.all_to_all(
         attention,

time: 48.5 us -> 47.3 us (0.975)
  waiting for transfers between devices: 16.4 us -> 14.5 us
  starting transfers between devices: 12.6 us -> 14.4 us
  Pallas kernels: 7.49 us -> 5.78 us
    all_to_all x0 -> x1, starting transfers between devices: none -> 3.51 us  [half_path(): lax.all_to_all(packed, 'ctx', split_axis=0, concat_axis=0, tiled=True, ax...]
    ppermute x7 -> x4, waiting for transfers between devices: 14.9 us -> 13.1 us  [half_path(): lax.ppermute(part, 'ctx', [(i, i ^ flip) for i in range(ctx)])]
    ppermute x7 -> x4, starting transfers between devices: 12.6 us -> 10.9 us  [half_path(): lax.ppermute(part, 'ctx', [(i, i ^ flip) for i in range(ctx)])]
    pallas_call x3 -> x4, Pallas kernels: 5.78 us -> 4.09 us  [the longest x1 2.17 us: half_path(): pl.pallas_call(functools.partial(pack_near_kernel, ctx=ctx), in_specs=[sm...]
    squeeze x0 -> x1, local copies, waits for them, and re-layouts: none -> 1.1 us  [far_piece(): take = lambda block: lax.dynamic_slice_in_dim(block, seq, 1, 0)[0]]
    unnamed x6 -> x2, local copies, waits for them, and re-layouts: 0.94 us -> 0.01 us
  transfers between devices with their start and end apart: 8 -> 6, of which waited for: 4 -> 3; matrix products, arithmetic and copies ran while one was open for 0% -> 0% of each run, Pallas kernels for 6% -> 6%
where the time goes in v3:
time: 47.3 us; the launch traced here: 46.9 us
  waiting for transfers between devices  14.5 us (31%)
  starting transfers between devices  14.4 us (30%)
  blocking collectives  11 us (23%)
  Pallas kernels  5.78 us (12%)
  local copies, waits for them, and re-layouts  1.1 us (2%)
    ppermute x4, waiting for transfers between devices, half_path(): lax.ppermute(part, 'ctx', [(i, i ^ flip) for i in range(ctx)])  13.1 us
    all_to_all x1, blocking collectives, half_path(): lax.all_to_all(attention, ('ctx', 'head'), split_axis=0, concat_axis=0, t...  11 us
    ppermute x4, starting transfers between devices, half_path(): lax.ppermute(part, 'ctx', [(i, i ^ flip) for i in range(ctx)])  10.9 us
    all_to_all x1, starting transfers between devices, half_path(): lax.all_to_all(packed, 'ctx', split_axis=0, concat_axis=0, tiled=True, ax...  3.51 us
    pallas_call x1, Pallas kernels, half_path(): pl.pallas_call(functools.partial(pack_near_kernel, ctx=ctx), in_specs=[sm...  2.17 us
    pallas_call x2, Pallas kernels, project(): pl.pallas_call(functools.partial(project_kernel, flip=flip), in_specs=[sm...  1.69 us
    ppermute x1, waiting for transfers between devices, half_path(): beside = lax.ppermute(home, 'head', [(i, i ^ 1) for i in range(groups)])  1.45 us
    pallas_call x1, Pallas kernels, half_path(): pl.pallas_call(functools.partial(weigh_kernel, rows=rows, tiles=tiles), i...  1.17 us
  transfers between devices with their start and end apart: 6, of which 3 were waited for; matrix products, arithmetic and copies ran while one was open for 0% of the time, Pallas kernels for 6%

profile of v3, /device:TPU:0, one launch (start us, length us, event | category | flops | bytes accessed | tf_op | source)
XLA Modules:
  0.0 46.9 jit_solution(10297616082530434060)
XLA Ops:
  0.0 1.1 %dynamic-slice_bitcast_fusion = (bf16[128,256]{1,0:T(8,128)(2,1)S(1)}, bf16[128,256]{1,0:T(8,128)(2,1)S(1)}, bf16[128,256]{1,0:T(8,128)(2,1)S(1)}, bf16[128,256]...) fusion(bf16[4,128,256]{2,1,0:T(8,128)(2,1)} %v_ref.1, ...), kind=kLoop, calls=%fused_computation.4 | loop fusion | bytes 1048592 | tf_op jit(solution)/shard_map/squeeze | solution.py:297
  1.1 4.1 %collective-permute-start = (bf16[256,256]{1,0:T(8,128)(2,1)S(1)}, bf16[256,256]{1,0:T(8,128)(2,1)S(1)}, u32[]{:S(2)}, u32[]{:S(2)}) collective-permute-start(bf16[256,256]{1,0:T(8,128)(2,1)S(1)} %pad_maximum_fusion), channel_id=1, source_target_pairs={{0,16},{4,20},{8,24},{12,28},{16,0},{20,4},{24,8},{28,12},{1,17},{... | collective-permute-start | bytes 393224 | tf_op jit(solution)/shard_map/ppermute | solution.py:317
  5.2 1.4 %collective-permute-start.1 = (bf16[256,256]{1,0:T(8,128)(2,1)S(1)}, bf16[256,256]{1,0:T(8,128)(2,1)S(1)}, u32[]{:S(2)}, u32[]{:S(2)}) collective-permute-start(bf16[256,256]{1,0:T(8,128)(2,1)S(1)} %pad_maximum_fusion.1), channel_id=1, source_target_pairs={{0,24},{4,28},{8,16},{12,20},{16,8},{20,12},{24,0},{28,4},{1,25},{... | collective-permute-start | bytes 393224 | tf_op jit(solution)/shard_map/ppermute | solution.py:317
  6.6 2.2 %pack_near.1 = bf16[4,400,256]{2,1,0:T(8,128)(2,1)} custom-call(s32[1]{0:T(128)} %bitcast.1.me_ref, s32[2,4]{1,0:T(2,128)} %bitcast.20, s32[4,2,4]{2,1,0:T(2,128)} %rand_hbm.1, s32[2,4]{1,0:T(2,128)} %bitcast.21, bf16[4,128,256]{2,1,0:T(8,128)(2,1)} %q_ref.1, bf16[4,128,256]{2,1,0:T(8,128)(2,1)} %k_ref.1, bf16[4,128,256]{2,1,0:T(8,128)(2,1)} %v_ref.1), custom_call_target="tpu_custom_call" | custom-call | tf_op jit(solution)/shard_map/pack_near/pallas_call | solution.py:301
  8.8 3.5 %all-to-all-start = ((bf16[4,400,256]{2,1,0:T(8,128)(2,1)}), bf16[4,400,256]{2,1,0:T(8,128)(2,1)S(1)}, u32[]{:S(2)}, u32[]{:S(2)}) async-start(bf16[4,400,256]{2,1,0:T(8,128)(2,1)} %pack_near.1), calls=%async_computation | async-start | bytes 1638400 | tf_op jit(solution)/shard_map/all_to_all | solution.py:321
  12.4 3.3 %collective-permute-start.2 = (bf16[256,256]{1,0:T(8,128)(2,1)S(1)}, bf16[256,256]{1,0:T(8,128)(2,1)S(1)}, u32[]{:S(2)}, u32[]{:S(2)}) collective-permute-start(bf16[256,256]{1,0:T(8,128)(2,1)S(1)} %pad_maximum_fusion.2), channel_id=1, source_target_pairs={{0,20},{4,16},{8,28},{12,24},{16,4},{20,0},{24,12},{28,8},{1,21},{... | collective-permute-start | bytes 393224 | tf_op jit(solution)/shard_map/ppermute | solution.py:317
  15.6 2.1 %collective-permute-start.3 = (bf16[256,256]{1,0:T(8,128)(2,1)S(1)}, bf16[256,256]{1,0:T(8,128)(2,1)S(1)}, u32[]{:S(2)}, u32[]{:S(2)}) collective-permute-start(bf16[256,256]{1,0:T(8,128)(2,1)S(1)} %pad_maximum_fusion.3), channel_id=1, source_target_pairs={{0,28},{4,24},{8,20},{12,16},{16,12},{20,8},{24,4},{28,0},{1,29},{... | collective-permute-start | bytes 393224 | tf_op jit(solution)/shard_map/ppermute | solution.py:317
  17.7 0.0 collective-permute-done.refs_0_
  17.7 0.0 collective-permute-done.1.refs_1_
  17.8 7.5 %collective-permute-done.2.refs_0_ = bf16[256,256]{1,0:T(8,128)(2,1)S(1)} collective-permute-done((bf16[256,256]{1,0:T(8,128)(2,1)S(1)}, bf16[256,256]{1,0:T(8,128)(2,1)S(1)}, u32[]{:S(2)}, u32[]{:S(2)}) %collective-permute-start.2) | collective-permute-done | bytes 131104 | tf_op jit(solution)/shard_map/ppermute | solution.py:317
  25.3 5.6 %collective-permute-done.3.refs_1_ = bf16[256,256]{1,0:T(8,128)(2,1)S(1)} collective-permute-done((bf16[256,256]{1,0:T(8,128)(2,1)S(1)}, bf16[256,256]{1,0:T(8,128)(2,1)S(1)}, u32[]{:S(2)}, u32[]{:S(2)}) %collective-permute-start.3) | collective-permute-done | bytes 131104 | tf_op jit(solution)/shard_map/ppermute | solution.py:317
  30.8 0.0 all-to-all-done.near_ref
  30.9 1.2 %weigh.1.weights_ref = bf16[8,128,1024]{2,1,0:T(8,128)(2,1)S(1)} custom-call(bf16[4,400,256]{2,1,0:T(8,128)(2,1)S(1)} %all-to-all-done.near_ref, bf16[2,256,256]{2,1,0:T(8,128)(2,1)S(1)} %stack.1.early_ref, bf16[256,256]{1,0:T(8,128)(2,1)S(1)} %collective-permute-done.2.refs_0_, bf16[256,256]{1,0:T(8,128)(2,1)S(1)} %collective-permute-done.3.refs_1_), custom_call_target="tpu_custom_call" | custom-call | flops 268435456 | bytes 2097152 | tf_op jit(solution)/shard_map/weigh/pallas_call | solution.py:336
  32.0 0.0 copy-start
  32.0 0.7 %sum.1 = bf16[8,128,256]{2,1,0:T(8,128)(2,1)S(1)} custom-call(bf16[8,128,1024]{2,1,0:T(8,128)(2,1)S(1)} %weigh.1.weights_ref, bf16[4,400,256]{2,1,0:T(8,128)(2,1)S(1)} %all-to-all-done.near_ref, bf16[2,256,256]{2,1,0:T(8,128)(2,1)S(1)} %stack.1.early_ref, bf16[256,256]{1,0:T(8,128)(2,1)S(1)} %collective-permute-done.2.refs_0_, ...), custom_call_target="tpu_custom_call" | custom-call | flops 268435456 | bytes 2097152 | tf_op jit(solution)/shard_map/sum/pallas_call | solution.py:346
  32.8 11.0 %all_to_all.10.refs_0_ = bf16[8,128,256]{2,1,0:T(8,128)(2,1)S(1)} all-to-all(bf16[8,128,256]{2,1,0:T(8,128)(2,1)S(1)} %sum.1), channel_id=1, replica_groups={{0,2,4,6,8,10,12,14},{1,3,5,7,9,11,13,15},{16,18,20,22,24,26,28,30},{17..., dimensions={0} | all-to-all | bytes 1048576 | tf_op jit(solution)/shard_map/all_to_all | solution.py:356
  43.8 0.0 collective-permute-start.4
  43.8 0.0 copy-done
  43.8 0.4 project.2.refs_0_
  44.2 1.5 %collective-permute-done.4.refs_1_ = bf16[8,128,256]{2,1,0:T(8,128)(2,1)S(1)} collective-permute-done((bf16[8,128,256]{2,1,0:T(8,128)(2,1)S(1)}, bf16[8,128,256]{2,1,0:T(8,128)(2,1)S(1)}, u32[]{:S(2)}, u32[]{:S(2)}) %collective-permute-start.4) | collective-permute-done | bytes 524320 | tf_op jit(solution)/shard_map/ppermute | solution.py:368
  45.7 1.2 %project.3 = bf16[4,128,512]{2,1,0:T(8,128)(2,1)} custom-call(s32[1]{0:T(128)} %bitcast.group_ref, f32[4,128,512]{2,1,0:T(8,128)S(1)} %project.2.refs_0_, bf16[8,128,256]{2,1,0:T(8,128)(2,1)S(1)} %collective-permute-done.4.refs_1_, bf16[1024,512]{1,0:T(8,128)(2,1)S(1)} %copy-done), custom_call_target="tpu_custom_call" | custom-call | flops 268435456 | bytes 1048576 | tf_op jit(solution)/shard_map/project/pallas_call | solution.py:372
  (5 shorter events, 0.1 us)
Async XLA Ops:
  1.1 16.6 %collective-permute-start = (bf16[256,256]{1,0:T(8,128)(2,1)S(1)}, bf16[256,256]{1,0:T(8,128)(2,1)S(1)}, u32[]{:S(2)}, u32[]{:S(2)}) collective-permute-start(bf16[256,256]{1,0:T(8,128)(2,1)S(1)} %pad_maximum_fusion), channel_id=1, source_target_pairs={{0,16},{4,20},{8,24},{12,28},{16,0},{20,4},{24,8},{28,12},{1,17},{... | collective-permute-start | bytes 393224 | tf_op jit(solution)/shard_map/ppermute | solution.py:317
  5.2 12.5 %collective-permute-start.1 = (bf16[256,256]{1,0:T(8,128)(2,1)S(1)}, bf16[256,256]{1,0:T(8,128)(2,1)S(1)}, u32[]{:S(2)}, u32[]{:S(2)}) collective-permute-start(bf16[256,256]{1,0:T(8,128)(2,1)S(1)} %pad_maximum_fusion.1), channel_id=1, source_target_pairs={{0,24},{4,28},{8,16},{12,20},{16,8},{20,12},{24,0},{28,4},{1,25},{... | collective-permute-start | bytes 393224 | tf_op jit(solution)/shard_map/ppermute | solution.py:317
  8.8 22.0 %all-to-all-start = ((bf16[4,400,256]{2,1,0:T(8,128)(2,1)}), bf16[4,400,256]{2,1,0:T(8,128)(2,1)S(1)}, u32[]{:S(2)}, u32[]{:S(2)}) async-start(bf16[4,400,256]{2,1,0:T(8,128)(2,1)} %pack_near.1), calls=%async_computation | async-start | bytes 1638400 | tf_op jit(solution)/shard_map/all_to_all | solution.py:321
  12.4 12.9 %collective-permute-start.2 = (bf16[256,256]{1,0:T(8,128)(2,1)S(1)}, bf16[256,256]{1,0:T(8,128)(2,1)S(1)}, u32[]{:S(2)}, u32[]{:S(2)}) collective-permute-start(bf16[256,256]{1,0:T(8,128)(2,1)S(1)} %pad_maximum_fusion.2), channel_id=1, source_target_pairs={{0,20},{4,16},{8,28},{12,24},{16,4},{20,0},{24,12},{28,8},{1,21},{... | collective-permute-start | bytes 393224 | tf_op jit(solution)/shard_map/ppermute | solution.py:317
  15.6 15.2 %collective-permute-start.3 = (bf16[256,256]{1,0:T(8,128)(2,1)S(1)}, bf16[256,256]{1,0:T(8,128)(2,1)S(1)}, u32[]{:S(2)}, u32[]{:S(2)}) collective-permute-start(bf16[256,256]{1,0:T(8,128)(2,1)S(1)} %pad_maximum_fusion.3), channel_id=1, source_target_pairs={{0,28},{4,24},{8,20},{12,16},{16,12},{20,8},{24,4},{28,0},{1,29},{... | collective-permute-start | bytes 393224 | tf_op jit(solution)/shard_map/ppermute | solution.py:317
  32.0 11.8 %copy-start = (bf16[1024,512]{1,0:T(8,128)(2,1)S(1)}, bf16[1024,512]{1,0:T(8,128)(2,1)}, u32[]{:S(2)}) copy-start(bf16[1024,512]{1,0:T(8,128)(2,1)} %refs_2_.1) | copy-start | bytes 3145732
  43.8 1.9 %collective-permute-start.4 = (bf16[8,128,256]{2,1,0:T(8,128)(2,1)S(1)}, bf16[8,128,256]{2,1,0:T(8,128)(2,1)S(1)}, u32[]{:S(2)}, u32[]{:S(2)}) collective-permute-start(bf16[8,128,256]{2,1,0:T(8,128)(2,1)S(1)} %all_to_all.10.refs_0_), channel_id=1, source_target_pairs={{0,1},{1,0},{2,3},{3,2},{4,5},{5,4},{6,7},{7,6},{8,9},{9,8},{10,11... | collective-permute-start | bytes 1572872 | tf_op jit(solution)/shard_map/ppermute | solution.py:368

commit v4 on v3

--- a/solution.py
+++ b/solution.py
@@ -140,42 +140,24 @@
 
 
 NEAR = (1, 2, 3)
-FAR = (4, 6, 5, 7)
-EARLY, LATE = FAR[:2], FAR[2:]
-
-
-def pack_near_kernel(me_ref, glob_hbm, rand_hbm, count_hbm, q_ref, k_ref, v_ref, *refs, ctx):
-    near_ref, glob_ref, rand_ref, count_ref, id_sems, sems = refs
-    seqs, rows, width = q_ref.shape
+FAR = (6, 5, 4, 7)
+EARLY, LATE = FAR, ()
+
+
+def count_kernel(me_ref, glob_ref, rand_ref, count_ref, *outs, ctx):
+    seqs = rand_ref.shape[0]
+    blocks_here = rand_ref.shape[1]
+    mask_rows = outs[0].shape[0]
+    tiles = mask_rows // blocks_here
+    blocks = ctx * blocks_here
     me = me_ref[0]
     base = me - lax.rem(me, seqs)
-    blocks_here = rows // BLOCK
-    blocks = ctx * blocks_here
-    tiles = ctx * rows // HEAD_DIM
-    mask_rows = blocks_here * tiles
-    ids = [
-        pltpu.make_async_copy(src, dst, id_sems.at[i])
-        for i, (src, dst) in enumerate(
-            ((glob_hbm, glob_ref), (rand_hbm, rand_ref), (count_hbm, count_ref))
-        )
-    ]
-    copies = [
-        pltpu.make_async_copy(
-            source.at[seq], near_ref.at[seq, pl.ds(start, rows), :], sems.at[3 * seq + i]
-        )
-        for seq in range(seqs)
-        for i, (source, start) in enumerate(
-            ((q_ref, 0), (k_ref, rows + mask_rows), (v_ref, 2 * rows + mask_rows))
-        )
-    ]
-    for copy in ids + copies:
-        copy.start()
-    for copy in ids:
-        copy.wait()
     tile = lax.broadcasted_iota(jnp.int32, (tiles, HEAD_DIM), 0)
     lane = lax.broadcasted_iota(jnp.int32, (tiles, HEAD_DIM), 1)
-    for seq in range(seqs):
-        holder = jnp.where(tile < seqs, base + tile, (base + seq) ^ tile)
+    for flip, out in enumerate(outs):
+        asker = me ^ flip
+        seq = lax.rem(asker, seqs)
+        holder = jnp.where(tile < seqs, base + tile, asker ^ tile)
         key_block = (holder * HEAD_DIM + lane) // BLOCK
         counts = []
         for j in range(blocks_here):
@@ -186,11 +168,7 @@
                 jnp.where(r < count_ref[j, seq], rand_ref[seq, j, r], -1) for r in range(RMAX)
             ]
             counts.append(sum((key_block == one).astype(jnp.float32) for one in listed))
-        counts = jnp.concatenate(counts, 0).astype(jnp.bfloat16)
-        for h in range(width // HEAD_DIM):
-            near_ref[seq, rows : rows + mask_rows, h * HEAD_DIM : (h + 1) * HEAD_DIM] = counts
-    for copy in copies:
-        copy.wait()
+        out[...] = jnp.concatenate(counts, 0).astype(jnp.bfloat16)
 
 
 def stack_kernel(*refs):
@@ -204,15 +182,17 @@
     return pieces + [early_ref.at[n] for n in range(early_ref.shape[0])] + list(late_refs)
 
 
-def weigh_kernel(near_ref, early_ref, *refs, rows, tiles):
-    *late_refs, weights_ref = refs
+def weigh_kernel(me_ref, near_ref, early_ref, *refs, rows, tiles, late):
+    *refs, weights_ref = refs
+    late_refs, counts_refs = refs[:late], refs[late:]
     pieces = pieces_of(near_ref, early_ref, late_refs)
     askers, _, width = near_ref.shape
+    spot = lax.rem(me_ref[0], askers)
     blocks_here = rows // BLOCK
     heads = width // HEAD_DIM
     scale = HEAD_DIM ** (-0.5) * 1.4426950408889634
     for n in range(askers):
-        counts = near_ref[n, rows : rows + blocks_here * tiles, 0:HEAD_DIM].astype(jnp.float32)
+        counts = counts_refs[n][...].astype(jnp.float32)
         bias = jnp.where(counts > 0, jnp.log2(jnp.maximum(counts, 1.0)), -1e30)
         wide = jnp.concatenate(
             [
@@ -231,7 +211,7 @@
             cols = slice(h * HEAD_DIM, (h + 1) * HEAD_DIM)
             keys = [ref[ref.shape[0] - 2 * rows : ref.shape[0] - rows, cols] for ref in pieces]
             scores = lax.dot_general(
-                near_ref[n, 0:rows, cols],
+                near_ref[spot ^ n, 0:rows, cols],
                 jnp.concatenate(keys, 0),
                 (((1,), (1,)), ((), ())),
                 preferred_element_type=jnp.float32,
@@ -241,10 +221,11 @@
             weights_ref[n * heads + h] = weights.astype(jnp.bfloat16)
 
 
-def sum_kernel(weights_ref, near_ref, early_ref, *refs, copies):
+def sum_kernel(me_ref, weights_ref, near_ref, early_ref, *refs, copies):
     *late_refs, out_ref = refs
     pieces = pieces_of(near_ref, early_ref, late_refs)
     count, rows, span = weights_ref.shape
+    spot = lax.rem(me_ref[0], near_ref.shape[0])
     heads = near_ref.shape[2] // HEAD_DIM
     ones = jnp.ones((span, HEAD_DIM), jnp.bfloat16)
     for h in range(heads):
@@ -255,7 +236,7 @@
             sums = jnp.dot(weights_ref[n * heads + h], both, preferred_element_type=jnp.float32)
             result = (sums[:, :HEAD_DIM] / sums[:, HEAD_DIM:]).astype(jnp.bfloat16)
             for copy in range(copies):
-                out_ref[n * copies + copy, :, cols] = result
+                out_ref[(spot ^ n) * copies + copy, :, cols] = result
 
 
 def project_kernel(group_ref, *refs, flip):
@@ -263,9 +244,10 @@
     slots, rows, depth = part_ref.shape
     seqs = out_ref.shape[0]
     sides = slots // seqs
-    core = lax.rem(group_ref[0], weight_ref.shape[0] // (depth * sides)) ^ flip
+    cores = weight_ref.shape[0] // (depth * sides)
+    core = lax.rem(group_ref[0], cores) ^ flip
     weights = [
-        weight_ref[pl.ds(pl.multiple_of((side * sides + core) * depth, depth), depth), :]
+        weight_ref[pl.ds(pl.multiple_of((side * cores + core) * depth, depth), depth), :]
         for side in range(sides)
     ]
     for seq in range(seqs):
@@ -275,6 +257,30 @@
                 part_ref[seq * sides + side], weights[side], preferred_element_type=jnp.float32
             )
         out_ref[seq] = total.astype(out_ref.dtype)
+
+
+def finish_kernel(group_ref, before_ref, part_ref, weight_ref, *refs, flip, first):
+    *_, out_ref, buffer, sems = refs
+    slots, rows, depth = part_ref.shape
+    sides = slots // buffer.shape[0]
+    cores = weight_ref.shape[0] // (depth * sides)
+    core = lax.rem(group_ref[0], cores) ^ flip
+    weights = [
+        weight_ref[pl.ds(pl.multiple_of((side * cores + core) * depth, depth), depth), :]
+        for side in range(sides)
+    ]
+    copies = []
+    for n in range(buffer.shape[0]):
+        total = before_ref[first + n]
+        for side in range(sides):
+            total = total + jnp.dot(
+                part_ref[n * sides + side], weights[side], preferred_element_type=jnp.float32
+            )
+        buffer[n] = total.astype(buffer.dtype)
+        copies.append(pltpu.make_async_copy(buffer.at[n], out_ref.at[first + n], sems.at[n]))
+        copies[-1].start()
+    for copy in copies:
+        copy.wait()
 
 
 def half_path(queries, keys, values, out_weight, global_ids, rand_ids, rand_count):
@@ -289,43 +295,38 @@
     smem = pl.BlockSpec(memory_space=pltpu.SMEM)
     vmem = pl.BlockSpec(memory_space=pltpu.VMEM)
     anywhere = pl.BlockSpec(memory_space=pl.ANY)
-    all_room = pltpu.CompilerParams(vmem_limit_bytes=60 << 20)
     room = pltpu.CompilerParams(vmem_limit_bytes=8 << 20)
-    high = 3 * rows + mask_rows
     def far_piece(flip):
         seq = (me[0] ^ flip) % seqs
         take = lambda block: lax.dynamic_slice_in_dim(block, seq, 1, 0)[0]
         return jnp.concatenate([take(keys), take(values)], 0)
 
     sent = [far_piece(flip) for flip in FAR]
-    packed = pl.pallas_call(
-        functools.partial(pack_near_kernel, ctx=ctx),
-        in_specs=[smem] + [anywhere] * 6,
-        out_specs=vmem,
-        out_shape=jax.ShapeDtypeStruct((seqs, high, local_width), jnp.bfloat16),
-        scratch_shapes=[
-            pltpu.SMEM((GLOB, seqs), jnp.int32),
-            pltpu.SMEM((seqs, rows // BLOCK, RMAX), jnp.int32),
-            pltpu.SMEM((rows // BLOCK, seqs), jnp.int32),
-            pltpu.SemaphoreType.DMA((3,)),
-            pltpu.SemaphoreType.DMA((3 * seqs,)),
-        ],
-        compiler_params=all_room,
-        name="pack_near",
-    )(me, global_ids.T, rand_ids, rand_count.T, queries, keys, values)
+    own, *asked = pl.pallas_call(
+        functools.partial(count_kernel, ctx=ctx),
+        in_specs=[smem] * 4,
+        out_specs=[vmem] * seqs,
+        out_shape=[jax.ShapeDtypeStruct((mask_rows, HEAD_DIM), jnp.bfloat16)] * seqs,
+        compiler_params=room,
+        name="count",
+    )(me, global_ids.T, rand_ids, rand_count.T)
+    packed = jnp.concatenate([queries, keys, values], 1)
     got = {
         flip: lax.ppermute(part, "ctx", [(i, i ^ flip) for i in range(ctx)])
         for flip, part in zip(FAR, sent)
     }
     halves = [[half * seqs + c for c in range(seqs)] for half in range(ctx // seqs)]
     near = lax.all_to_all(packed, "ctx", split_axis=0, concat_axis=0, tiled=True, axis_index_groups=halves)
+    counts = [own] + [
+        lax.ppermute(part, "ctx", [(i, i ^ (n + 1)) for i in range(ctx)]) for n, part in enumerate(asked)
+    ]
     early = pl.pallas_call(
         stack_kernel,
         in_specs=[vmem] * len(EARLY),
         out_specs=vmem,
         out_shape=jax.ShapeDtypeStruct((len(EARLY), 2 * rows, local_width), jnp.bfloat16),
         compiler_params=room,
-        cost_estimate=pl.CostEstimate(flops=11 * 10**9, bytes_accessed=0, transcendentals=0),
+        cost_estimate=pl.CostEstimate(flops=9 * 10**9, bytes_accessed=0, transcendentals=0),
         name="stack",
     )(*[got[flip] for flip in EARLY])
     late = [got[flip] for flip in LATE]
@@ -334,24 +335,24 @@
         flops=2 * pairs * HEAD_DIM, bytes_accessed=2 * pairs, transcendentals=pairs
     )
     weights = pl.pallas_call(
-        functools.partial(weigh_kernel, rows=rows, tiles=tiles),
-        in_specs=[vmem] * (2 + len(late)),
+        functools.partial(weigh_kernel, rows=rows, tiles=tiles, late=len(late)),
+        in_specs=[smem] + [vmem] * (2 + len(late) + seqs),
         out_specs=vmem,
         out_shape=jax.ShapeDtypeStruct((seqs * heads, rows, ctx * rows), jnp.bfloat16),
         compiler_params=room,
         cost_estimate=cost,
         name="weigh",
-    )(near, early, *late)
+    )(me, near, early, *late, *counts)
     sides = 2
     attention = pl.pallas_call(
         functools.partial(sum_kernel, copies=sides),
-        in_specs=[vmem] * (3 + len(late)),
+        in_specs=[smem] + [vmem] * (3 + len(late)),
         out_specs=vmem,
         out_shape=jax.ShapeDtypeStruct((seqs * sides, rows, local_width), jnp.bfloat16),
         compiler_params=room,
         cost_estimate=cost,
         name="sum",
-    )(weights, near, early, *late)
+    )(me, weights, near, early, *late)
     cores = groups // sides
     home = lax.all_to_all(
         attention,
@@ -383,7 +384,18 @@
             name="project",
         )(group, *parts, out_weight)
 
-    return project(1, jnp.bfloat16, project(0, jnp.float32, home), beside)
+    return pl.pallas_call(
+        functools.partial(finish_kernel, flip=1, first=0),
+        in_specs=[smem] + [vmem] * 3,
+        out_specs=anywhere,
+        out_shape=jax.ShapeDtypeStruct((seqs, rows, width), jnp.bfloat16),
+        scratch_shapes=[
+            pltpu.VMEM((seqs, rows, width), jnp.bfloat16),
+            pltpu.SemaphoreType.DMA((seqs,)),
+        ],
+        compiler_params=room,
+        name="finish",
+    )(group, project(0, jnp.float32, home), beside, out_weight)
 
 
 def on_device(queries, keys, values, out_weight, global_ids, rand_ids, rand_count):

time: 47.3 us -> 47.3 us (level)
  waiting for transfers between devices: 14.5 us -> 10.2 us
  starting transfers between devices: 14.4 us -> 18 us
  Pallas kernels: 5.78 us -> 4.28 us
  blocking collectives: 11 us -> 12.3 us
  other arithmetic: 0.04 us -> 0.99 us
    ppermute x4, waiting for transfers between devices: 13.1 us -> 8.69 us  [half_path(): lax.ppermute(part, 'ctx', [(i, i ^ flip) for i in range(ctx)])]
    ppermute x0 -> x3, starting transfers between devices: none -> 3.55 us  [half_path(): lax.ppermute(part, 'ctx', [(i, i ^ n + 1) for i in range(ctx)])]
    all_to_all x1, blocking collectives: 11 us -> 12.3 us  [half_path(): lax.all_to_all(attention, ('ctx', 'head'), split_axis=0, concat_axis=0, t...]
    pallas_call x2 -> x1, Pallas kernels: 1.69 us -> 0.45 us  [project(): pl.pallas_call(functools.partial(project_kernel, flip=flip), in_specs=[sm...]
    concatenate x0 -> x1, other arithmetic: none -> 0.94 us  [half_path(): packed = jnp.concatenate([queries, keys, values], 1)]
    pallas_call x3 -> x4, Pallas kernels: 4.07 us -> 3.79 us  [the longest x1 1.18 us: half_path(): pl.pallas_call(functools.partial(weigh_kernel, rows=rows, tiles=tiles, la...]
  transfers between devices with their start and end apart: 6 -> 9, of which waited for: 3 -> 3; matrix products, arithmetic and copies ran while one was open for 0% -> 2% of each run, Pallas kernels for 6% -> 2%
where the time goes in v4:
time: 47.3 us; the launch traced here: 47.1 us
  starting transfers between devices  18 us (38%)
  blocking collectives  12.3 us (26%)
  waiting for transfers between devices  10.2 us (22%)
  Pallas kernels  4.28 us (9%)
  local copies, waits for them, and re-layouts  1.2 us (3%)
  other arithmetic  0.99 us (2%)
    all_to_all x1, blocking collectives, half_path(): lax.all_to_all(attention, ('ctx', 'head'), split_axis=0, concat_axis=0, t...  12.3 us
    ppermute x4, starting transfers between devices, half_path(): lax.ppermute(part, 'ctx', [(i, i ^ flip) for i in range(ctx)])  11 us
    ppermute x4, waiting for transfers between devices, half_path(): lax.ppermute(part, 'ctx', [(i, i ^ flip) for i in range(ctx)])  8.69 us
    ppermute x3, starting transfers between devices, half_path(): lax.ppermute(part, 'ctx', [(i, i ^ n + 1) for i in range(ctx)])  3.55 us
    all_to_all x1, starting transfers between devices, half_path(): lax.all_to_all(packed, 'ctx', split_axis=0, concat_axis=0, tiled=True, ax...  3.49 us
    ppermute x1, waiting for transfers between devices, half_path(): beside = lax.ppermute(home, 'head', [(i, i ^ 1) for i in range(groups)])  1.45 us
    pallas_call x1, Pallas kernels, half_path(): pl.pallas_call(functools.partial(weigh_kernel, rows=rows, tiles=tiles, la...  1.18 us
    squeeze x1, local copies, waits for them, and re-layouts, far_piece(): take = lambda block: lax.dynamic_slice_in_dim(block, seq, 1, 0)[0]  1.17 us
  transfers between devices with their start and end apart: 9, of which 3 were waited for; matrix products, arithmetic and copies ran while one was open for 2% of the time, Pallas kernels for 2%

profile of v4, /device:TPU:0, one launch (start us, length us, event | category | flops | bytes accessed | tf_op | source)
XLA Modules:
  0.0 47.1 jit_solution(11231787852694228907)
XLA Ops:
  0.0 0.0 copy-start.4
  0.0 0.0 copy-start.5
  0.0 0.0 copy-start.6
  0.0 1.2 %dynamic-slice_bitcast_fusion = (bf16[128,256]{1,0:T(8,128)(2,1)S(1)}, bf16[128,256]{1,0:T(8,128)(2,1)S(1)}, bf16[128,256]{1,0:T(8,128)(2,1)S(1)}, bf16[128,256]...) fusion(bf16[4,128,256]{2,1,0:T(8,128)(2,1)} %param.9, ...), kind=kLoop, calls=%fused_computation.5 | loop fusion | bytes 1048592 | tf_op jit(solution)/shard_map/squeeze | solution.py:301
  1.2 4.2 %collective-permute-start.2 = (bf16[256,256]{1,0:T(8,128)(2,1)S(1)}, bf16[256,256]{1,0:T(8,128)(2,1)S(1)}, u32[]{:S(2)}, u32[]{:S(2)}) collective-permute-start(bf16[256,256]{1,0:T(8,128)(2,1)S(1)} %pad_maximum_fusion.3), channel_id=1, source_target_pairs={{0,16},{4,20},{8,24},{12,28},{16,0},{20,4},{24,8},{28,12},{1,17},{... | collective-permute-start | bytes 393224 | tf_op jit(solution)/shard_map/ppermute | solution.py:315
  5.4 0.0 copy-start.1
  5.4 0.0 copy-start.2
  5.4 0.0 copy-start.3
  5.4 1.4 %collective-permute-start = (bf16[256,256]{1,0:T(8,128)(2,1)S(1)}, bf16[256,256]{1,0:T(8,128)(2,1)S(1)}, u32[]{:S(2)}, u32[]{:S(2)}) collective-permute-start(bf16[256,256]{1,0:T(8,128)(2,1)S(1)} %pad_maximum_fusion.1), channel_id=1, source_target_pairs={{0,24},{4,28},{8,16},{12,20},{16,8},{20,12},{24,0},{28,4},{1,25},{... | collective-permute-start | bytes 393224 | tf_op jit(solution)/shard_map/ppermute | solution.py:315
  6.8 0.0 copy-done.4
  6.8 0.0 copy-done.5
  6.8 0.0 copy-done.6
  6.8 0.9 %pad_maximum_fusion = bf16[4,384,256]{2,1,0:T(8,128)(2,1)} fusion(bf16[4,128,256]{2,1,0:T(8,128)(2,1)S(1)} %copy-done.4, bf16[4,128,256]{2,1,0:T(8,128)(2,1)S(1)} %copy-done.5, bf16[4,128,256]{2,1,0:T(8,128)(2,1)S(1)} %copy-done.6), kind=kLoop, calls=%fused_computation | loop fusion | flops 2359296 | bytes 1572864 | tf_op jit(solution)/shard_map/concatenate | solution.py:313
  7.8 3.5 %all-to-all-start = ((bf16[4,384,256]{2,1,0:T(8,128)(2,1)}), bf16[4,384,256]{2,1,0:T(8,128)(2,1)S(1)}, u32[]{:S(2)}, u32[]{:S(2)}) async-start(bf16[4,384,256]{2,1,0:T(8,128)(2,1)} %pad_maximum_fusion), calls=%async_computation | async-start | bytes 1572864 | tf_op jit(solution)/shard_map/all_to_all | solution.py:319
  11.3 3.3 %collective-permute-start.1 = (bf16[256,256]{1,0:T(8,128)(2,1)S(1)}, bf16[256,256]{1,0:T(8,128)(2,1)S(1)}, u32[]{:S(2)}, u32[]{:S(2)}) collective-permute-start(bf16[256,256]{1,0:T(8,128)(2,1)S(1)} %pad_maximum_fusion.2), channel_id=1, source_target_pairs={{0,20},{4,16},{8,28},{12,24},{16,4},{20,0},{24,12},{28,8},{1,21},{... | collective-permute-start | bytes 393224 | tf_op jit(solution)/shard_map/ppermute | solution.py:315
  14.6 2.1 %collective-permute-start.3 = (bf16[256,256]{1,0:T(8,128)(2,1)S(1)}, bf16[256,256]{1,0:T(8,128)(2,1)S(1)}, u32[]{:S(2)}, u32[]{:S(2)}) collective-permute-start(bf16[256,256]{1,0:T(8,128)(2,1)S(1)} %pad_maximum_fusion.4), channel_id=1, source_target_pairs={{0,28},{4,24},{8,20},{12,16},{16,12},{20,8},{24,4},{28,0},{1,29},{... | collective-permute-start | bytes 393224 | tf_op jit(solution)/shard_map/ppermute | solution.py:315
  16.7 0.0 copy-done.1
  16.7 0.0 copy-done.2
  16.7 0.0 copy-done.3
  16.7 0.7 %count.1 = (bf16[16,128]{1,0:T(8,128)(2,1)S(1)}, bf16[16,128]{1,0:T(8,128)(2,1)S(1)}, bf16[16,128]{1,0:T(8,128)(2,1)S(1)}, bf16[16,128]{1,0:T(8,128)(2,1)S(1)}) custom-call(s32[1]{0:T(128)} %bitcast.1.me_ref, s32[2,4]{1,0:T(2,128)S(1)} %bitcast.20, s32[4,2,4]{2,1,0:T(2,128)S(1)} %copy-done.1, s32[2,4]{1,0:T(2,128)S(1)} %bitcast.21), custom_call_target="tpu_custom_call" | custom-call | tf_op jit(solution)/shard_map/count/pallas_call | solution.py:305
  17.4 1.5 %collective-permute-start.4 = (bf16[16,128]{1,0:T(8,128)(2,1)S(1)}, bf16[16,128]{1,0:T(8,128)(2,1)S(1)}, u32[]{:S(2)}, u32[]{:S(2)}) collective-permute-start(bf16[16,128]{1,0:T(8,128)(2,1)S(1)} %get-tuple-element.10), channel_id=1, source_target_pairs={{0,4},{4,0},{8,12},{12,8},{16,20},{20,16},{24,28},{28,24},{1,5},{5... | collective-permute-start | bytes 12296 | tf_op jit(solution)/shard_map/ppermute | solution.py:321
  18.9 0.0 collective-permute-done.2.refs_2_
  18.9 0.0 collective-permute-start.5
  18.9 0.0 collective-permute-done.refs_0_
  19.0 2.0 %collective-permute-start.6 = (bf16[16,128]{1,0:T(8,128)(2,1)S(1)}, bf16[16,128]{1,0:T(8,128)(2,1)S(1)}, u32[]{:S(2)}, u32[]{:S(2)}) collective-permute-start(bf16[16,128]{1,0:T(8,128)(2,1)S(1)} %get-tuple-element.12), channel_id=1, source_target_pairs={{0,12},{4,8},{8,4},{12,0},{16,28},{20,24},{24,20},{28,16},{1,13},{... | collective-permute-start | bytes 12296 | tf_op jit(solution)/shard_map/ppermute | solution.py:321
  21.0 3.0 %collective-permute-done.1.refs_1_ = bf16[256,256]{1,0:T(8,128)(2,1)S(1)} collective-permute-done((bf16[256,256]{1,0:T(8,128)(2,1)S(1)}, bf16[256,256]{1,0:T(8,128)(2,1)S(1)}, u32[]{:S(2)}, u32[]{:S(2)}) %collective-permute-start.1) | collective-permute-done | bytes 131104 | tf_op jit(solution)/shard_map/ppermute | solution.py:315
  23.9 5.7 %collective-permute-done.3.refs_3_ = bf16[256,256]{1,0:T(8,128)(2,1)S(1)} collective-permute-done((bf16[256,256]{1,0:T(8,128)(2,1)S(1)}, bf16[256,256]{1,0:T(8,128)(2,1)S(1)}, u32[]{:S(2)}, u32[]{:S(2)}) %collective-permute-start.3) | collective-permute-done | bytes 131104 | tf_op jit(solution)/shard_map/ppermute | solution.py:315
  29.7 0.0 collective-permute-done.4.refs_1_
  29.7 0.0 collective-permute-done.5.refs_2_
  29.7 0.0 collective-permute-done.6.refs_3_
  29.7 0.0 all-to-all-done.near_ref
  29.7 1.2 %weigh.1.weights_ref = bf16[8,128,1024]{2,1,0:T(8,128)(2,1)S(1)} custom-call(s32[1]{0:T(128)} %bitcast.1.me_ref, bf16[4,384,256]{2,1,0:T(8,128)(2,1)S(1)} %all-to-all-done.near_ref, bf16[4,256,256]{2,1,0:T(8,128)(2,1)S(1)} %stack.1.early_ref, bf16[16,128]{1,0:T(8,128)(2,1)S(1)} %get-tuple-element.9.refs_0_, ...), custom_call_target="tpu_custom_call" | custom-call | flops 268435456 | bytes 2097152 | tf_op jit(solution)/shard_map/weigh/pallas_call | solution.py:337
  30.9 0.0 copy-start
  30.9 0.8 %sum.1 = bf16[8,128,256]{2,1,0:T(8,128)(2,1)S(1)} custom-call(s32[1]{0:T(128)} %bitcast.1.me_ref, bf16[8,128,1024]{2,1,0:T(8,128)(2,1)S(1)} %weigh.1.weights_ref, bf16[4,384,256]{2,1,0:T(8,128)(2,1)S(1)} %all-to-all-done.near_ref, bf16[4,256,256]{2,1,0:T(8,128)(2,1)S(1)} %stack.1.early_ref), custom_call_target="tpu_custom_call" | custom-call | flops 268435456 | bytes 2097152 | tf_op jit(solution)/shard_map/sum/pallas_call | solution.py:347
  31.7 12.3 %all_to_all.10.refs_0_ = bf16[8,128,256]{2,1,0:T(8,128)(2,1)S(1)} all-to-all(bf16[8,128,256]{2,1,0:T(8,128)(2,1)S(1)} %sum.1), channel_id=1, replica_groups={{0,2,4,6,8,10,12,14},{1,3,5,7,9,11,13,15},{16,18,20,22,24,26,28,30},{17..., dimensions={0} | all-to-all | bytes 1048576 | tf_op jit(solution)/shard_map/all_to_all | solution.py:357
  44.0 0.0 collective-permute-start.7
  44.0 0.0 copy-done
  44.0 0.4 project.1.before_ref
  44.5 1.4 %collective-permute-done.7.part_ref = bf16[8,128,256]{2,1,0:T(8,128)(2,1)S(1)} collective-permute-done((bf16[8,128,256]{2,1,0:T(8,128)(2,1)S(1)}, bf16[8,128,256]{2,1,0:T(8,128)(2,1)S(1)}, u32[]{:S(2)}, u32[]{:S(2)}) %collective-permute-start.7) | collective-permute-done | bytes 524320 | tf_op jit(solution)/shard_map/ppermute | solution.py:369
  45.9 1.2 %finish.1 = bf16[4,128,512]{2,1,0:T(8,128)(2,1)} custom-call(s32[1]{0:T(128)} %bitcast.group_ref, f32[4,128,512]{2,1,0:T(8,128)S(1)} %project.1.before_ref, bf16[8,128,256]{2,1,0:T(8,128)(2,1)S(1)} %collective-permute-done.7.part_ref, bf16[1024,512]{1,0:T(8,128)(2,1)S(1)} %copy-done), custom_call_target="tpu_custom_call" | custom-call | tf_op jit(solution)/shard_map/finish/pallas_call | solution.py:387
  (5 shorter events, 0.1 us)
Async XLA Ops:
  0.0 6.8 %copy-start.4 = (bf16[4,128,256]{2,1,0:T(8,128)(2,1)S(1)}, bf16[4,128,256]{2,1,0:T(8,128)(2,1)}, u32[]{:S(2)}) copy-start(bf16[4,128,256]{2,1,0:T(8,128)(2,1)} %param.9) | copy-start | bytes 786436
  0.0 6.8 %copy-start.5 = (bf16[4,128,256]{2,1,0:T(8,128)(2,1)S(1)}, bf16[4,128,256]{2,1,0:T(8,128)(2,1)}, u32[]{:S(2)}) copy-start(bf16[4,128,256]{2,1,0:T(8,128)(2,1)} %param.8) | copy-start | bytes 786436
  0.0 6.8 %copy-start.6 = (bf16[4,128,256]{2,1,0:T(8,128)(2,1)S(1)}, bf16[4,128,256]{2,1,0:T(8,128)(2,1)}, u32[]{:S(2)}) copy-start(bf16[4,128,256]{2,1,0:T(8,128)(2,1)} %param.7) | copy-start | bytes 786436
  1.2 17.7 %collective-permute-start.2 = (bf16[256,256]{1,0:T(8,128)(2,1)S(1)}, bf16[256,256]{1,0:T(8,128)(2,1)S(1)}, u32[]{:S(2)}, u32[]{:S(2)}) collective-permute-start(bf16[256,256]{1,0:T(8,128)(2,1)S(1)} %pad_maximum_fusion.3), channel_id=1, source_target_pairs={{0,16},{4,20},{8,24},{12,28},{16,0},{20,4},{24,8},{28,12},{1,17},{... | collective-permute-start | bytes 393224 | tf_op jit(solution)/shard_map/ppermute | solution.py:315
  5.4 11.3 %copy-start.1 = (s32[4,2,4]{2,1,0:T(2,128)S(1)}, s32[4,2,4]{2,1,0:T(2,128)}, u32[]{:S(2)}) copy-start(s32[4,2,4]{2,1,0:T(2,128)} %rand_ref.1) | copy-start | bytes 388
  5.4 11.3 %copy-start.2 = (s32[4,2]{0,1:T(2,128)S(1)}, s32[4,2]{0,1:T(2,128)}, u32[]{:S(2)}) copy-start(s32[4,2]{0,1:T(2,128)} %param.11) | copy-start | bytes 100
  5.4 11.3 %copy-start.3 = (s32[4,2]{0,1:T(2,128)S(1)}, s32[4,2]{0,1:T(2,128)}, u32[]{:S(2)}) copy-start(s32[4,2]{0,1:T(2,128)} %param.13) | copy-start | bytes 100
  5.4 13.5 %collective-permute-start = (bf16[256,256]{1,0:T(8,128)(2,1)S(1)}, bf16[256,256]{1,0:T(8,128)(2,1)S(1)}, u32[]{:S(2)}, u32[]{:S(2)}) collective-permute-start(bf16[256,256]{1,0:T(8,128)(2,1)S(1)} %pad_maximum_fusion.1), channel_id=1, source_target_pairs={{0,24},{4,28},{8,16},{12,20},{16,8},{20,12},{24,0},{28,4},{1,25},{... | collective-permute-start | bytes 393224 | tf_op jit(solution)/shard_map/ppermute | solution.py:315
  7.8 21.9 %all-to-all-start = ((bf16[4,384,256]{2,1,0:T(8,128)(2,1)}), bf16[4,384,256]{2,1,0:T(8,128)(2,1)S(1)}, u32[]{:S(2)}, u32[]{:S(2)}) async-start(bf16[4,384,256]{2,1,0:T(8,128)(2,1)} %pad_maximum_fusion), calls=%async_computation | async-start | bytes 1572864 | tf_op jit(solution)/shard_map/all_to_all | solution.py:319
  11.3 12.6 %collective-permute-start.1 = (bf16[256,256]{1,0:T(8,128)(2,1)S(1)}, bf16[256,256]{1,0:T(8,128)(2,1)S(1)}, u32[]{:S(2)}, u32[]{:S(2)}) collective-permute-start(bf16[256,256]{1,0:T(8,128)(2,1)S(1)} %pad_maximum_fusion.2), channel_id=1, source_target_pairs={{0,20},{4,16},{8,28},{12,24},{16,4},{20,0},{24,12},{28,8},{1,21},{... | collective-permute-start | bytes 393224 | tf_op jit(solution)/shard_map/ppermute | solution.py:315
  14.6 15.1 %collective-permute-start.3 = (bf16[256,256]{1,0:T(8,128)(2,1)S(1)}, bf16[256,256]{1,0:T(8,128)(2,1)S(1)}, u32[]{:S(2)}, u32[]{:S(2)}) collective-permute-start(bf16[256,256]{1,0:T(8,128)(2,1)S(1)} %pad_maximum_fusion.4), channel_id=1, source_target_pairs={{0,28},{4,24},{8,20},{12,16},{16,12},{20,8},{24,4},{28,0},{1,29},{... | collective-permute-start | bytes 393224 | tf_op jit(solution)/shard_map/ppermute | solution.py:315
  17.4 12.3 %collective-permute-start.4 = (bf16[16,128]{1,0:T(8,128)(2,1)S(1)}, bf16[16,128]{1,0:T(8,128)(2,1)S(1)}, u32[]{:S(2)}, u32[]{:S(2)}) collective-permute-start(bf16[16,128]{1,0:T(8,128)(2,1)S(1)} %get-tuple-element.10), channel_id=1, source_target_pairs={{0,4},{4,0},{8,12},{12,8},{16,20},{20,16},{24,28},{28,24},{1,5},{5... | collective-permute-start | bytes 12296 | tf_op jit(solution)/shard_map/ppermute | solution.py:321
  18.9 10.8 %collective-permute-start.5 = (bf16[16,128]{1,0:T(8,128)(2,1)S(1)}, bf16[16,128]{1,0:T(8,128)(2,1)S(1)}, u32[]{:S(2)}, u32[]{:S(2)}) collective-permute-start(bf16[16,128]{1,0:T(8,128)(2,1)S(1)} %get-tuple-element.11), channel_id=1, source_target_pairs={{0,8},{4,12},{8,0},{12,4},{16,24},{20,28},{24,16},{28,20},{1,9},{5... | collective-permute-start | bytes 12296 | tf_op jit(solution)/shard_map/ppermute | solution.py:321
  19.0 10.8 %collective-permute-start.6 = (bf16[16,128]{1,0:T(8,128)(2,1)S(1)}, bf16[16,128]{1,0:T(8,128)(2,1)S(1)}, u32[]{:S(2)}, u32[]{:S(2)}) collective-permute-start(bf16[16,128]{1,0:T(8,128)(2,1)S(1)} %get-tuple-element.12), channel_id=1, source_target_pairs={{0,12},{4,8},{8,4},{12,0},{16,28},{20,24},{24,20},{28,16},{1,13},{... | collective-permute-start | bytes 12296 | tf_op jit(solution)/shard_map/ppermute | solution.py:321
  30.9 13.1 %copy-start = (bf16[1024,512]{1,0:T(8,128)(2,1)S(1)}, bf16[1024,512]{1,0:T(8,128)(2,1)}, u32[]{:S(2)}) copy-start(bf16[1024,512]{1,0:T(8,128)(2,1)} %weight_ref.1) | copy-start | bytes 3145732
  44.0 1.9 %collective-permute-start.7 = (bf16[8,128,256]{2,1,0:T(8,128)(2,1)S(1)}, bf16[8,128,256]{2,1,0:T(8,128)(2,1)S(1)}, u32[]{:S(2)}, u32[]{:S(2)}) collective-permute-start(bf16[8,128,256]{2,1,0:T(8,128)(2,1)S(1)} %all_to_all.10.refs_0_), channel_id=1, source_target_pairs={{0,1},{1,0},{2,3},{3,2},{4,5},{5,4},{6,7},{7,6},{8,9},{9,8},{10,11... | collective-permute-start | bytes 1572872 | tf_op jit(solution)/shard_map/ppermute | solution.py:369

commit v5 on v4

--- a/solution.py
+++ b/solution.py
@@ -140,7 +140,7 @@
 
 
 NEAR = (1, 2, 3)
-FAR = (6, 5, 4, 7)
+FAR = (4, 5, 6, 7)
 EARLY, LATE = FAR, ()
 
 
@@ -191,34 +191,28 @@
     blocks_here = rows // BLOCK
     heads = width // HEAD_DIM
     scale = HEAD_DIM ** (-0.5) * 1.4426950408889634
+    biases = []
     for n in range(askers):
         counts = counts_refs[n][...].astype(jnp.float32)
-        bias = jnp.where(counts > 0, jnp.log2(jnp.maximum(counts, 1.0)), -1e30)
-        wide = jnp.concatenate(
-            [
-                jnp.concatenate(
-                    [
-                        jnp.broadcast_to(bias[j * tiles + i : j * tiles + i + 1, :], (BLOCK, HEAD_DIM))
-                        for i in tuple(range(askers)) + FAR
-                    ],
-                    1,
+        biases.append(jnp.where(counts > 0, jnp.log2(jnp.maximum(counts, 1.0)), -1e30))
+    for h in range(heads):
+        cols = slice(h * HEAD_DIM, (h + 1) * HEAD_DIM)
+        keys = [ref[ref.shape[0] - 2 * rows : ref.shape[0] - rows, cols] for ref in pieces]
+        scores = lax.dot_general(
+            jnp.concatenate([near_ref[spot ^ n, 0:rows, cols] for n in range(askers)], 0),
+            jnp.concatenate(keys, 0),
+            (((1,), (1,)), ((), ())),
+            preferred_element_type=jnp.float32,
+        )
+        for n in range(askers):
+            for j in range(blocks_here):
+                at = n * rows + j * BLOCK
+                wide = jnp.concatenate(
+                    [biases[n][j * tiles + i : j * tiles + i + 1, :] for i in tuple(range(askers)) + FAR], 1
                 )
-                for j in range(blocks_here)
-            ],
-            0,
-        )
-        for h in range(heads):
-            cols = slice(h * HEAD_DIM, (h + 1) * HEAD_DIM)
-            keys = [ref[ref.shape[0] - 2 * rows : ref.shape[0] - rows, cols] for ref in pieces]
-            scores = lax.dot_general(
-                near_ref[spot ^ n, 0:rows, cols],
-                jnp.concatenate(keys, 0),
-                (((1,), (1,)), ((), ())),
-                preferred_element_type=jnp.float32,
-            )
-            shifted = scores * scale + wide
-            weights = jnp.exp2(shifted - jnp.max(shifted, axis=1, keepdims=True))
-            weights_ref[n * heads + h] = weights.astype(jnp.bfloat16)
+                shifted = scores[at : at + BLOCK] * scale + wide
+                weights = jnp.exp2(shifted - jnp.max(shifted, axis=1, keepdims=True))
+                weights_ref[n * heads + h, j * BLOCK : (j + 1) * BLOCK, :] = weights.astype(jnp.bfloat16)
 
 
 def sum_kernel(me_ref, weights_ref, near_ref, early_ref, *refs, copies):

time: 47.3 us -> 47.2 us (level)
  waiting for transfers between devices: 10.2 us -> 12 us
  blocking collectives: 12.3 us -> 10.6 us
    all_to_all x1, blocking collectives: 12.3 us -> 10.6 us  [half_path(): lax.all_to_all(attention, ('ctx', 'head'), split_axis=0, concat_axis=0, t...]
    ppermute x4, waiting for transfers between devices: 8.69 us -> 9.88 us  [half_path(): lax.ppermute(part, 'ctx', [(i, i ^ flip) for i in range(ctx)])]
    ppermute x3, waiting for transfers between devices: 0.03 us -> 0.69 us  [half_path(): lax.ppermute(part, 'ctx', [(i, i ^ n + 1) for i in range(ctx)])]
  transfers between devices with their start and end apart: 9 -> 9, of which waited for: 3 -> 4; matrix products, arithmetic and copies ran while one was open for 2% -> 2% of each run, Pallas kernels for 2% -> 3%
where the time goes in v5:
time: 47.2 us; the launch traced here: 46.9 us
  starting transfers between devices  17.7 us (38%)
  waiting for transfers between devices  12 us (25%)
  blocking collectives  10.6 us (22%)
  Pallas kernels  4.25 us (9%)
  local copies, waits for them, and re-layouts  1.2 us (3%)
  other arithmetic  0.99 us (2%)
    ppermute x4, starting transfers between devices, half_path(): lax.ppermute(part, 'ctx', [(i, i ^ flip) for i in range(ctx)])  10.6 us
    all_to_all x1, blocking collectives, half_path(): lax.all_to_all(attention, ('ctx', 'head'), split_axis=0, concat_axis=0, t...  10.6 us
    ppermute x4, waiting for transfers between devices, half_path(): lax.ppermute(part, 'ctx', [(i, i ^ flip) for i in range(ctx)])  9.88 us
    ppermute x3, starting transfers between devices, half_path(): lax.ppermute(part, 'ctx', [(i, i ^ n + 1) for i in range(ctx)])  3.55 us
    all_to_all x1, starting transfers between devices, half_path(): lax.all_to_all(packed, 'ctx', split_axis=0, concat_axis=0, tiled=True, ax...  3.49 us
    ppermute x1, waiting for transfers between devices, half_path(): beside = lax.ppermute(home, 'head', [(i, i ^ 1) for i in range(groups)])  1.45 us
    squeeze x1, local copies, waits for them, and re-layouts, far_piece(): take = lambda block: lax.dynamic_slice_in_dim(block, seq, 1, 0)[0]  1.17 us
    pallas_call x1, Pallas kernels, half_path(): pl.pallas_call(functools.partial(finish_kernel, flip=1, first=0), in_spec...  1.16 us
  transfers between devices with their start and end apart: 9, of which 4 were waited for; matrix products, arithmetic and copies ran while one was open for 2% of the time, Pallas kernels for 3%

profile of v5, /device:TPU:0, one launch (start us, length us, event | category | flops | bytes accessed | tf_op | source)
XLA Modules:
  0.0 46.9 jit_solution(11173533646855629568)
XLA Ops:
  0.0 0.0 copy-start.4
  0.0 0.0 copy-start.5
  0.0 0.0 copy-start.6
  0.0 1.2 %dynamic-slice_bitcast_fusion = (bf16[128,256]{1,0:T(8,128)(2,1)S(1)}, bf16[128,256]{1,0:T(8,128)(2,1)S(1)}, bf16[128,256]{1,0:T(8,128)(2,1)S(1)}, bf16[128,256]...) fusion(bf16[4,128,256]{2,1,0:T(8,128)(2,1)} %param.9, ...), kind=kLoop, calls=%fused_computation.5 | loop fusion | bytes 1048592 | tf_op jit(solution)/shard_map/squeeze | solution.py:295
  1.2 5.2 %collective-permute-start.2 = (bf16[256,256]{1,0:T(8,128)(2,1)S(1)}, bf16[256,256]{1,0:T(8,128)(2,1)S(1)}, u32[]{:S(2)}, u32[]{:S(2)}) collective-permute-start(bf16[256,256]{1,0:T(8,128)(2,1)S(1)} %pad_maximum_fusion.3), channel_id=1, source_target_pairs={{0,24},{4,28},{8,16},{12,20},{16,8},{20,12},{24,0},{28,4},{1,25},{... | collective-permute-start | bytes 393224 | tf_op jit(solution)/shard_map/ppermute | solution.py:309
  6.4 0.0 copy-start.1
  6.4 0.0 copy-start.2
  6.4 0.0 copy-start.3
  6.4 0.1 collective-permute-start
  6.5 0.0 copy-done.4
  6.5 0.0 copy-done.5
  6.5 0.0 copy-done.6
  6.5 0.9 %pad_maximum_fusion = bf16[4,384,256]{2,1,0:T(8,128)(2,1)} fusion(bf16[4,128,256]{2,1,0:T(8,128)(2,1)S(1)} %copy-done.4, bf16[4,128,256]{2,1,0:T(8,128)(2,1)S(1)} %copy-done.5, bf16[4,128,256]{2,1,0:T(8,128)(2,1)S(1)} %copy-done.6), kind=kLoop, calls=%fused_computation | loop fusion | flops 2359296 | bytes 1572864 | tf_op jit(solution)/shard_map/concatenate | solution.py:307
  7.5 3.5 %all-to-all-start = ((bf16[4,384,256]{2,1,0:T(8,128)(2,1)}), bf16[4,384,256]{2,1,0:T(8,128)(2,1)S(1)}, u32[]{:S(2)}, u32[]{:S(2)}) async-start(bf16[4,384,256]{2,1,0:T(8,128)(2,1)} %pad_maximum_fusion), calls=%async_computation | async-start | bytes 1572864 | tf_op jit(solution)/shard_map/all_to_all | solution.py:313
  11.0 4.4 %collective-permute-start.1 = (bf16[256,256]{1,0:T(8,128)(2,1)S(1)}, bf16[256,256]{1,0:T(8,128)(2,1)S(1)}, u32[]{:S(2)}, u32[]{:S(2)}) collective-permute-start(bf16[256,256]{1,0:T(8,128)(2,1)S(1)} %pad_maximum_fusion.2), channel_id=1, source_target_pairs={{0,20},{4,16},{8,28},{12,24},{16,4},{20,0},{24,12},{28,8},{1,21},{... | collective-permute-start | bytes 393224 | tf_op jit(solution)/shard_map/ppermute | solution.py:309
  15.4 1.0 %collective-permute-start.3 = (bf16[256,256]{1,0:T(8,128)(2,1)S(1)}, bf16[256,256]{1,0:T(8,128)(2,1)S(1)}, u32[]{:S(2)}, u32[]{:S(2)}) collective-permute-start(bf16[256,256]{1,0:T(8,128)(2,1)S(1)} %pad_maximum_fusion.4), channel_id=1, source_target_pairs={{0,28},{4,24},{8,20},{12,16},{16,12},{20,8},{24,4},{28,0},{1,29},{... | collective-permute-start | bytes 393224 | tf_op jit(solution)/shard_map/ppermute | solution.py:309
  16.4 0.0 copy-done.1
  16.4 0.0 copy-done.2
  16.4 0.0 copy-done.3
  16.4 0.7 %count.1 = (bf16[16,128]{1,0:T(8,128)(2,1)S(1)}, bf16[16,128]{1,0:T(8,128)(2,1)S(1)}, bf16[16,128]{1,0:T(8,128)(2,1)S(1)}, bf16[16,128]{1,0:T(8,128)(2,1)S(1)}) custom-call(s32[1]{0:T(128)} %bitcast.1.me_ref, s32[2,4]{1,0:T(2,128)S(1)} %bitcast.20, s32[4,2,4]{2,1,0:T(2,128)S(1)} %copy-done.1, s32[2,4]{1,0:T(2,128)S(1)} %bitcast.21), custom_call_target="tpu_custom_call" | custom-call | tf_op jit(solution)/shard_map/count/pallas_call | solution.py:299
  17.1 1.5 %collective-permute-start.4 = (bf16[16,128]{1,0:T(8,128)(2,1)S(1)}, bf16[16,128]{1,0:T(8,128)(2,1)S(1)}, u32[]{:S(2)}, u32[]{:S(2)}) collective-permute-start(bf16[16,128]{1,0:T(8,128)(2,1)S(1)} %get-tuple-element.10), channel_id=1, source_target_pairs={{0,4},{4,0},{8,12},{12,8},{16,20},{20,16},{24,28},{28,24},{1,5},{5... | collective-permute-start | bytes 12296 | tf_op jit(solution)/shard_map/ppermute | solution.py:315
  18.6 0.0 collective-permute-done.2.refs_2_
  18.6 0.0 collective-permute-start.5
  18.6 0.0 collective-permute-done.refs_0_
  18.6 2.0 %collective-permute-start.6 = (bf16[16,128]{1,0:T(8,128)(2,1)S(1)}, bf16[16,128]{1,0:T(8,128)(2,1)S(1)}, u32[]{:S(2)}, u32[]{:S(2)}) collective-permute-start(bf16[16,128]{1,0:T(8,128)(2,1)S(1)} %get-tuple-element.12), channel_id=1, source_target_pairs={{0,12},{4,8},{8,4},{12,0},{16,28},{20,24},{24,20},{28,16},{1,13},{... | collective-permute-start | bytes 12296 | tf_op jit(solution)/shard_map/ppermute | solution.py:315
  20.7 3.5 %collective-permute-done.1.refs_1_ = bf16[256,256]{1,0:T(8,128)(2,1)S(1)} collective-permute-done((bf16[256,256]{1,0:T(8,128)(2,1)S(1)}, bf16[256,256]{1,0:T(8,128)(2,1)S(1)}, u32[]{:S(2)}, u32[]{:S(2)}) %collective-permute-start.1) | collective-permute-done | bytes 131104 | tf_op jit(solution)/shard_map/ppermute | solution.py:309
  24.1 6.4 %collective-permute-done.3.refs_3_ = bf16[256,256]{1,0:T(8,128)(2,1)S(1)} collective-permute-done((bf16[256,256]{1,0:T(8,128)(2,1)S(1)}, bf16[256,256]{1,0:T(8,128)(2,1)S(1)}, u32[]{:S(2)}, u32[]{:S(2)}) %collective-permute-start.3) | collective-permute-done | bytes 131104 | tf_op jit(solution)/shard_map/ppermute | solution.py:309
  30.6 0.0 collective-permute-done.4.refs_1_
  30.6 0.0 collective-permute-done.5.refs_2_
  30.6 0.7 %collective-permute-done.6.refs_3_ = bf16[16,128]{1,0:T(8,128)(2,1)S(1)} collective-permute-done((bf16[16,128]{1,0:T(8,128)(2,1)S(1)}, bf16[16,128]{1,0:T(8,128)(2,1)S(1)}, u32[]{:S(2)}, u32[]{:S(2)}) %collective-permute-start.6) | collective-permute-done | bytes 4128 | tf_op jit(solution)/shard_map/ppermute | solution.py:315
  31.3 0.0 all-to-all-done.near_ref
  31.3 1.1 %weigh.1.weights_ref = bf16[8,128,1024]{2,1,0:T(8,128)(2,1)S(1)} custom-call(s32[1]{0:T(128)} %bitcast.1.me_ref, bf16[4,384,256]{2,1,0:T(8,128)(2,1)S(1)} %all-to-all-done.near_ref, bf16[4,256,256]{2,1,0:T(8,128)(2,1)S(1)} %stack.1.early_ref, bf16[16,128]{1,0:T(8,128)(2,1)S(1)} %get-tuple-element.9.refs_0_, ...), custom_call_target="tpu_custom_call" | custom-call | flops 268435456 | bytes 2097152 | tf_op jit(solution)/shard_map/weigh/pallas_call | solution.py:331
  32.4 0.0 copy-start
  32.5 0.8 %sum.1 = bf16[8,128,256]{2,1,0:T(8,128)(2,1)S(1)} custom-call(s32[1]{0:T(128)} %bitcast.1.me_ref, bf16[8,128,1024]{2,1,0:T(8,128)(2,1)S(1)} %weigh.1.weights_ref, bf16[4,384,256]{2,1,0:T(8,128)(2,1)S(1)} %all-to-all-done.near_ref, bf16[4,256,256]{2,1,0:T(8,128)(2,1)S(1)} %stack.1.early_ref), custom_call_target="tpu_custom_call" | custom-call | flops 268435456 | bytes 2097152 | tf_op jit(solution)/shard_map/sum/pallas_call | solution.py:341
  33.2 10.6 %all_to_all.10.refs_0_ = bf16[8,128,256]{2,1,0:T(8,128)(2,1)S(1)} all-to-all(bf16[8,128,256]{2,1,0:T(8,128)(2,1)S(1)} %sum.1), channel_id=1, replica_groups={{0,2,4,6,8,10,12,14},{1,3,5,7,9,11,13,15},{16,18,20,22,24,26,28,30},{17..., dimensions={0} | all-to-all | bytes 1048576 | tf_op jit(solution)/shard_map/all_to_all | solution.py:351
  43.8 0.0 collective-permute-start.7
  43.9 0.0 copy-done
  43.9 0.4 project.1.before_ref
  44.3 1.4 %collective-permute-done.7.part_ref = bf16[8,128,256]{2,1,0:T(8,128)(2,1)S(1)} collective-permute-done((bf16[8,128,256]{2,1,0:T(8,128)(2,1)S(1)}, bf16[8,128,256]{2,1,0:T(8,128)(2,1)S(1)}, u32[]{:S(2)}, u32[]{:S(2)}) %collective-permute-start.7) | collective-permute-done | bytes 524320 | tf_op jit(solution)/shard_map/ppermute | solution.py:363
  45.8 1.2 %finish.1 = bf16[4,128,512]{2,1,0:T(8,128)(2,1)} custom-call(s32[1]{0:T(128)} %bitcast.group_ref, f32[4,128,512]{2,1,0:T(8,128)S(1)} %project.1.before_ref, bf16[8,128,256]{2,1,0:T(8,128)(2,1)S(1)} %collective-permute-done.7.part_ref, bf16[1024,512]{1,0:T(8,128)(2,1)S(1)} %copy-done), custom_call_target="tpu_custom_call" | custom-call | tf_op jit(solution)/shard_map/finish/pallas_call | solution.py:381
  (5 shorter events, 0.1 us)
Async XLA Ops:
  0.0 6.5 %copy-start.4 = (bf16[4,128,256]{2,1,0:T(8,128)(2,1)S(1)}, bf16[4,128,256]{2,1,0:T(8,128)(2,1)}, u32[]{:S(2)}) copy-start(bf16[4,128,256]{2,1,0:T(8,128)(2,1)} %param.9) | copy-start | bytes 786436
  0.0 6.5 %copy-start.5 = (bf16[4,128,256]{2,1,0:T(8,128)(2,1)S(1)}, bf16[4,128,256]{2,1,0:T(8,128)(2,1)}, u32[]{:S(2)}) copy-start(bf16[4,128,256]{2,1,0:T(8,128)(2,1)} %param.8) | copy-start | bytes 786436
  0.0 6.5 %copy-start.6 = (bf16[4,128,256]{2,1,0:T(8,128)(2,1)S(1)}, bf16[4,128,256]{2,1,0:T(8,128)(2,1)}, u32[]{:S(2)}) copy-start(bf16[4,128,256]{2,1,0:T(8,128)(2,1)} %param.7) | copy-start | bytes 786436
  1.2 17.4 %collective-permute-start.2 = (bf16[256,256]{1,0:T(8,128)(2,1)S(1)}, bf16[256,256]{1,0:T(8,128)(2,1)S(1)}, u32[]{:S(2)}, u32[]{:S(2)}) collective-permute-start(bf16[256,256]{1,0:T(8,128)(2,1)S(1)} %pad_maximum_fusion.3), channel_id=1, source_target_pairs={{0,24},{4,28},{8,16},{12,20},{16,8},{20,12},{24,0},{28,4},{1,25},{... | collective-permute-start | bytes 393224 | tf_op jit(solution)/shard_map/ppermute | solution.py:309
  6.4 10.0 %copy-start.1 = (s32[4,2,4]{2,1,0:T(2,128)S(1)}, s32[4,2,4]{2,1,0:T(2,128)}, u32[]{:S(2)}) copy-start(s32[4,2,4]{2,1,0:T(2,128)} %rand_ref.1) | copy-start | bytes 388
  6.4 10.0 %copy-start.2 = (s32[4,2]{0,1:T(2,128)S(1)}, s32[4,2]{0,1:T(2,128)}, u32[]{:S(2)}) copy-start(s32[4,2]{0,1:T(2,128)} %param.11) | copy-start | bytes 100
  6.4 10.0 %copy-start.3 = (s32[4,2]{0,1:T(2,128)S(1)}, s32[4,2]{0,1:T(2,128)}, u32[]{:S(2)}) copy-start(s32[4,2]{0,1:T(2,128)} %param.13) | copy-start | bytes 100
  6.4 12.2 %collective-permute-start = (bf16[256,256]{1,0:T(8,128)(2,1)S(1)}, bf16[256,256]{1,0:T(8,128)(2,1)S(1)}, u32[]{:S(2)}, u32[]{:S(2)}) collective-permute-start(bf16[256,256]{1,0:T(8,128)(2,1)S(1)} %pad_maximum_fusion.1), channel_id=1, source_target_pairs={{0,16},{4,20},{8,24},{12,28},{16,0},{20,4},{24,8},{28,12},{1,17},{... | collective-permute-start | bytes 393224 | tf_op jit(solution)/shard_map/ppermute | solution.py:309
  7.5 23.8 %all-to-all-start = ((bf16[4,384,256]{2,1,0:T(8,128)(2,1)}), bf16[4,384,256]{2,1,0:T(8,128)(2,1)S(1)}, u32[]{:S(2)}, u32[]{:S(2)}) async-start(bf16[4,384,256]{2,1,0:T(8,128)(2,1)} %pad_maximum_fusion), calls=%async_computation | async-start | bytes 1572864 | tf_op jit(solution)/shard_map/all_to_all | solution.py:313
  11.0 13.1 %collective-permute-start.1 = (bf16[256,256]{1,0:T(8,128)(2,1)S(1)}, bf16[256,256]{1,0:T(8,128)(2,1)S(1)}, u32[]{:S(2)}, u32[]{:S(2)}) collective-permute-start(bf16[256,256]{1,0:T(8,128)(2,1)S(1)} %pad_maximum_fusion.2), channel_id=1, source_target_pairs={{0,20},{4,16},{8,28},{12,24},{16,4},{20,0},{24,12},{28,8},{1,21},{... | collective-permute-start | bytes 393224 | tf_op jit(solution)/shard_map/ppermute | solution.py:309
  15.4 15.1 %collective-permute-start.3 = (bf16[256,256]{1,0:T(8,128)(2,1)S(1)}, bf16[256,256]{1,0:T(8,128)(2,1)S(1)}, u32[]{:S(2)}, u32[]{:S(2)}) collective-permute-start(bf16[256,256]{1,0:T(8,128)(2,1)S(1)} %pad_maximum_fusion.4), channel_id=1, source_target_pairs={{0,28},{4,24},{8,20},{12,16},{16,12},{20,8},{24,4},{28,0},{1,29},{... | collective-permute-start | bytes 393224 | tf_op jit(solution)/shard_map/ppermute | solution.py:309
  17.1 13.5 %collective-permute-start.4 = (bf16[16,128]{1,0:T(8,128)(2,1)S(1)}, bf16[16,128]{1,0:T(8,128)(2,1)S(1)}, u32[]{:S(2)}, u32[]{:S(2)}) collective-permute-start(bf16[16,128]{1,0:T(8,128)(2,1)S(1)} %get-tuple-element.10), channel_id=1, source_target_pairs={{0,4},{4,0},{8,12},{12,8},{16,20},{20,16},{24,28},{28,24},{1,5},{5... | collective-permute-start | bytes 12296 | tf_op jit(solution)/shard_map/ppermute | solution.py:315
  18.6 12.0 %collective-permute-start.5 = (bf16[16,128]{1,0:T(8,128)(2,1)S(1)}, bf16[16,128]{1,0:T(8,128)(2,1)S(1)}, u32[]{:S(2)}, u32[]{:S(2)}) collective-permute-start(bf16[16,128]{1,0:T(8,128)(2,1)S(1)} %get-tuple-element.11), channel_id=1, source_target_pairs={{0,8},{4,12},{8,0},{12,4},{16,24},{20,28},{24,16},{28,20},{1,9},{5... | collective-permute-start | bytes 12296 | tf_op jit(solution)/shard_map/ppermute | solution.py:315
  18.6 12.6 %collective-permute-start.6 = (bf16[16,128]{1,0:T(8,128)(2,1)S(1)}, bf16[16,128]{1,0:T(8,128)(2,1)S(1)}, u32[]{:S(2)}, u32[]{:S(2)}) collective-permute-start(bf16[16,128]{1,0:T(8,128)(2,1)S(1)} %get-tuple-element.12), channel_id=1, source_target_pairs={{0,12},{4,8},{8,4},{12,0},{16,28},{20,24},{24,20},{28,16},{1,13},{... | collective-permute-start | bytes 12296 | tf_op jit(solution)/shard_map/ppermute | solution.py:315
  32.4 11.4 %copy-start = (bf16[1024,512]{1,0:T(8,128)(2,1)S(1)}, bf16[1024,512]{1,0:T(8,128)(2,1)}, u32[]{:S(2)}) copy-start(bf16[1024,512]{1,0:T(8,128)(2,1)} %weight_ref.1) | copy-start | bytes 3145732
  43.8 1.9 %collective-permute-start.7 = (bf16[8,128,256]{2,1,0:T(8,128)(2,1)S(1)}, bf16[8,128,256]{2,1,0:T(8,128)(2,1)S(1)}, u32[]{:S(2)}, u32[]{:S(2)}) collective-permute-start(bf16[8,128,256]{2,1,0:T(8,128)(2,1)S(1)} %all_to_all.10.refs_0_), channel_id=1, source_target_pairs={{0,1},{1,0},{2,3},{3,2},{4,5},{5,4},{6,7},{7,6},{8,9},{9,8},{10,11... | collective-permute-start | bytes 1572872 | tf_op jit(solution)/shard_map/ppermute | solution.py:363

commit v6 on v5

--- a/solution.py
+++ b/solution.py
@@ -263,13 +263,11 @@
         weight_ref[pl.ds(pl.multiple_of((side * cores + core) * depth, depth), depth), :]
         for side in range(sides)
     ]
+    weight = jnp.concatenate(weights, 0)
     copies = []
     for n in range(buffer.shape[0]):
-        total = before_ref[first + n]
-        for side in range(sides):
-            total = total + jnp.dot(
-                part_ref[n * sides + side], weights[side], preferred_element_type=jnp.float32
-            )
+        features = jnp.concatenate([part_ref[n * sides + side] for side in range(sides)], 1)
+        total = before_ref[first + n] + jnp.dot(features, weight, preferred_element_type=jnp.float32)
         buffer[n] = total.astype(buffer.dtype)
         copies.append(pltpu.make_async_copy(buffer.at[n], out_ref.at[first + n], sems.at[n]))
         copies[-1].start()

time: 47.2 us -> 47.2 us (level)
  no operation moved by 1% of the time
where the time goes in v6:
time: 47.2 us; the launch traced here: 46.9 us
  starting transfers between devices  17.7 us (38%)
  waiting for transfers between devices  12 us (25%)
  blocking collectives  10.6 us (22%)
  Pallas kernels  4.25 us (9%)
  local copies, waits for them, and re-layouts  1.2 us (3%)
  other arithmetic  0.99 us (2%)
    ppermute x4, starting transfers between devices, half_path(): lax.ppermute(part, 'ctx', [(i, i ^ flip) for i in range(ctx)])  10.6 us
    all_to_all x1, blocking collectives, half_path(): lax.all_to_all(attention, ('ctx', 'head'), split_axis=0, concat_axis=0, t...  10.6 us
    ppermute x4, waiting for transfers between devices, half_path(): lax.ppermute(part, 'ctx', [(i, i ^ flip) for i in range(ctx)])  9.88 us
    ppermute x3, starting transfers between devices, half_path(): lax.ppermute(part, 'ctx', [(i, i ^ n + 1) for i in range(ctx)])  3.55 us
    all_to_all x1, starting transfers between devices, half_path(): lax.all_to_all(packed, 'ctx', split_axis=0, concat_axis=0, tiled=True, ax...  3.49 us
    ppermute x1, waiting for transfers between devices, half_path(): beside = lax.ppermute(home, 'head', [(i, i ^ 1) for i in range(groups)])  1.45 us
    squeeze x1, local copies, waits for them, and re-layouts, far_piece(): take = lambda block: lax.dynamic_slice_in_dim(block, seq, 1, 0)[0]  1.17 us
    pallas_call x1, Pallas kernels, half_path(): pl.pallas_call(functools.partial(finish_kernel, flip=1, first=0), in_spec...  1.16 us
  transfers between devices with their start and end apart: 9, of which 4 were waited for; matrix products, arithmetic and copies ran while one was open for 2% of the time, Pallas kernels for 3%

profile of v6, /device:TPU:0, one launch (start us, length us, event | category | flops | bytes accessed | tf_op | source)
XLA Modules:
  0.0 46.9 jit_solution(11173533646855629568)
XLA Ops:
  0.0 0.0 copy-start.4
  0.0 0.0 copy-start.5
  0.0 0.0 copy-start.6
  0.0 1.2 %dynamic-slice_bitcast_fusion = (bf16[128,256]{1,0:T(8,128)(2,1)S(1)}, bf16[128,256]{1,0:T(8,128)(2,1)S(1)}, bf16[128,256]{1,0:T(8,128)(2,1)S(1)}, bf16[128,256]...) fusion(bf16[4,128,256]{2,1,0:T(8,128)(2,1)} %param.9, ...), kind=kLoop, calls=%fused_computation.5 | loop fusion | bytes 1048592 | tf_op jit(solution)/shard_map/squeeze | solution.py:293
  1.2 5.2 %collective-permute-start.2 = (bf16[256,256]{1,0:T(8,128)(2,1)S(1)}, bf16[256,256]{1,0:T(8,128)(2,1)S(1)}, u32[]{:S(2)}, u32[]{:S(2)}) collective-permute-start(bf16[256,256]{1,0:T(8,128)(2,1)S(1)} %pad_maximum_fusion.3), channel_id=1, source_target_pairs={{0,24},{4,28},{8,16},{12,20},{16,8},{20,12},{24,0},{28,4},{1,25},{... | collective-permute-start | bytes 393224 | tf_op jit(solution)/shard_map/ppermute | solution.py:307
  6.4 0.0 copy-start.1
  6.4 0.0 copy-start.2
  6.4 0.0 copy-start.3
  6.4 0.1 collective-permute-start
  6.5 0.0 copy-done.4
  6.5 0.0 copy-done.5
  6.5 0.0 copy-done.6
  6.5 0.9 %pad_maximum_fusion = bf16[4,384,256]{2,1,0:T(8,128)(2,1)} fusion(bf16[4,128,256]{2,1,0:T(8,128)(2,1)S(1)} %copy-done.4, bf16[4,128,256]{2,1,0:T(8,128)(2,1)S(1)} %copy-done.5, bf16[4,128,256]{2,1,0:T(8,128)(2,1)S(1)} %copy-done.6), kind=kLoop, calls=%fused_computation | loop fusion | flops 2359296 | bytes 1572864 | tf_op jit(solution)/shard_map/concatenate | solution.py:305
  7.5 3.5 %all-to-all-start = ((bf16[4,384,256]{2,1,0:T(8,128)(2,1)}), bf16[4,384,256]{2,1,0:T(8,128)(2,1)S(1)}, u32[]{:S(2)}, u32[]{:S(2)}) async-start(bf16[4,384,256]{2,1,0:T(8,128)(2,1)} %pad_maximum_fusion), calls=%async_computation | async-start | bytes 1572864 | tf_op jit(solution)/shard_map/all_to_all | solution.py:311
  11.0 4.4 %collective-permute-start.1 = (bf16[256,256]{1,0:T(8,128)(2,1)S(1)}, bf16[256,256]{1,0:T(8,128)(2,1)S(1)}, u32[]{:S(2)}, u32[]{:S(2)}) collective-permute-start(bf16[256,256]{1,0:T(8,128)(2,1)S(1)} %pad_maximum_fusion.2), channel_id=1, source_target_pairs={{0,20},{4,16},{8,28},{12,24},{16,4},{20,0},{24,12},{28,8},{1,21},{... | collective-permute-start | bytes 393224 | tf_op jit(solution)/shard_map/ppermute | solution.py:307
  15.4 1.0 %collective-permute-start.3 = (bf16[256,256]{1,0:T(8,128)(2,1)S(1)}, bf16[256,256]{1,0:T(8,128)(2,1)S(1)}, u32[]{:S(2)}, u32[]{:S(2)}) collective-permute-start(bf16[256,256]{1,0:T(8,128)(2,1)S(1)} %pad_maximum_fusion.4), channel_id=1, source_target_pairs={{0,28},{4,24},{8,20},{12,16},{16,12},{20,8},{24,4},{28,0},{1,29},{... | collective-permute-start | bytes 393224 | tf_op jit(solution)/shard_map/ppermute | solution.py:307
  16.4 0.0 copy-done.1
  16.4 0.0 copy-done.2
  16.4 0.0 copy-done.3
  16.4 0.7 %count.1 = (bf16[16,128]{1,0:T(8,128)(2,1)S(1)}, bf16[16,128]{1,0:T(8,128)(2,1)S(1)}, bf16[16,128]{1,0:T(8,128)(2,1)S(1)}, bf16[16,128]{1,0:T(8,128)(2,1)S(1)}) custom-call(s32[1]{0:T(128)} %bitcast.1.me_ref, s32[2,4]{1,0:T(2,128)S(1)} %bitcast.20, s32[4,2,4]{2,1,0:T(2,128)S(1)} %copy-done.1, s32[2,4]{1,0:T(2,128)S(1)} %bitcast.21), custom_call_target="tpu_custom_call" | custom-call | tf_op jit(solution)/shard_map/count/pallas_call | solution.py:297
  17.1 1.5 %collective-permute-start.4 = (bf16[16,128]{1,0:T(8,128)(2,1)S(1)}, bf16[16,128]{1,0:T(8,128)(2,1)S(1)}, u32[]{:S(2)}, u32[]{:S(2)}) collective-permute-start(bf16[16,128]{1,0:T(8,128)(2,1)S(1)} %get-tuple-element.10), channel_id=1, source_target_pairs={{0,4},{4,0},{8,12},{12,8},{16,20},{20,16},{24,28},{28,24},{1,5},{5... | collective-permute-start | bytes 12296 | tf_op jit(solution)/shard_map/ppermute | solution.py:313
  18.6 0.0 collective-permute-done.2.refs_2_
  18.6 0.0 collective-permute-start.5
  18.6 0.0 collective-permute-done.refs_0_
  18.6 2.0 %collective-permute-start.6 = (bf16[16,128]{1,0:T(8,128)(2,1)S(1)}, bf16[16,128]{1,0:T(8,128)(2,1)S(1)}, u32[]{:S(2)}, u32[]{:S(2)}) collective-permute-start(bf16[16,128]{1,0:T(8,128)(2,1)S(1)} %get-tuple-element.12), channel_id=1, source_target_pairs={{0,12},{4,8},{8,4},{12,0},{16,28},{20,24},{24,20},{28,16},{1,13},{... | collective-permute-start | bytes 12296 | tf_op jit(solution)/shard_map/ppermute | solution.py:313
  20.7 3.5 %collective-permute-done.1.refs_1_ = bf16[256,256]{1,0:T(8,128)(2,1)S(1)} collective-permute-done((bf16[256,256]{1,0:T(8,128)(2,1)S(1)}, bf16[256,256]{1,0:T(8,128)(2,1)S(1)}, u32[]{:S(2)}, u32[]{:S(2)}) %collective-permute-start.1) | collective-permute-done | bytes 131104 | tf_op jit(solution)/shard_map/ppermute | solution.py:307
  24.1 6.4 %collective-permute-done.3.refs_3_ = bf16[256,256]{1,0:T(8,128)(2,1)S(1)} collective-permute-done((bf16[256,256]{1,0:T(8,128)(2,1)S(1)}, bf16[256,256]{1,0:T(8,128)(2,1)S(1)}, u32[]{:S(2)}, u32[]{:S(2)}) %collective-permute-start.3) | collective-permute-done | bytes 131104 | tf_op jit(solution)/shard_map/ppermute | solution.py:307
  30.6 0.0 collective-permute-done.4.refs_1_
  30.6 0.0 collective-permute-done.5.refs_2_
  30.6 0.7 %collective-permute-done.6.refs_3_ = bf16[16,128]{1,0:T(8,128)(2,1)S(1)} collective-permute-done((bf16[16,128]{1,0:T(8,128)(2,1)S(1)}, bf16[16,128]{1,0:T(8,128)(2,1)S(1)}, u32[]{:S(2)}, u32[]{:S(2)}) %collective-permute-start.6) | collective-permute-done | bytes 4128 | tf_op jit(solution)/shard_map/ppermute | solution.py:313
  31.3 0.0 all-to-all-done.near_ref
  31.3 1.1 %weigh.1.weights_ref = bf16[8,128,1024]{2,1,0:T(8,128)(2,1)S(1)} custom-call(s32[1]{0:T(128)} %bitcast.1.me_ref, bf16[4,384,256]{2,1,0:T(8,128)(2,1)S(1)} %all-to-all-done.near_ref, bf16[4,256,256]{2,1,0:T(8,128)(2,1)S(1)} %stack.1.early_ref, bf16[16,128]{1,0:T(8,128)(2,1)S(1)} %get-tuple-element.9.refs_0_, ...), custom_call_target="tpu_custom_call" | custom-call | flops 268435456 | bytes 2097152 | tf_op jit(solution)/shard_map/weigh/pallas_call | solution.py:329
  32.4 0.0 copy-start
  32.5 0.8 %sum.1 = bf16[8,128,256]{2,1,0:T(8,128)(2,1)S(1)} custom-call(s32[1]{0:T(128)} %bitcast.1.me_ref, bf16[8,128,1024]{2,1,0:T(8,128)(2,1)S(1)} %weigh.1.weights_ref, bf16[4,384,256]{2,1,0:T(8,128)(2,1)S(1)} %all-to-all-done.near_ref, bf16[4,256,256]{2,1,0:T(8,128)(2,1)S(1)} %stack.1.early_ref), custom_call_target="tpu_custom_call" | custom-call | flops 268435456 | bytes 2097152 | tf_op jit(solution)/shard_map/sum/pallas_call | solution.py:339
  33.2 10.6 %all_to_all.10.refs_0_ = bf16[8,128,256]{2,1,0:T(8,128)(2,1)S(1)} all-to-all(bf16[8,128,256]{2,1,0:T(8,128)(2,1)S(1)} %sum.1), channel_id=1, replica_groups={{0,2,4,6,8,10,12,14},{1,3,5,7,9,11,13,15},{16,18,20,22,24,26,28,30},{17..., dimensions={0} | all-to-all | bytes 1048576 | tf_op jit(solution)/shard_map/all_to_all | solution.py:349
  43.8 0.0 collective-permute-start.7
  43.9 0.0 copy-done
  43.9 0.4 project.1.before_ref
  44.3 1.4 %collective-permute-done.7.part_ref = bf16[8,128,256]{2,1,0:T(8,128)(2,1)S(1)} collective-permute-done((bf16[8,128,256]{2,1,0:T(8,128)(2,1)S(1)}, bf16[8,128,256]{2,1,0:T(8,128)(2,1)S(1)}, u32[]{:S(2)}, u32[]{:S(2)}) %collective-permute-start.7) | collective-permute-done | bytes 524320 | tf_op jit(solution)/shard_map/ppermute | solution.py:361
  45.8 1.2 %finish.1 = bf16[4,128,512]{2,1,0:T(8,128)(2,1)} custom-call(s32[1]{0:T(128)} %bitcast.group_ref, f32[4,128,512]{2,1,0:T(8,128)S(1)} %project.1.before_ref, bf16[8,128,256]{2,1,0:T(8,128)(2,1)S(1)} %collective-permute-done.7.part_ref, bf16[1024,512]{1,0:T(8,128)(2,1)S(1)} %copy-done), custom_call_target="tpu_custom_call" | custom-call | tf_op jit(solution)/shard_map/finish/pallas_call | solution.py:379
  (5 shorter events, 0.1 us)
Async XLA Ops:
  0.0 6.5 %copy-start.4 = (bf16[4,128,256]{2,1,0:T(8,128)(2,1)S(1)}, bf16[4,128,256]{2,1,0:T(8,128)(2,1)}, u32[]{:S(2)}) copy-start(bf16[4,128,256]{2,1,0:T(8,128)(2,1)} %param.9) | copy-start | bytes 786436
  0.0 6.5 %copy-start.5 = (bf16[4,128,256]{2,1,0:T(8,128)(2,1)S(1)}, bf16[4,128,256]{2,1,0:T(8,128)(2,1)}, u32[]{:S(2)}) copy-start(bf16[4,128,256]{2,1,0:T(8,128)(2,1)} %param.8) | copy-start | bytes 786436
  0.0 6.5 %copy-start.6 = (bf16[4,128,256]{2,1,0:T(8,128)(2,1)S(1)}, bf16[4,128,256]{2,1,0:T(8,128)(2,1)}, u32[]{:S(2)}) copy-start(bf16[4,128,256]{2,1,0:T(8,128)(2,1)} %param.7) | copy-start | bytes 786436
  1.2 17.4 %collective-permute-start.2 = (bf16[256,256]{1,0:T(8,128)(2,1)S(1)}, bf16[256,256]{1,0:T(8,128)(2,1)S(1)}, u32[]{:S(2)}, u32[]{:S(2)}) collective-permute-start(bf16[256,256]{1,0:T(8,128)(2,1)S(1)} %pad_maximum_fusion.3), channel_id=1, source_target_pairs={{0,24},{4,28},{8,16},{12,20},{16,8},{20,12},{24,0},{28,4},{1,25},{... | collective-permute-start | bytes 393224 | tf_op jit(solution)/shard_map/ppermute | solution.py:307
  6.4 10.0 %copy-start.1 = (s32[4,2,4]{2,1,0:T(2,128)S(1)}, s32[4,2,4]{2,1,0:T(2,128)}, u32[]{:S(2)}) copy-start(s32[4,2,4]{2,1,0:T(2,128)} %rand_ref.1) | copy-start | bytes 388
  6.4 10.0 %copy-start.2 = (s32[4,2]{0,1:T(2,128)S(1)}, s32[4,2]{0,1:T(2,128)}, u32[]{:S(2)}) copy-start(s32[4,2]{0,1:T(2,128)} %param.11) | copy-start | bytes 100
  6.4 10.0 %copy-start.3 = (s32[4,2]{0,1:T(2,128)S(1)}, s32[4,2]{0,1:T(2,128)}, u32[]{:S(2)}) copy-start(s32[4,2]{0,1:T(2,128)} %param.13) | copy-start | bytes 100
  6.4 12.2 %collective-permute-start = (bf16[256,256]{1,0:T(8,128)(2,1)S(1)}, bf16[256,256]{1,0:T(8,128)(2,1)S(1)}, u32[]{:S(2)}, u32[]{:S(2)}) collective-permute-start(bf16[256,256]{1,0:T(8,128)(2,1)S(1)} %pad_maximum_fusion.1), channel_id=1, source_target_pairs={{0,16},{4,20},{8,24},{12,28},{16,0},{20,4},{24,8},{28,12},{1,17},{... | collective-permute-start | bytes 393224 | tf_op jit(solution)/shard_map/ppermute | solution.py:307
  7.5 23.8 %all-to-all-start = ((bf16[4,384,256]{2,1,0:T(8,128)(2,1)}), bf16[4,384,256]{2,1,0:T(8,128)(2,1)S(1)}, u32[]{:S(2)}, u32[]{:S(2)}) async-start(bf16[4,384,256]{2,1,0:T(8,128)(2,1)} %pad_maximum_fusion), calls=%async_computation | async-start | bytes 1572864 | tf_op jit(solution)/shard_map/all_to_all | solution.py:311
  11.0 13.1 %collective-permute-start.1 = (bf16[256,256]{1,0:T(8,128)(2,1)S(1)}, bf16[256,256]{1,0:T(8,128)(2,1)S(1)}, u32[]{:S(2)}, u32[]{:S(2)}) collective-permute-start(bf16[256,256]{1,0:T(8,128)(2,1)S(1)} %pad_maximum_fusion.2), channel_id=1, source_target_pairs={{0,20},{4,16},{8,28},{12,24},{16,4},{20,0},{24,12},{28,8},{1,21},{... | collective-permute-start | bytes 393224 | tf_op jit(solution)/shard_map/ppermute | solution.py:307
  15.4 15.1 %collective-permute-start.3 = (bf16[256,256]{1,0:T(8,128)(2,1)S(1)}, bf16[256,256]{1,0:T(8,128)(2,1)S(1)}, u32[]{:S(2)}, u32[]{:S(2)}) collective-permute-start(bf16[256,256]{1,0:T(8,128)(2,1)S(1)} %pad_maximum_fusion.4), channel_id=1, source_target_pairs={{0,28},{4,24},{8,20},{12,16},{16,12},{20,8},{24,4},{28,0},{1,29},{... | collective-permute-start | bytes 393224 | tf_op jit(solution)/shard_map/ppermute | solution.py:307
  17.1 13.5 %collective-permute-start.4 = (bf16[16,128]{1,0:T(8,128)(2,1)S(1)}, bf16[16,128]{1,0:T(8,128)(2,1)S(1)}, u32[]{:S(2)}, u32[]{:S(2)}) collective-permute-start(bf16[16,128]{1,0:T(8,128)(2,1)S(1)} %get-tuple-element.10), channel_id=1, source_target_pairs={{0,4},{4,0},{8,12},{12,8},{16,20},{20,16},{24,28},{28,24},{1,5},{5... | collective-permute-start | bytes 12296 | tf_op jit(solution)/shard_map/ppermute | solution.py:313
  18.6 12.0 %collective-permute-start.5 = (bf16[16,128]{1,0:T(8,128)(2,1)S(1)}, bf16[16,128]{1,0:T(8,128)(2,1)S(1)}, u32[]{:S(2)}, u32[]{:S(2)}) collective-permute-start(bf16[16,128]{1,0:T(8,128)(2,1)S(1)} %get-tuple-element.11), channel_id=1, source_target_pairs={{0,8},{4,12},{8,0},{12,4},{16,24},{20,28},{24,16},{28,20},{1,9},{5... | collective-permute-start | bytes 12296 | tf_op jit(solution)/shard_map/ppermute | solution.py:313
  18.6 12.6 %collective-permute-start.6 = (bf16[16,128]{1,0:T(8,128)(2,1)S(1)}, bf16[16,128]{1,0:T(8,128)(2,1)S(1)}, u32[]{:S(2)}, u32[]{:S(2)}) collective-permute-start(bf16[16,128]{1,0:T(8,128)(2,1)S(1)} %get-tuple-element.12), channel_id=1, source_target_pairs={{0,12},{4,8},{8,4},{12,0},{16,28},{20,24},{24,20},{28,16},{1,13},{... | collective-permute-start | bytes 12296 | tf_op jit(solution)/shard_map/ppermute | solution.py:313
  32.4 11.4 %copy-start = (bf16[1024,512]{1,0:T(8,128)(2,1)S(1)}, bf16[1024,512]{1,0:T(8,128)(2,1)}, u32[]{:S(2)}) copy-start(bf16[1024,512]{1,0:T(8,128)(2,1)} %weight_ref.1) | copy-start | bytes 3145732
  43.8 1.9 %collective-permute-start.7 = (bf16[8,128,256]{2,1,0:T(8,128)(2,1)S(1)}, bf16[8,128,256]{2,1,0:T(8,128)(2,1)S(1)}, u32[]{:S(2)}, u32[]{:S(2)}) collective-permute-start(bf16[8,128,256]{2,1,0:T(8,128)(2,1)S(1)} %all_to_all.10.refs_0_), channel_id=1, source_target_pairs={{0,1},{1,0},{2,3},{3,2},{4,5},{5,4},{6,7},{7,6},{8,9},{9,8},{10,11... | collective-permute-start | bytes 1572872 | tf_op jit(solution)/shard_map/ppermute | solution.py:361

commit v7 on v6

--- a/solution.py
+++ b/solution.py
@@ -212,7 +212,7 @@
                 )
                 shifted = scores[at : at + BLOCK] * scale + wide
                 weights = jnp.exp2(shifted - jnp.max(shifted, axis=1, keepdims=True))
-                weights_ref[n * heads + h, j * BLOCK : (j + 1) * BLOCK, :] = weights.astype(jnp.bfloat16)
+                weights_ref[h * askers + n, j * BLOCK : (j + 1) * BLOCK, :] = weights.astype(jnp.bfloat16)
 
 
 def sum_kernel(me_ref, weights_ref, near_ref, early_ref, *refs, copies):
@@ -226,8 +226,11 @@
         cols = slice(h * HEAD_DIM, (h + 1) * HEAD_DIM)
         values = jnp.concatenate([ref[ref.shape[0] - rows :, cols] for ref in pieces], 0)
         both = jnp.concatenate([values, ones], 1)
-        for n in range(count // heads):
-            sums = jnp.dot(weights_ref[n * heads + h], both, preferred_element_type=jnp.float32)
+        asked = count // heads
+        left = weights_ref[h * asked : (h + 1) * asked].reshape(asked * rows, span)
+        totals = jnp.dot(left, both, preferred_element_type=jnp.float32)
+        for n in range(asked):
+            sums = totals[n * rows : (n + 1) * rows]
             result = (sums[:, :HEAD_DIM] / sums[:, HEAD_DIM:]).astype(jnp.bfloat16)
             for copy in range(copies):
                 out_ref[(spot ^ n) * copies + copy, :, cols] = result

time: 47.2 us -> 47.1 us (level)
  no operation moved by 1% of the time
where the time goes in v7:
time: 47.1 us; the launch traced here: 46.9 us
  starting transfers between devices  17.7 us (38%)
  waiting for transfers between devices  12 us (25%)
  blocking collectives  10.6 us (23%)
  Pallas kernels  4.24 us (9%)
  local copies, waits for them, and re-layouts  1.2 us (3%)
  other arithmetic  0.99 us (2%)
    ppermute x4, starting transfers between devices, half_path(): lax.ppermute(part, 'ctx', [(i, i ^ flip) for i in range(ctx)])  10.6 us
    all_to_all x1, blocking collectives, half_path(): lax.all_to_all(attention, ('ctx', 'head'), split_axis=0, concat_axis=0, t...  10.6 us
    ppermute x4, waiting for transfers between devices, half_path(): lax.ppermute(part, 'ctx', [(i, i ^ flip) for i in range(ctx)])  9.88 us
    ppermute x3, starting transfers between devices, half_path(): lax.ppermute(part, 'ctx', [(i, i ^ n + 1) for i in range(ctx)])  3.55 us
    all_to_all x1, starting transfers between devices, half_path(): lax.all_to_all(packed, 'ctx', split_axis=0, concat_axis=0, tiled=True, ax...  3.49 us
    ppermute x1, waiting for transfers between devices, half_path(): beside = lax.ppermute(home, 'head', [(i, i ^ 1) for i in range(groups)])  1.45 us
    squeeze x1, local copies, waits for them, and re-layouts, far_piece(): take = lambda block: lax.dynamic_slice_in_dim(block, seq, 1, 0)[0]  1.17 us
    pallas_call x1, Pallas kernels, half_path(): pl.pallas_call(functools.partial(finish_kernel, flip=1, first=0), in_spec...  1.16 us
  transfers between devices with their start and end apart: 9, of which 4 were waited for; matrix products, arithmetic and copies ran while one was open for 2% of the time, Pallas kernels for 3%

profile of v7, /device:TPU:0, one launch (start us, length us, event | category | flops | bytes accessed | tf_op | source)
XLA Modules:
  0.0 46.9 jit_solution(6375243503102125371)
XLA Ops:
  0.0 0.0 copy-start.4
  0.0 0.0 copy-start.5
  0.0 0.0 copy-start.6
  0.0 1.2 %dynamic-slice_bitcast_fusion = (bf16[128,256]{1,0:T(8,128)(2,1)S(1)}, bf16[128,256]{1,0:T(8,128)(2,1)S(1)}, bf16[128,256]{1,0:T(8,128)(2,1)S(1)}, bf16[128,256]...) fusion(bf16[4,128,256]{2,1,0:T(8,128)(2,1)} %param.9, ...), kind=kLoop, calls=%fused_computation.5 | loop fusion | bytes 1048592 | tf_op jit(solution)/shard_map/squeeze | solution.py:296
  1.2 5.2 %collective-permute-start.2 = (bf16[256,256]{1,0:T(8,128)(2,1)S(1)}, bf16[256,256]{1,0:T(8,128)(2,1)S(1)}, u32[]{:S(2)}, u32[]{:S(2)}) collective-permute-start(bf16[256,256]{1,0:T(8,128)(2,1)S(1)} %pad_maximum_fusion.3), channel_id=1, source_target_pairs={{0,24},{4,28},{8,16},{12,20},{16,8},{20,12},{24,0},{28,4},{1,25},{... | collective-permute-start | bytes 393224 | tf_op jit(solution)/shard_map/ppermute | solution.py:310
  6.4 0.0 copy-start.1
  6.4 0.0 copy-start.2
  6.4 0.0 copy-start.3
  6.4 0.1 collective-permute-start
  6.5 0.0 copy-done.4
  6.5 0.0 copy-done.5
  6.5 0.0 copy-done.6
  6.5 0.9 %pad_maximum_fusion = bf16[4,384,256]{2,1,0:T(8,128)(2,1)} fusion(bf16[4,128,256]{2,1,0:T(8,128)(2,1)S(1)} %copy-done.4, bf16[4,128,256]{2,1,0:T(8,128)(2,1)S(1)} %copy-done.5, bf16[4,128,256]{2,1,0:T(8,128)(2,1)S(1)} %copy-done.6), kind=kLoop, calls=%fused_computation | loop fusion | flops 2359296 | bytes 1572864 | tf_op jit(solution)/shard_map/concatenate | solution.py:308
  7.5 3.5 %all-to-all-start = ((bf16[4,384,256]{2,1,0:T(8,128)(2,1)}), bf16[4,384,256]{2,1,0:T(8,128)(2,1)S(1)}, u32[]{:S(2)}, u32[]{:S(2)}) async-start(bf16[4,384,256]{2,1,0:T(8,128)(2,1)} %pad_maximum_fusion), calls=%async_computation | async-start | bytes 1572864 | tf_op jit(solution)/shard_map/all_to_all | solution.py:314
  11.0 4.4 %collective-permute-start.1 = (bf16[256,256]{1,0:T(8,128)(2,1)S(1)}, bf16[256,256]{1,0:T(8,128)(2,1)S(1)}, u32[]{:S(2)}, u32[]{:S(2)}) collective-permute-start(bf16[256,256]{1,0:T(8,128)(2,1)S(1)} %pad_maximum_fusion.2), channel_id=1, source_target_pairs={{0,20},{4,16},{8,28},{12,24},{16,4},{20,0},{24,12},{28,8},{1,21},{... | collective-permute-start | bytes 393224 | tf_op jit(solution)/shard_map/ppermute | solution.py:310
  15.4 1.0 %collective-permute-start.3 = (bf16[256,256]{1,0:T(8,128)(2,1)S(1)}, bf16[256,256]{1,0:T(8,128)(2,1)S(1)}, u32[]{:S(2)}, u32[]{:S(2)}) collective-permute-start(bf16[256,256]{1,0:T(8,128)(2,1)S(1)} %pad_maximum_fusion.4), channel_id=1, source_target_pairs={{0,28},{4,24},{8,20},{12,16},{16,12},{20,8},{24,4},{28,0},{1,29},{... | collective-permute-start | bytes 393224 | tf_op jit(solution)/shard_map/ppermute | solution.py:310
  16.4 0.0 copy-done.1
  16.4 0.0 copy-done.2
  16.4 0.0 copy-done.3
  16.4 0.7 %count.1 = (bf16[16,128]{1,0:T(8,128)(2,1)S(1)}, bf16[16,128]{1,0:T(8,128)(2,1)S(1)}, bf16[16,128]{1,0:T(8,128)(2,1)S(1)}, bf16[16,128]{1,0:T(8,128)(2,1)S(1)}) custom-call(s32[1]{0:T(128)} %bitcast.1.me_ref, s32[2,4]{1,0:T(2,128)S(1)} %bitcast.20, s32[4,2,4]{2,1,0:T(2,128)S(1)} %copy-done.1, s32[2,4]{1,0:T(2,128)S(1)} %bitcast.21), custom_call_target="tpu_custom_call" | custom-call | tf_op jit(solution)/shard_map/count/pallas_call | solution.py:300
  17.1 1.5 %collective-permute-start.4 = (bf16[16,128]{1,0:T(8,128)(2,1)S(1)}, bf16[16,128]{1,0:T(8,128)(2,1)S(1)}, u32[]{:S(2)}, u32[]{:S(2)}) collective-permute-start(bf16[16,128]{1,0:T(8,128)(2,1)S(1)} %get-tuple-element.10), channel_id=1, source_target_pairs={{0,4},{4,0},{8,12},{12,8},{16,20},{20,16},{24,28},{28,24},{1,5},{5... | collective-permute-start | bytes 12296 | tf_op jit(solution)/shard_map/ppermute | solution.py:316
  18.6 0.0 collective-permute-done.2.refs_2_
  18.6 0.0 collective-permute-start.5
  18.6 0.0 collective-permute-done.refs_0_
  18.6 2.0 %collective-permute-start.6 = (bf16[16,128]{1,0:T(8,128)(2,1)S(1)}, bf16[16,128]{1,0:T(8,128)(2,1)S(1)}, u32[]{:S(2)}, u32[]{:S(2)}) collective-permute-start(bf16[16,128]{1,0:T(8,128)(2,1)S(1)} %get-tuple-element.12), channel_id=1, source_target_pairs={{0,12},{4,8},{8,4},{12,0},{16,28},{20,24},{24,20},{28,16},{1,13},{... | collective-permute-start | bytes 12296 | tf_op jit(solution)/shard_map/ppermute | solution.py:316
  20.7 3.5 %collective-permute-done.1.refs_1_ = bf16[256,256]{1,0:T(8,128)(2,1)S(1)} collective-permute-done((bf16[256,256]{1,0:T(8,128)(2,1)S(1)}, bf16[256,256]{1,0:T(8,128)(2,1)S(1)}, u32[]{:S(2)}, u32[]{:S(2)}) %collective-permute-start.1) | collective-permute-done | bytes 131104 | tf_op jit(solution)/shard_map/ppermute | solution.py:310
  24.1 6.4 %collective-permute-done.3.refs_3_ = bf16[256,256]{1,0:T(8,128)(2,1)S(1)} collective-permute-done((bf16[256,256]{1,0:T(8,128)(2,1)S(1)}, bf16[256,256]{1,0:T(8,128)(2,1)S(1)}, u32[]{:S(2)}, u32[]{:S(2)}) %collective-permute-start.3) | collective-permute-done | bytes 131104 | tf_op jit(solution)/shard_map/ppermute | solution.py:310
  30.6 0.0 collective-permute-done.4.refs_1_
  30.6 0.0 collective-permute-done.5.refs_2_
  30.6 0.7 %collective-permute-done.6.refs_3_ = bf16[16,128]{1,0:T(8,128)(2,1)S(1)} collective-permute-done((bf16[16,128]{1,0:T(8,128)(2,1)S(1)}, bf16[16,128]{1,0:T(8,128)(2,1)S(1)}, u32[]{:S(2)}, u32[]{:S(2)}) %collective-permute-start.6) | collective-permute-done | bytes 4128 | tf_op jit(solution)/shard_map/ppermute | solution.py:316
  31.3 0.0 all-to-all-done.near_ref
  31.3 1.1 %weigh.1.weights_ref = bf16[8,128,1024]{2,1,0:T(8,128)(2,1)S(1)} custom-call(s32[1]{0:T(128)} %bitcast.1.me_ref, bf16[4,384,256]{2,1,0:T(8,128)(2,1)S(1)} %all-to-all-done.near_ref, bf16[4,256,256]{2,1,0:T(8,128)(2,1)S(1)} %stack.1.early_ref, bf16[16,128]{1,0:T(8,128)(2,1)S(1)} %get-tuple-element.9.refs_0_, ...), custom_call_target="tpu_custom_call" | custom-call | flops 268435456 | bytes 2097152 | tf_op jit(solution)/shard_map/weigh/pallas_call | solution.py:332
  32.4 0.0 copy-start
  32.5 0.8 %sum.1 = bf16[8,128,256]{2,1,0:T(8,128)(2,1)S(1)} custom-call(s32[1]{0:T(128)} %bitcast.1.me_ref, bf16[8,128,1024]{2,1,0:T(8,128)(2,1)S(1)} %weigh.1.weights_ref, bf16[4,384,256]{2,1,0:T(8,128)(2,1)S(1)} %all-to-all-done.near_ref, bf16[4,256,256]{2,1,0:T(8,128)(2,1)S(1)} %stack.1.early_ref), custom_call_target="tpu_custom_call" | custom-call | flops 268435456 | bytes 2097152 | tf_op jit(solution)/shard_map/sum/pallas_call | solution.py:342
  33.2 10.6 %all_to_all.10.refs_0_ = bf16[8,128,256]{2,1,0:T(8,128)(2,1)S(1)} all-to-all(bf16[8,128,256]{2,1,0:T(8,128)(2,1)S(1)} %sum.1), channel_id=1, replica_groups={{0,2,4,6,8,10,12,14},{1,3,5,7,9,11,13,15},{16,18,20,22,24,26,28,30},{17..., dimensions={0} | all-to-all | bytes 1048576 | tf_op jit(solution)/shard_map/all_to_all | solution.py:352
  43.8 0.0 collective-permute-start.7
  43.8 0.0 copy-done
  43.8 0.4 project.1.before_ref
  44.3 1.4 %collective-permute-done.7.part_ref = bf16[8,128,256]{2,1,0:T(8,128)(2,1)S(1)} collective-permute-done((bf16[8,128,256]{2,1,0:T(8,128)(2,1)S(1)}, bf16[8,128,256]{2,1,0:T(8,128)(2,1)S(1)}, u32[]{:S(2)}, u32[]{:S(2)}) %collective-permute-start.7) | collective-permute-done | bytes 524320 | tf_op jit(solution)/shard_map/ppermute | solution.py:364
  45.8 1.2 %finish.1 = bf16[4,128,512]{2,1,0:T(8,128)(2,1)} custom-call(s32[1]{0:T(128)} %bitcast.group_ref, f32[4,128,512]{2,1,0:T(8,128)S(1)} %project.1.before_ref, bf16[8,128,256]{2,1,0:T(8,128)(2,1)S(1)} %collective-permute-done.7.part_ref, bf16[1024,512]{1,0:T(8,128)(2,1)S(1)} %copy-done), custom_call_target="tpu_custom_call" | custom-call | tf_op jit(solution)/shard_map/finish/pallas_call | solution.py:382
  (5 shorter events, 0.1 us)
Async XLA Ops:
  0.0 6.5 %copy-start.4 = (bf16[4,128,256]{2,1,0:T(8,128)(2,1)S(1)}, bf16[4,128,256]{2,1,0:T(8,128)(2,1)}, u32[]{:S(2)}) copy-start(bf16[4,128,256]{2,1,0:T(8,128)(2,1)} %param.9) | copy-start | bytes 786436
  0.0 6.5 %copy-start.5 = (bf16[4,128,256]{2,1,0:T(8,128)(2,1)S(1)}, bf16[4,128,256]{2,1,0:T(8,128)(2,1)}, u32[]{:S(2)}) copy-start(bf16[4,128,256]{2,1,0:T(8,128)(2,1)} %param.8) | copy-start | bytes 786436
  0.0 6.5 %copy-start.6 = (bf16[4,128,256]{2,1,0:T(8,128)(2,1)S(1)}, bf16[4,128,256]{2,1,0:T(8,128)(2,1)}, u32[]{:S(2)}) copy-start(bf16[4,128,256]{2,1,0:T(8,128)(2,1)} %param.7) | copy-start | bytes 786436
  1.2 17.4 %collective-permute-start.2 = (bf16[256,256]{1,0:T(8,128)(2,1)S(1)}, bf16[256,256]{1,0:T(8,128)(2,1)S(1)}, u32[]{:S(2)}, u32[]{:S(2)}) collective-permute-start(bf16[256,256]{1,0:T(8,128)(2,1)S(1)} %pad_maximum_fusion.3), channel_id=1, source_target_pairs={{0,24},{4,28},{8,16},{12,20},{16,8},{20,12},{24,0},{28,4},{1,25},{... | collective-permute-start | bytes 393224 | tf_op jit(solution)/shard_map/ppermute | solution.py:310
  6.4 10.0 %copy-start.1 = (s32[4,2,4]{2,1,0:T(2,128)S(1)}, s32[4,2,4]{2,1,0:T(2,128)}, u32[]{:S(2)}) copy-start(s32[4,2,4]{2,1,0:T(2,128)} %rand_ref.1) | copy-start | bytes 388
  6.4 10.0 %copy-start.2 = (s32[4,2]{0,1:T(2,128)S(1)}, s32[4,2]{0,1:T(2,128)}, u32[]{:S(2)}) copy-start(s32[4,2]{0,1:T(2,128)} %param.11) | copy-start | bytes 100
  6.4 10.0 %copy-start.3 = (s32[4,2]{0,1:T(2,128)S(1)}, s32[4,2]{0,1:T(2,128)}, u32[]{:S(2)}) copy-start(s32[4,2]{0,1:T(2,128)} %param.13) | copy-start | bytes 100
  6.4 12.2 %collective-permute-start = (bf16[256,256]{1,0:T(8,128)(2,1)S(1)}, bf16[256,256]{1,0:T(8,128)(2,1)S(1)}, u32[]{:S(2)}, u32[]{:S(2)}) collective-permute-start(bf16[256,256]{1,0:T(8,128)(2,1)S(1)} %pad_maximum_fusion.1), channel_id=1, source_target_pairs={{0,16},{4,20},{8,24},{12,28},{16,0},{20,4},{24,8},{28,12},{1,17},{... | collective-permute-start | bytes 393224 | tf_op jit(solution)/shard_map/ppermute | solution.py:310
  7.5 23.8 %all-to-all-start = ((bf16[4,384,256]{2,1,0:T(8,128)(2,1)}), bf16[4,384,256]{2,1,0:T(8,128)(2,1)S(1)}, u32[]{:S(2)}, u32[]{:S(2)}) async-start(bf16[4,384,256]{2,1,0:T(8,128)(2,1)} %pad_maximum_fusion), calls=%async_computation | async-start | bytes 1572864 | tf_op jit(solution)/shard_map/all_to_all | solution.py:314
  11.0 13.1 %collective-permute-start.1 = (bf16[256,256]{1,0:T(8,128)(2,1)S(1)}, bf16[256,256]{1,0:T(8,128)(2,1)S(1)}, u32[]{:S(2)}, u32[]{:S(2)}) collective-permute-start(bf16[256,256]{1,0:T(8,128)(2,1)S(1)} %pad_maximum_fusion.2), channel_id=1, source_target_pairs={{0,20},{4,16},{8,28},{12,24},{16,4},{20,0},{24,12},{28,8},{1,21},{... | collective-permute-start | bytes 393224 | tf_op jit(solution)/shard_map/ppermute | solution.py:310
  15.4 15.1 %collective-permute-start.3 = (bf16[256,256]{1,0:T(8,128)(2,1)S(1)}, bf16[256,256]{1,0:T(8,128)(2,1)S(1)}, u32[]{:S(2)}, u32[]{:S(2)}) collective-permute-start(bf16[256,256]{1,0:T(8,128)(2,1)S(1)} %pad_maximum_fusion.4), channel_id=1, source_target_pairs={{0,28},{4,24},{8,20},{12,16},{16,12},{20,8},{24,4},{28,0},{1,29},{... | collective-permute-start | bytes 393224 | tf_op jit(solution)/shard_map/ppermute | solution.py:310
  17.1 13.5 %collective-permute-start.4 = (bf16[16,128]{1,0:T(8,128)(2,1)S(1)}, bf16[16,128]{1,0:T(8,128)(2,1)S(1)}, u32[]{:S(2)}, u32[]{:S(2)}) collective-permute-start(bf16[16,128]{1,0:T(8,128)(2,1)S(1)} %get-tuple-element.10), channel_id=1, source_target_pairs={{0,4},{4,0},{8,12},{12,8},{16,20},{20,16},{24,28},{28,24},{1,5},{5... | collective-permute-start | bytes 12296 | tf_op jit(solution)/shard_map/ppermute | solution.py:316
  18.6 12.0 %collective-permute-start.5 = (bf16[16,128]{1,0:T(8,128)(2,1)S(1)}, bf16[16,128]{1,0:T(8,128)(2,1)S(1)}, u32[]{:S(2)}, u32[]{:S(2)}) collective-permute-start(bf16[16,128]{1,0:T(8,128)(2,1)S(1)} %get-tuple-element.11), channel_id=1, source_target_pairs={{0,8},{4,12},{8,0},{12,4},{16,24},{20,28},{24,16},{28,20},{1,9},{5... | collective-permute-start | bytes 12296 | tf_op jit(solution)/shard_map/ppermute | solution.py:316
  18.6 12.6 %collective-permute-start.6 = (bf16[16,128]{1,0:T(8,128)(2,1)S(1)}, bf16[16,128]{1,0:T(8,128)(2,1)S(1)}, u32[]{:S(2)}, u32[]{:S(2)}) collective-permute-start(bf16[16,128]{1,0:T(8,128)(2,1)S(1)} %get-tuple-element.12), channel_id=1, source_target_pairs={{0,12},{4,8},{8,4},{12,0},{16,28},{20,24},{24,20},{28,16},{1,13},{... | collective-permute-start | bytes 12296 | tf_op jit(solution)/shard_map/ppermute | solution.py:316
  32.4 11.4 %copy-start = (bf16[1024,512]{1,0:T(8,128)(2,1)S(1)}, bf16[1024,512]{1,0:T(8,128)(2,1)}, u32[]{:S(2)}) copy-start(bf16[1024,512]{1,0:T(8,128)(2,1)} %weight_ref.1) | copy-start | bytes 3145732
  43.8 1.9 %collective-permute-start.7 = (bf16[8,128,256]{2,1,0:T(8,128)(2,1)S(1)}, bf16[8,128,256]{2,1,0:T(8,128)(2,1)S(1)}, u32[]{:S(2)}, u32[]{:S(2)}) collective-permute-start(bf16[8,128,256]{2,1,0:T(8,128)(2,1)S(1)} %all_to_all.10.refs_0_), channel_id=1, source_target_pairs={{0,1},{1,0},{2,3},{3,2},{4,5},{5,4},{6,7},{7,6},{8,9},{9,8},{10,11... | collective-permute-start | bytes 1572872 | tf_op jit(solution)/shard_map/ppermute | solution.py:364
